TPU v7x, 256 devices: a whole 4x4x8 slice. The times are simulated.
256 devices in a mesh: line: 4 (over x), plane: 64 (over y, z, core).
Axes of the slice: x: 4, y: 4, z: 8, core: 2. Of those that a mesh axis runs over, the one named last changes fastest.
Arguments:
- adjoint: float32 [5, 64, 512, 256], P(None, 'line', 'plane'), may hold values from -6 to 6
- forcing: float32 [5, 64, 512, 256], P(None, 'line', 'plane'), may hold values from -6 to 6
- eigen_values: float32 [5, 64, 512, 256], P(None, 'line', 'plane'), may hold values from -1.5 to 1.5
- face_masks: int32 [2, 512, 256], P(None, 'plane'), may hold values 0 or 1
- line_coeffs: float32 [5, 6, 64, 256], P(None, None, 'line'), may hold values from 0 to 1, as said below
- cross_coeffs: float32 [5, 4, 512, 256], P(None, None, 'plane'), may hold values from 0 to 1, as said below
Outputs:
- update: float32 [5, 64, 512, 256], P(None, 'line', 'plane')
Inputs may be any that keep to these rules, and one draw needn't show every extreme that they name: `line_coeffs`: every entry lies in [0, 1]; for each point the two lower coefficients and their diagonal inverse sum to 1, likewise the upper ones. `cross_coeffs`: every entry lies in [0, 1]; for each point a coefficient and its diagonal inverse sum to 1.
All inputs are finite; a program needn't handle non-finite values. No bound on the sum of `face_masks` on one device may be relied on, other than what follows from the above.
Results may differ from a plain program's by a relative error of at most 0.000022.
Values sent between devices are 32-bit elements; how exact they have to be, the bound alone decides.
No kernel may reach another device: no remote copies, remote signals or barrier semaphores. Data moves between devices by JAX's collectives and lax.ppermute only.
A program may use at most 64 MiB of HBM per device.

v0:
```python
import jax
import jax.numpy as jnp
from jax import lax
from jax.experimental import pallas as pl
from jax.experimental.pallas import tpu as pltpu
from jax.sharding import PartitionSpec as P

F32 = jnp.float32
NV, NI, NJ, NK = 5, 16, 8, 256
HALF = NK // 2
PLANE = NI * NJ
TILE = (NJ, NK)
MAPS = NV * 8


def rows_of(shape):
    return lax.broadcasted_iota(jnp.int32, shape, len(shape) - 2)


def lanes_of(shape):
    return lax.broadcasted_iota(jnp.int32, shape, len(shape) - 1)


def call(kernel, outs, *args, scratch=(), in_hbm=0, out_hbm=False, name=None, flops=1000):
    outs = [jax.ShapeDtypeStruct(s, F32) for s in outs]
    args = [
        pltpu.with_memory_space_constraint(x, pltpu.HBM) if n < in_hbm else x
        for n, x in enumerate(args)
    ]
    spaces = [pltpu.HBM] * in_hbm + [pltpu.VMEM] * (len(args) - in_hbm)
    return pl.pallas_call(
        kernel,
        out_shape=outs,
        in_specs=[pl.BlockSpec(memory_space=s) for s in spaces],
        out_specs=[pl.BlockSpec(memory_space=pltpu.HBM if out_hbm else pltpu.VMEM)] * len(outs),
        scratch_shapes=list(scratch),
        compiler_params=pltpu.CompilerParams(vmem_limit_bytes=40 * 1024 * 1024),
        cost_estimate=pl.CostEstimate(flops=flops, bytes_accessed=flops, transcendentals=0),
        name=name,
    )(*args)


def place():
    q = lax.axis_index("plane")
    return lax.rem(q, 2), lax.rem(q // 2, 8), q // 16


def pick(p, options):
    out = options[-1]
    for n in reversed(range(len(options) - 1)):
        out = jnp.where(p == n, options[n], out)
    return out


def faces_kernel(
    a_hbm, e_hbm, w_ref, ia_ref, ib_ref, ja_ref, jb_ref, a_scr, e_scr, scr, sems
):
    even_line = lax.rem(lax.axis_index("line"), 2) == 0
    even_plane = lax.rem(lax.axis_index("plane"), 2) == 0

    def fetch(v, n):
        src, dst = ((a_hbm, a_scr), (e_hbm, e_scr))[n]
        at = pl.ds(v * PLANE, PLANE)
        return pltpu.make_async_copy(src.at[at], dst.at[at], sems.at[v, n])

    for v in range(NV):
        for n in range(2):
            fetch(v, n).start()
    for v in range(NV):
        for n in range(2):
            fetch(v, n).wait()
        base = v * PLANE
        for part in range(2):
            lane = slice(part * HALF, part * HALF + HALF)
            w = a_scr[base : base + PLANE, lane] * e_scr[base : base + PLANE, lane]
            w_ref[base : base + PLANE, lane] = w
            scr[v, part] = w
            low, high = w[:NJ], w[PLANE - NJ :]
            ia_ref[v, :, lane] = jnp.where(even_line, high, low)
            ib_ref[v, :, lane] = jnp.where(even_line, low, high)
            low = scr[v, part, pl.ds(0, NI, stride=NJ), :]
            high = scr[v, part, pl.ds(NJ - 1, NI, stride=NJ), :]
            ja_ref[v, :, lane] = jnp.where(even_plane, high, low)
            jb_ref[v, :, lane] = jnp.where(even_plane, low, high)


def prep_kernel(
    f_hbm, c_hbm, x_hbm, m_hbm, w_ref,
    c_ref, line_resp_ref, maps_ref, cross_resp_ref, halo_resp_ref, co_ref, g_ref, t_ref, x_ref,
    f_ref, m_ref, sems,
):
    pairs = ((c_hbm, c_ref), (x_hbm, x_ref), (m_hbm, m_ref), (f_hbm, f_ref))
    copies = [pltpu.make_async_copy(a, b, sems.at[n]) for n, (a, b) in enumerate(pairs)]
    for copy in copies:
        copy.start()
    copies[0].wait()
    line_coeffs_of(c_ref, line_resp_ref, maps_ref)
    copies[1].wait()
    cross_coeffs_of(x_ref, cross_resp_ref, halo_resp_ref, co_ref)
    copies[2].wait()
    copies[3].wait()
    local_source(w_ref, f_ref, m_ref, x_ref, g_ref, t_ref)


def line_coeffs_of(c_ref, resp_ref, msg_ref):
    row = rows_of(TILE)
    unit = [jnp.where(row == n, 1.0, 0.0) for n in range(4)]
    one, two = [unit[0]] * NV, [unit[1]] * NV
    lower = [[None] * NI for _ in range(NV)]
    for i in range(NI):
        for v in range(NV):
            first, second = (c_ref[v, n, i : i + 1, :] for n in range(2))
            one[v], two[v] = first * one[v] + second * two[v], one[v]
            lower[v][i] = one[v]
    for v in range(NV):
        msg_ref[v * 12 : v * 12 + 2, :] = one[v][0:2]
        msg_ref[v * 12 + 2 : v * 12 + 4, :] = two[v][0:2]
    one, two = [unit[2]] * NV, [unit[3]] * NV
    for i in reversed(range(NI)):
        for v in range(NV):
            first, second, scale = (c_ref[v, n, i : i + 1, :] for n in range(3, 6))
            one[v], two[v] = scale * lower[v][i] + first * one[v] + second * two[v], one[v]
            at = v * PLANE + i * NJ
            for part in range(2):
                resp_ref[part, at : at + NJ, :] = one[v][:, part * HALF : part * HALF + HALF]
    for v in range(NV):
        msg_ref[v * 12 + 4 : v * 12 + 8, :] = one[v][0:4]
        msg_ref[v * 12 + 8 : v * 12 + 12, :] = two[v][0:4]
    msg_ref[60:, :] = jnp.zeros((4, NK), F32)


def up_steps(c):
    row = rows_of(TILE)
    one = jnp.where(row == 0, 0.0, c)
    two = one * pltpu.roll(one, 1, 0)
    return (one, two, two * pltpu.roll(two, 2, 0))


def down_steps(c):
    row = rows_of(TILE)
    one = jnp.where(row == NJ - 1, 0.0, c)
    two = one * pltpu.roll(one, NJ - 1, 0)
    return (one, two, two * pltpu.roll(two, NJ - 2, 0))


def scan_up(x, steps):
    for n, c in zip((1, 2, 4), steps):
        x = x + c * pltpu.roll(x, n, 0)
    return x


def scan_down(x, steps):
    for n, c in zip((1, 2, 4), steps):
        x = x + c * pltpu.roll(x, NJ - n, 0)
    return x


def cross_coeffs_of(x_ref, resp_ref, halo_ref, co_ref):
    row = rows_of(TILE)
    co_ref[15:, :] = jnp.zeros((1, NK), F32)
    for v in range(NV):
        fc, fd, bc, bd = (x_ref[v, n] for n in range(4))
        up, dn = up_steps(fc), down_steps(bc)
        f_resp = scan_up(jnp.where(row == 0, fc, 0.0), up)
        g_resp = scan_down(bd * f_resp, dn)
        b_resp = scan_down(jnp.where(row == NJ - 1, bc, 0.0), dn)
        resp_ref[v, 0] = g_resp
        resp_ref[v, 1] = b_resp
        for n, at, half in ((0, 0, 0.5), (1, NJ - 1, -0.5)):
            f = scan_up(jnp.where(row == at, half * fd, 0.0), up)
            g = scan_down(bd * f, dn)
            halo_ref[v, n] = g
            halo_ref[v, n + 2] = edge_rows(f, g)
        co_ref[v : v + 1, :] = f_resp[NJ - 1 : NJ]
        co_ref[NV + v : NV + v + 1, :] = b_resp[0:1]
        co_ref[2 * NV + v : 2 * NV + v + 1, :] = g_resp[0:1]


def edge_rows(f, g):
    row = rows_of(TILE)
    return jnp.where(row == 0, pltpu.roll(f, 1, 0), pltpu.roll(g, 1, 0))


def local_source(w_ref, f_ref, m_ref, x_ref, g_ref, t_ref):
    p = lax.axis_index("line")
    row, lane = rows_of(TILE), lanes_of(TILE)
    zero = jnp.zeros(TILE, F32)
    low_mask = jnp.where(p == 0, m_ref[0].astype(F32), zero)
    high_mask = jnp.where(p == 3, m_ref[1].astype(F32), zero)

    def step(v, _):
        base = pl.multiple_of(v * PLANE, PLANE)
        at = [pl.ds(base + i * NJ, NJ) for i in range(NI)]
        w = [w_ref[at[i], :] for i in range(NI)]
        fd, bd = x_ref[v, 1], x_ref[v, 3]
        up, dn = up_steps(x_ref[v, 0]), down_steps(x_ref[v, 2])
        for i in range(NI):
            x = w[i]
            before = low_mask * x if i == 0 else w[i - 1]
            after = high_mask * x if i == NI - 1 else w[i + 1]
            j_before = jnp.where(row == 0, 0.0, pltpu.roll(x, 1, 0))
            j_after = jnp.where(row == NJ - 1, 0.0, pltpu.roll(x, NJ - 1, 0))
            k_before = jnp.where(lane == 0, 0.0, pltpu.roll(x, 1, 1))
            k_after = jnp.where(lane == NK - 1, 0.0, pltpu.roll(x, NK - 1, 1))
            s = f_ref[at[i], :] + 0.5 * (
                (before - after) + (j_before - j_after) + (k_before - k_after)
            )
            f = scan_up(fd * s, up)
            g = scan_down(bd * f, dn)
            g_ref[at[i], :] = g
            t_ref[at[i], :] = edge_rows(f, g)
        return 0

    lax.fori_loop(0, NV, step, 0)


def source_kernel(
    g_in, t_in, ia_ref, ib_ref, ja_ref, jb_ref, c_ref, x_ref, halo_ref, maps_ref,
    low_ref, high_ref, gi_ref, edge_ref, msg_ref, t_scr,
):
    p, q = lax.axis_index("line"), lax.axis_index("plane")
    even_line, even_plane = lax.rem(p, 2) == 0, lax.rem(q, 2) == 0
    for v in range(NV):
        ia, ib = ia_ref[v], ib_ref[v]
        low = jnp.where(p == 0, 0.0, jnp.where(even_line, ib, ia))
        high = jnp.where(p == 3, 0.0, jnp.where(even_line, ia, ib))
        ja, jb = ja_ref[v], jb_ref[v]
        j_low = jnp.where(q == 0, 0.0, jnp.where(even_plane, jb, ja))
        j_high = jnp.where(q == 63, 0.0, jnp.where(even_plane, ja, jb))
        low_ref[v] = j_low
        high_ref[v] = j_high
        fd, bd = x_ref[v, 1], x_ref[v, 3]
        up, dn = up_steps(x_ref[v, 0]), down_steps(x_ref[v, 2])
        ends = []
        for n, face in enumerate((0.5 * low, -0.5 * high)):
            f = scan_up(fd * face, up)
            g = scan_down(bd * f, dn)
            gi_ref[v, n] = g
            ends.append(edge_rows(f, g))
        a, b = halo_ref[v, 2], halo_ref[v, 3]
        for i in range(NI):
            at = slice(v * PLANE + i * NJ, v * PLANE + i * NJ + NJ)
            t = t_in[at, :] + a * j_low[i : i + 1] + b * j_high[i : i + 1]
            if i == 0:
                t = t + ends[0]
            if i == NI - 1:
                t = t + ends[1]
            t_scr[at, :] = t
    local_sweeps(c_ref, t_scr, t_scr, edge_ref, msg_ref, small=True)
    msg_ref[MAPS:, :] = maps_ref[...]


def local_sweeps(c_ref, src_ref, tmp_ref, out_ref, msg_ref, small):
    row = rows_of(TILE)
    zero = jnp.zeros(TILE, F32)
    one, two = [zero] * NV, [zero] * NV
    for i in range(NI):
        for v in range(NV):
            first, second, scale = (c_ref[v, n, i : i + 1, :] for n in range(3))
            at = slice(v * PLANE + i * NJ, v * PLANE + i * NJ + NJ)
            one[v], two[v] = scale * src_ref[at, :] + first * one[v] + second * two[v], one[v]
            tmp_ref[at, :] = one[v]
    ends = list(zip(one, two))
    one, two = [zero] * NV, [zero] * NV
    for i in reversed(range(NI)):
        for v in range(NV):
            first, second, scale = (c_ref[v, n, i : i + 1, :] for n in range(3, 6))
            at = slice(v * PLANE + i * NJ, v * PLANE + i * NJ + NJ)
            one[v], two[v] = scale * tmp_ref[at, :] + first * one[v] + second * two[v], one[v]
            if small:
                for part in range(2):
                    out_ref[part, at, :] = one[v][:, part * HALF : part * HALF + HALF]
            else:
                out_ref[at, :] = one[v]
    for v in range(NV):
        if small:
            a, b, c, d = ends[v][0], ends[v][1], one[v], two[v]
            msg_ref[v * 8 : v * 8 + 8, :] = jnp.where(
                row < 2,
                a,
                jnp.where(
                    row < 4,
                    pltpu.roll(b, 2, 0),
                    jnp.where(row < 6, pltpu.roll(c, 4, 0), pltpu.roll(d, 6, 0)),
                ),
            )
        else:
            for n, x in enumerate((ends[v][0], ends[v][1], one[v], two[v])):
                msg_ref[v, n * NJ : n * NJ + NJ, :] = x


def planes_kernel(c_ref, g_ref, halo_ref, low_ref, high_ref, gi_ref, out_ref, msg_ref, g_scr):
    for v in range(NV):
        a, b = halo_ref[v, 0], halo_ref[v, 1]
        for i in range(NI):
            at = slice(v * PLANE + i * NJ, v * PLANE + i * NJ + NJ)
            g = g_ref[at, :] + a * low_ref[v, i : i + 1, :] + b * high_ref[v, i : i + 1, :]
            if i == 0:
                g = g + gi_ref[v, 0]
            if i == NI - 1:
                g = g + gi_ref[v, 1]
            g_scr[at, :] = g
    local_sweeps(c_ref, g_scr, out_ref, out_ref, msg_ref, small=False)


def maps_of(ref, v):
    return ref[MAPS + v * 12 : MAPS + v * 12 + 12, :]


def line_pair(p, own, got):
    is_low = lax.rem(p, 2) == 0
    return (
        [jnp.where(is_low, a, b) for a, b in zip(own, got)],
        [jnp.where(is_low, b, a) for a, b in zip(own, got)],
    )


def l_after(m, phi, l):
    return (
        m[0:1] * l[0] + m[1:2] * l[1] + phi[0],
        m[2:3] * l[0] + m[3:4] * l[1] + phi[1],
    )


def u_before(m, beta, l, u):
    return (
        m[4:5] * l[0] + m[5:6] * l[1] + m[6:7] * u[0] + m[7:8] * u[1] + beta[0],
        m[8:9] * l[0] + m[9:10] * l[1] + m[10:11] * u[0] + m[11:12] * u[1] + beta[1],
    )


def pair_states(p, low, high):
    lm, la, lb, lc, ld = low
    hm, ha, hb, hc, hd = high
    phi = l_after(hm, (ha, hb), (la, lb))
    zero = jnp.zeros_like(la)
    beta = u_before(lm, (lc, ld), (zero, zero), u_before(hm, (hc, hd), (la, lb), (zero, zero)))
    upper = p >= 2
    return [jnp.where(upper, a, b) for a, b in zip(beta, phi)]


def pair_gamma(low_m, high_m):
    columns = []
    for c in range(2):
        l = (low_m[c : c + 1], low_m[2 + c : 3 + c])
        a = high_m[4:5] * l[0] + high_m[5:6] * l[1]
        b = high_m[8:9] * l[0] + high_m[9:10] * l[1]
        columns.append(
            (
                low_m[4 + c : 5 + c] + low_m[6:7] * a + low_m[7:8] * b,
                low_m[8 + c : 9 + c] + low_m[10:11] * a + low_m[11:12] * b,
            )
        )
    (raa, rba), (rab, rbb) = columns
    return raa, rab, rba, rbb


def entering(p, low, high, mine, got, gamma):
    upper, is_low = p >= 2, lax.rem(p, 2) == 0
    zero = jnp.zeros_like(mine[0])
    l = [jnp.where(upper, x, zero) for x in got]
    raa, rab, rba, rbb = gamma
    u = (
        got[0] + raa * mine[0] + rab * mine[1],
        got[1] + rba * mine[0] + rbb * mine[1],
    )
    u = [jnp.where(upper, zero, x) for x in u]
    l_high = l_after(low[0], low[1:3], l)
    u_low = u_before(high[0], high[3:5], l_high, u)
    return [jnp.where(is_low, a, b) for a, b in zip(l, l_high)] + [
        jnp.where(is_low, a, b) for a, b in zip(u_low, u)
    ]


def edges_kernel(
    edge_ref, resp_ref, co_ref, own_ref, got1_ref, got2_ref, got3_ref,
    keep_ref, send_ref, gamma_ref,
):
    p = lax.axis_index("line")
    even = place()[0] == 0
    refs = (own_ref, got1_ref, got2_ref, got3_ref)

    def put(at, x, y):
        keep_ref[at, :] = jnp.where(even, x, y)
        send_ref[at, :] = jnp.where(even, y, x)

    for v in range(NV):
        rows, maps = [], []
        for r in range(4):
            rows.append(pick(p, [refs[r ^ own][v * 8 : v * 8 + 8, :] for own in range(4)]))
            maps.append(pick(p, [maps_of(refs[r ^ own], v) for own in range(4)]))
        part = [[x[n * 2 : n * 2 + 2] for n in range(4)] for x in rows]
        zero = jnp.zeros((2, NK), F32)
        low = [(zero, zero), (part[0][0], part[0][1])]
        for r in (1, 2):
            low.append(l_after(maps[r], part[r][:2], low[r]))
        high = [None, None, None, (zero, zero)]
        for r in (3, 2, 1):
            high[r - 1] = u_before(maps[r], part[r][2:], low[r], high[r])
        states = [pick(p, [x[t] for x in low]) for t in range(2)]
        states += [pick(p, [x[t] for x in high]) for t in range(2)]
        for t in range(2):
            parts = []
            for half in range(2):
                lane = slice(half * HALF, half * HALF + HALF)
                x = edge_ref[half, pl.ds(v * PLANE + t, NI, stride=NJ), :]
                for n in range(4):
                    r = resp_ref[half, pl.ds(v * PLANE + n, NI, stride=NJ), :]
                    x = x + r * states[n][t : t + 1, lane]
                parts.append(x)
            put(slice(v * 32 + t * 16, v * 32 + t * 16 + 16), *parts)
        for n, x in enumerate(pair_gamma(maps[2], maps[3])):
            gamma_ref[v * 4 + n : v * 4 + n + 1, :] = x
    put(slice(160, 176), co_ref[:, :HALF], co_ref[:, HALF:])
    gamma_ref[20:24, :] = jnp.zeros((4, NK), F32)


def last_gamma(ref, v):
    return [ref[v * 4 + n : v * 4 + n + 1, :] for n in range(4)]


def big_parts(ref, maps_ref, v):
    return [maps_of(maps_ref, v)] + [ref[v, n * NJ : n * NJ + NJ, :] for n in range(4)]


def plane_pair_kernel(own_ref, got_ref, own_maps, got_maps, out_ref):
    p = lax.axis_index("line")
    for v in range(NV):
        low, high = line_pair(p, big_parts(own_ref, own_maps, v), big_parts(got_ref, got_maps, v))
        a, b = pair_states(p, low, high)
        out_ref[v, :NJ, :] = a
        out_ref[v, NJ:, :] = b


def solved_kernel(
    local_ref, resp_ref, own_ref, got_ref, own_maps, got_maps, mine2_ref, got2_ref, last_ref, out_ref
):
    p = lax.axis_index("line")
    for v in range(NV):
        low, high = line_pair(p, big_parts(own_ref, own_maps, v), big_parts(got_ref, got_maps, v))
        mine = (mine2_ref[v, :NJ, :], mine2_ref[v, NJ:, :])
        got = (got2_ref[v, :NJ, :], got2_ref[v, NJ:, :])
        states = entering(p, low, high, mine, got, last_gamma(last_ref, v))
        for i in range(NI):
            at = v * PLANE + i * NJ
            for part in range(2):
                lane = slice(part * HALF, part * HALF + HALF)
                x = local_ref[at : at + NJ, lane]
                for n in range(4):
                    x = x + resp_ref[part, at + n : at + n + 1, :] * states[n][:, lane]
                out_ref[at : at + NJ, lane] = x


def load(ref):
    phi = [ref[v * 32 : v * 32 + NI, :] for v in range(NV)]
    beta = [ref[v * 32 + NI : v * 32 + 2 * NI, :] for v in range(NV)]
    return (phi, beta, ref[160:165, :], ref[165:170, :], ref[170:175, :])


def store(ref, agg):
    phi, beta, F, B, g = agg
    for v in range(NV):
        ref[v * 32 : v * 32 + NI, :] = phi[v]
        ref[v * 32 + NI : v * 32 + 2 * NI, :] = beta[v]
    ref[160:165, :] = F
    ref[165:170, :] = B
    ref[170:175, :] = g
    ref[175:176, :] = jnp.zeros((1, HALF), F32)


def choose(low_is_own, own, other):
    return jax.tree.map(lambda a, b: jnp.where(low_is_own, a, b), own, other)


def ordered(low_is_own, own, other):
    return choose(low_is_own, own, other), choose(low_is_own, other, own)


def compose(low, high):
    lp, lb, lF, lB, lg = low
    hp, hb, hF, hB, hg = high
    at = [slice(v, v + 1) for v in range(NV)]
    return (
        [hF[at[v]] * lp[v] + hp[v] for v in range(NV)],
        [lb[v] + lB[at[v]] * (hb[v] + hg[at[v]] * lp[v]) for v in range(NV)],
        hF * lF,
        lB * hB,
        lg + lB * hg * lF,
    )


def f_after(agg, f):
    return [agg[2][v : v + 1] * f[v] + agg[0][v] for v in range(NV)]


def g_before(agg, f, u):
    return [agg[1][v] + agg[4][v : v + 1] * f[v] + agg[3][v : v + 1] * u[v] for v in range(NV)]


def bit_clear(z, n):
    return lax.rem(z // n, 2) == 0


def chip_kernel(keep_ref, got_ref, out_ref):
    store(out_ref, compose(*ordered(place()[0] == 0, load(keep_ref), load(got_ref))))


def members(refs):
    m = lax.rem(place()[1], 4)
    parts = [load(r) for r in refs]
    return [
        jax.tree.map(lambda *x: pick(m, x), *(parts[r ^ own] for own in range(4)))
        for r in range(4)
    ]


def quad_kernel(*refs):
    a, b, c, d = members(refs[:4])
    store(refs[4], compose(compose(a, b), compose(c, d)))


def ring_kernel(own_ref, got_ref, out_ref):
    store(out_ref, compose(*ordered(bit_clear(place()[1], 4), load(own_ref), load(got_ref))))


def top_kernel(own_ref, got_ref, out_ref):
    y = place()[2]
    agg = compose(*ordered(bit_clear(y, 1), load(own_ref), load(got_ref)))
    for v in range(NV):
        out_ref[v * NI : v * NI + NI, :] = jnp.where(y >= 2, agg[1][v], agg[0][v])
    out_ref[80:85, :] = agg[4]
    out_ref[85:88, :] = jnp.zeros((3, HALF), F32)


def step_down(is_low, low, high, f, u):
    f_high = f_after(low, f)
    u_low = g_before(high, f_high, u)
    return (f, u_low), (f_high, u)


def put_states(ref, states):
    for v in range(NV):
        ref[v * 32 : v * 32 + NI, :] = states[0][v]
        ref[v * 32 + NI : v * 32 + 2 * NI, :] = states[1][v]


def down_kernel(
    mine_ref, got_ref, own8_ref, got8_ref, own4_ref, got4_ref,
    q0_ref, q1_ref, q2_ref, q3_ref, own1_ref, got1_ref, keep_ref, send_ref,
):
    core, z, y = place()
    upper = y >= 2
    zero = jnp.zeros((NI, HALF), F32)
    at = [slice(v * NI, v * NI + NI) for v in range(NV)]
    f = [jnp.where(upper, got_ref[x, :], zero) for x in at]
    u = [
        jnp.where(upper, zero, got_ref[x, :] + got_ref[80 + v : 81 + v, :] * mine_ref[x, :])
        for v, x in enumerate(at)
    ]
    for is_low, mine, got in (
        (bit_clear(y, 1), own8_ref, got8_ref),
        (bit_clear(z, 4), own4_ref, got4_ref),
    ):
        low, high = ordered(is_low, load(mine), load(got))
        f, u = choose(is_low, *step_down(is_low, low, high, f, u))
    parts = members((q0_ref, q1_ref, q2_ref, q3_ref))
    fs, us = [f], [None, None, None, u]
    for r in range(3):
        fs.append(f_after(parts[r], fs[r]))
    for r in (3, 2, 1):
        us[r - 1] = g_before(parts[r], fs[r], us[r])
    m = lax.rem(z, 4)
    f = [pick(m, [x[v] for x in fs]) for v in range(NV)]
    u = [pick(m, [x[v] for x in us]) for v in range(NV)]
    is_low = core == 0
    low, high = ordered(is_low, load(own1_ref), load(got1_ref))
    low, high = step_down(is_low, low, high, f, u)
    put_states(keep_ref, choose(is_low, low, high))
    put_states(send_ref, choose(is_low, high, low))


def final_kernel(g_ref, resp_ref, mine_ref, other_ref, out_ref, scr, fu_scr, sems):
    even = place()[0] == 0

    def copy(v):
        at = pl.ds(v * PLANE, PLANE)
        return pltpu.make_async_copy(scr.at[at], out_ref.at[at], sems.at[v])

    for v in range(NV):
        x, y = mine_ref[v * 32 : v * 32 + 32, :], other_ref[v * 32 : v * 32 + 32, :]
        fu_scr[v, :, :HALF] = jnp.where(even, x, y)
        fu_scr[v, :, HALF:] = jnp.where(even, y, x)
        a, b = resp_ref[v, 0], resp_ref[v, 1]
        for i in range(NI):
            at = slice(v * PLANE + i * NJ, v * PLANE + i * NJ + NJ)
            f, u = fu_scr[v, i : i + 1, :], fu_scr[v, NI + i : NI + i + 1, :]
            scr[at, :] = g_ref[at, :] + a * f + b * u
        copy(v).start()
    for v in range(NV):
        copy(v).wait()


def swap(x, axis, size, flip):
    return lax.ppermute(x, axis, [(i, i ^ flip) for i in range(size)])


def across(x):
    pairs = []
    for q in range(64):
        z = q // 2 % 8
        other = (6 - z if z % 2 == 0 else 8 - z) % 8
        pairs.append((q, q + 2 * (other - z)))
    return lax.ppermute(x, "plane", pairs)


def body(adjoint, forcing, eigen_values, face_masks, line_coeffs, cross_coeffs):
    flat = (NV * PLANE, NK)
    a, f, e = (x.reshape(flat) for x in (adjoint, forcing, eigen_values))
    i_face, j_face = (NV, NJ, NK), (NV, NI, NK)
    w, ia, ib, ja, jb = call(
        faces_kernel, [flat, i_face, i_face, j_face, j_face], a, e, in_hbm=2, name="faces",
        scratch=[
            pltpu.VMEM(flat, F32),
            pltpu.VMEM(flat, F32),
            pltpu.VMEM((NV, 2, PLANE, HALF), F32),
            pltpu.SemaphoreType.DMA((NV, 2)),
        ],
    )
    ia = swap(ia, "line", 4, 1)
    ib = swap(ib, "line", 4, 3)
    ja = swap(ja, "plane", 64, 1)
    jb = lax.ppermute(jb, "plane", [(i, (i + 1 if i % 2 else i - 1) % 64) for i in range(64)])

    halves = (2, NV * PLANE, HALF)
    c, line_resp, maps, cross_resp, halo_resp, co, g, t, x = call(
        prep_kernel,
        [
            line_coeffs.shape, halves, (64, NK), (NV, 2, NJ, NK), (NV, 4, NJ, NK), (16, NK),
            flat, flat, cross_coeffs.shape,
        ],
        f, line_coeffs, cross_coeffs, face_masks, w, in_hbm=4, name="prep", flops=10**7,
        scratch=[
            pltpu.VMEM(flat, F32),
            pltpu.VMEM(face_masks.shape, face_masks.dtype),
            pltpu.SemaphoreType.DMA((4,)),
        ],
    )
    j_low, j_high, gi, edge, small = call(
        source_kernel, [j_face, j_face, (NV, 2, NJ, NK), halves, (MAPS + 64, NK)],
        g, t, ia, ib, ja, jb, c, x, halo_resp, maps,
        scratch=[pltpu.VMEM(flat, F32)], name="source",
    )
    smalls = [small] + [swap(small, "line", 4, d) for d in (1, 2, 3)]

    local, big = call(
        planes_kernel, [flat, (NV, 32, NK)], c, g, halo_resp, j_low, j_high, gi,
        scratch=[pltpu.VMEM(flat, F32)], name="planes", flops=10**7,
    )
    got_big = swap(big, "line", 4, 1)
    last_big = call(
        plane_pair_kernel, [(NV, 16, NK)], big, got_big, small, smalls[1], name="plane_pair"
    )[0]
    got_last_big = swap(last_big, "line", 4, 3)

    msg = (176, HALF)
    keep, send, gamma = call(
        edges_kernel, [msg, msg, (24, NK)], edge, line_resp, co, *smalls, name="edges"
    )
    solved = call(
        solved_kernel, [flat],
        local, line_resp, big, got_big, small, smalls[1], last_big, got_last_big, gamma,
        name="solved", flops=10**7,
    )[0]
    got = swap(send, "plane", 64, 1)
    own1 = call(chip_kernel, [msg], keep, got, name="chip")[0]
    quad = [own1] + [swap(own1, "plane", 64, d) for d in (2, 4, 6)]
    own4 = call(quad_kernel, [msg], *quad, name="quad")[0]
    got4 = across(own4)
    own8 = call(ring_kernel, [msg], own4, got4, name="ring")[0]
    got8 = swap(own8, "plane", 64, 16)
    top = call(top_kernel, [(88, HALF)], own8, got8, name="top")[0]
    got_top = swap(top, "plane", 64, 48)
    mine, send = call(
        down_kernel, [(160, HALF)] * 2,
        top, got_top, own8, got8, own4, got4, *quad, keep, got, name="down",
    )
    other = swap(send, "plane", 64, 1)
    out = call(
        final_kernel, [flat], solved, cross_resp, mine, other, out_hbm=True, name="final",
        scratch=[
            pltpu.VMEM(flat, F32),
            pltpu.VMEM((NV, 2 * NI, NK), F32),
            pltpu.SemaphoreType.DMA((NV,)),
        ],
    )[0]
    return out.reshape(NV, NI, NJ, NK)


def solution(mesh):
    return jax.shard_map(
        body,
        mesh=mesh,
        in_specs=(
            P(None, "line", "plane", None),
            P(None, "line", "plane", None),
            P(None, "line", "plane", None),
            P(None, "plane", None),
            P(None, None, "line", None),
            P(None, None, "plane", None),
        ),
        out_specs=P(None, "line", "plane", None),
        check_vma=False,
    )
```

profile of v0, /device:TPU:1, one launch (start us, length us, event | category | flops | bytes accessed | tf_op | source)
XLA Modules:
  0.0 57.7 jit_solution(11306753622522373521)
XLA Ops:
  0.0 1.5 %faces.1 = (f32[640,256]{1,0:T(8,128)S(1)}, f32[5,8,256]{2,1,0:T(8,128)S(1)}, f32[5,8,256]{2,1,0:T(8,128)S(1)}, f32[5,16,256]{2,1,0:T(8,128)S(1)}, f32[5,16,256]{2,1,0:T(8,128)S(1)}) custom-call(f32[640,256]{1,0:T(8,128)} %bitcast.4, f32[640,256]{1,0:T(8,128)} %bitcast.5), custom_call_target="tpu_custom_call" | custom-call | flops 1000 | bytes 1000 | tf_op jit(solution)/shard_map/faces/pallas_call | solution.py:31
  1.5 3.3 %collective-permute-start.2 = (f32[5,16,256]{2,1,0:T(8,128)S(1)}, f32[5,16,256]{2,1,0:T(8,128)S(1)}, u32[]{:S(2)}, u32[]{:S(2)}) collective-permute-start(f32[5,16,256]{2,1,0:T(8,128)S(1)} %get-tuple-element.38), channel_id=1, source_target_pairs={{0,1},{1,0},{2,3},{3,2},{4,5},{5,4},{6,7},{7,6},{8,9},{9,8},{10,11... | collective-permute-start | bytes 245768 | tf_op jit(solution)/shard_map/ppermute | solution.py:604
  4.8 1.1 %collective-permute-start = (f32[5,8,256]{2,1,0:T(8,128)S(1)}, f32[5,8,256]{2,1,0:T(8,128)S(1)}, u32[]{:S(2)}, u32[]{:S(2)}) collective-permute-start(f32[5,8,256]{2,1,0:T(8,128)S(1)} %get-tuple-element.36), channel_id=1, source_target_pairs={{0,64},{64,0},{128,192},{192,128},{1,65},{65,1},{129,193},{193,129... | collective-permute-start | bytes 122888 | tf_op jit(solution)/shard_map/ppermute | solution.py:604
  5.9 1.8 %collective-permute-start.1 = (f32[5,8,256]{2,1,0:T(8,128)S(1)}, f32[5,8,256]{2,1,0:T(8,128)S(1)}, u32[]{:S(2)}, u32[]{:S(2)}) collective-permute-start(f32[5,8,256]{2,1,0:T(8,128)S(1)} %get-tuple-element.37), channel_id=1, source_target_pairs={{0,192},{64,128},{128,64},{192,0},{1,193},{65,129},{129,65},{193,1... | collective-permute-start | bytes 122888 | tf_op jit(solution)/shard_map/ppermute | solution.py:604
  7.7 2.6 %prep.1 = (f32[5,6,16,256]{3,2,1,0:T(8,128)S(1)}, f32[2,640,128]{2,1,0:T(8,128)S(1)}, f32[64,256]{1,0:T(8,128)S(1)}, f32[5,2,8,256]{3,2,1,0:T(8,128)S(1)}, f32[5...) custom-call(f32[640,256]{1,0:T(8,128)} %bitcast.6, ...), custom_call_target="tpu_custom_call" | custom-call | flops 10000000 | bytes 10000000 | tf_op jit(solution)/shard_map/prep/pallas_call | solution.py:31
  10.9 1.5 %collective-permute-start.8 = (f32[104,256]{1,0:T(8,128)S(1)}, f32[104,256]{1,0:T(8,128)S(1)}, u32[]{:S(2)}, u32[]{:S(2)}) collective-permute-start(f32[104,256]{1,0:T(8,128)S(1)} %get-tuple-element.48.own_maps.own_ref), channel_id=1, source_target_pairs={{0,192},{64,128},{128,64},{192,0},{1,193},{65,129},{129,65},{193,1... | collective-permute-start | bytes 319496 | tf_op jit(solution)/shard_map/ppermute | solution.py:604
  12.4 0.7 %collective-permute-start.7 = (f32[104,256]{1,0:T(8,128)S(1)}, f32[104,256]{1,0:T(8,128)S(1)}, u32[]{:S(2)}, u32[]{:S(2)}) collective-permute-start(f32[104,256]{1,0:T(8,128)S(1)} %get-tuple-element.48.own_maps.own_ref), channel_id=1, source_target_pairs={{0,128},{64,192},{128,0},{192,64},{1,129},{65,193},{129,1},{193,65... | collective-permute-start | bytes 319496 | tf_op jit(solution)/shard_map/ppermute | solution.py:604
  13.1 1.2 %collective-permute-start.5 = (f32[104,256]{1,0:T(8,128)S(1)}, f32[104,256]{1,0:T(8,128)S(1)}, u32[]{:S(2)}, u32[]{:S(2)}) collective-permute-start(f32[104,256]{1,0:T(8,128)S(1)} %get-tuple-element.48.own_maps.own_ref), channel_id=1, source_target_pairs={{0,64},{64,0},{128,192},{192,128},{1,65},{65,1},{129,193},{193,129... | collective-permute-start | bytes 319496 | tf_op jit(solution)/shard_map/ppermute | solution.py:604
  14.2 1.5 %collective-permute-done.8.got3_ref = f32[104,256]{1,0:T(8,128)S(1)} collective-permute-done((f32[104,256]{1,0:T(8,128)S(1)}, f32[104,256]{1,0:T(8,128)S(1)}, u32[]{:S(2)}, u32[]{:S(2)}) %collective-permute-start.8) | collective-permute-done | bytes 106528 | tf_op jit(solution)/shard_map/ppermute | solution.py:604
  15.7 2.3 %collective-permute-done.7.got2_ref = f32[104,256]{1,0:T(8,128)S(1)} collective-permute-done((f32[104,256]{1,0:T(8,128)S(1)}, f32[104,256]{1,0:T(8,128)S(1)}, u32[]{:S(2)}, u32[]{:S(2)}) %collective-permute-start.7) | collective-permute-done | bytes 106528 | tf_op jit(solution)/shard_map/ppermute | solution.py:604
  18.4 9.4 %collective-permute-start.9 = (f32[176,128]{1,0:T(8,128)S(1)}, f32[176,128]{1,0:T(8,128)S(1)}, u32[]{:S(2)}, u32[]{:S(2)}) collective-permute-start(f32[176,128]{1,0:T(8,128)S(1)} %get-tuple-element.54), channel_id=1, source_target_pairs={{0,1},{1,0},{2,3},{3,2},{4,5},{5,4},{6,7},{7,6},{8,9},{9,8},{10,11... | collective-permute-start | bytes 270344 | tf_op jit(solution)/shard_map/ppermute | solution.py:604
  27.8 0.9 %collective-permute-done.9.got_ref.got1_ref = f32[176,128]{1,0:T(8,128)S(1)} collective-permute-done((f32[176,128]{1,0:T(8,128)S(1)}, f32[176,128]{1,0:T(8,128)S(1)}, u32[]{:S(2)}, u32[]{:S(2)}) %collective-permute-start.9) | collective-permute-done | bytes 90144 | tf_op jit(solution)/shard_map/ppermute | solution.py:604
  29.0 3.4 %collective-permute-start.10 = (f32[176,128]{1,0:T(8,128)S(1)}, f32[176,128]{1,0:T(8,128)S(1)}, u32[]{:S(2)}, u32[]{:S(2)}) collective-permute-start(f32[176,128]{1,0:T(8,128)S(1)} %chip.1.refs_0_.q0_ref), channel_id=1, source_target_pairs={{0,2},{1,3},{2,0},{3,1},{4,6},{5,7},{6,4},{7,5},{8,10},{9,11},{10,... | collective-permute-start | bytes 270344 | tf_op jit(solution)/shard_map/ppermute | solution.py:604
  32.4 2.1 %collective-permute-done.12.refs_3_.q3_ref = f32[176,128]{1,0:T(8,128)S(1)} collective-permute-done((f32[176,128]{1,0:T(8,128)S(1)}, f32[176,128]{1,0:T(8,128)S(1)}, u32[]{:S(2)}, u32[]{:S(2)}) %collective-permute-start.12) | collective-permute-done | bytes 90144 | tf_op jit(solution)/shard_map/ppermute | solution.py:604
  34.5 2.5 %collective-permute-done.11.refs_2_.q2_ref = f32[176,128]{1,0:T(8,128)S(1)} collective-permute-done((f32[176,128]{1,0:T(8,128)S(1)}, f32[176,128]{1,0:T(8,128)S(1)}, u32[]{:S(2)}, u32[]{:S(2)}) %collective-permute-start.11) | collective-permute-done | bytes 90144 | tf_op jit(solution)/shard_map/ppermute | solution.py:604
  37.1 0.8 %collective-permute-done.10.refs_1_.q1_ref = f32[176,128]{1,0:T(8,128)S(1)} collective-permute-done((f32[176,128]{1,0:T(8,128)S(1)}, f32[176,128]{1,0:T(8,128)S(1)}, u32[]{:S(2)}, u32[]{:S(2)}) %collective-permute-start.10) | collective-permute-done | bytes 90144 | tf_op jit(solution)/shard_map/ppermute | solution.py:604
  38.4 0.7 %collective-permute-start.4 = (f32[5,32,256]{2,1,0:T(8,128)S(1)}, f32[5,32,256]{2,1,0:T(8,128)S(1)}, u32[]{:S(2)}, u32[]{:S(2)}) collective-permute-start(f32[5,32,256]{2,1,0:T(8,128)S(1)} %get-tuple-element.47.own_ref), channel_id=1, source_target_pairs={{0,64},{64,0},{128,192},{192,128},{1,65},{65,1},{129,193},{193,129... | collective-permute-start | bytes 491528 | tf_op jit(solution)/shard_map/ppermute | solution.py:604
  39.1 4.5 %collective-permute-done.13.got_ref.got4_ref = f32[176,128]{1,0:T(8,128)S(1)} collective-permute-done((f32[176,128]{1,0:T(8,128)S(1)}, f32[176,128]{1,0:T(8,128)S(1)}, u32[]{:S(2)}, u32[]{:S(2)}) %collective-permute-start.13) | collective-permute-done | bytes 90144 | tf_op jit(solution)/shard_map/ppermute | solution.py:613
  43.7 3.4 %collective-permute-done.14.got_ref.got8_ref = f32[176,128]{1,0:T(8,128)S(1)} collective-permute-done((f32[176,128]{1,0:T(8,128)S(1)}, f32[176,128]{1,0:T(8,128)S(1)}, u32[]{:S(2)}, u32[]{:S(2)}) %collective-permute-start.14) | collective-permute-done | bytes 90144 | tf_op jit(solution)/shard_map/ppermute | solution.py:604
  47.1 0.7 %collective-permute-start.15 = (f32[88,128]{1,0:T(8,128)S(1)}, f32[88,128]{1,0:T(8,128)S(1)}, u32[]{:S(2)}, u32[]{:S(2)}) collective-permute-start(f32[88,128]{1,0:T(8,128)S(1)} %top.1.mine_ref), channel_id=1, source_target_pairs={{0,48},{1,49},{2,50},{3,51},{4,52},{5,53},{6,54},{7,55},{8,56},{9,... | collective-permute-start | bytes 135176 | tf_op jit(solution)/shard_map/ppermute | solution.py:604
  47.9 1.5 %collective-permute-start.6 = (f32[5,16,256]{2,1,0:T(8,128)S(1)}, f32[5,16,256]{2,1,0:T(8,128)S(1)}, u32[]{:S(2)}, u32[]{:S(2)}) collective-permute-start(f32[5,16,256]{2,1,0:T(8,128)S(1)} %plane_pair.1.mine2_ref), channel_id=1, source_target_pairs={{0,192},{64,128},{128,64},{192,0},{1,193},{65,129},{129,65},{193,1... | collective-permute-start | bytes 245768 | tf_op jit(solution)/shard_map/ppermute | solution.py:604
  49.5 1.9 %collective-permute-done.15.got_ref = f32[88,128]{1,0:T(8,128)S(1)} collective-permute-done((f32[88,128]{1,0:T(8,128)S(1)}, f32[88,128]{1,0:T(8,128)S(1)}, u32[]{:S(2)}, u32[]{:S(2)}) %collective-permute-start.15) | collective-permute-done | bytes 45088 | tf_op jit(solution)/shard_map/ppermute | solution.py:604
  51.5 4.4 %collective-permute-start.16 = (f32[160,128]{1,0:T(8,128)S(1)}, f32[160,128]{1,0:T(8,128)S(1)}, u32[]{:S(2)}, u32[]{:S(2)}) collective-permute-start(f32[160,128]{1,0:T(8,128)S(1)} %get-tuple-element.56), channel_id=1, source_target_pairs={{0,1},{1,0},{2,3},{3,2},{4,5},{5,4},{6,7},{7,6},{8,9},{9,8},{10,11... | collective-permute-start | bytes 245768 | tf_op jit(solution)/shard_map/ppermute | solution.py:604
  56.8 0.9 %final.1 = f32[640,256]{1,0:T(8,128)} custom-call(f32[640,256]{1,0:T(8,128)S(1)} %solved.1.g_ref, f32[5,2,8,256]{3,2,1,0:T(8,128)S(1)} %get-tuple-element.52.resp_ref, f32[160,128]{1,0:T(8,128)S(1)} %get-tuple-element.55.mine_ref, f32[160,128]{1,0:T(8,128)S(1)} %collective-permute-done.16.other_ref), custom_call_target="tpu_custom_call" | custom-call | flops 1000 | bytes 1000 | tf_op jit(solution)/shard_map/final/pallas_call | solution.py:31
  (23 shorter events, 3.0 us)
Async XLA Ops:
  1.5 8.9 %collective-permute-start.2 = (f32[5,16,256]{2,1,0:T(8,128)S(1)}, f32[5,16,256]{2,1,0:T(8,128)S(1)}, u32[]{:S(2)}, u32[]{:S(2)}) collective-permute-start(f32[5,16,256]{2,1,0:T(8,128)S(1)} %get-tuple-element.38), channel_id=1, source_target_pairs={{0,1},{1,0},{2,3},{3,2},{4,5},{5,4},{6,7},{7,6},{8,9},{9,8},{10,11... | collective-permute-start | bytes 245768 | tf_op jit(solution)/shard_map/ppermute | solution.py:604
  4.8 5.6 %collective-permute-start.3 = (f32[5,16,256]{2,1,0:T(8,128)S(1)}, f32[5,16,256]{2,1,0:T(8,128)S(1)}, u32[]{:S(2)}, u32[]{:S(2)}) collective-permute-start(f32[5,16,256]{2,1,0:T(8,128)S(1)} %get-tuple-element.39), channel_id=1, source_target_pairs={{0,63},{1,2},{2,1},{3,4},{4,3},{5,6},{6,5},{7,8},{8,7},{9,10},{10,... | collective-permute-start | bytes 245768 | tf_op jit(solution)/shard_map/ppermute | solution.py:632
  4.8 5.5 %collective-permute-start = (f32[5,8,256]{2,1,0:T(8,128)S(1)}, f32[5,8,256]{2,1,0:T(8,128)S(1)}, u32[]{:S(2)}, u32[]{:S(2)}) collective-permute-start(f32[5,8,256]{2,1,0:T(8,128)S(1)} %get-tuple-element.36), channel_id=1, source_target_pairs={{0,64},{64,0},{128,192},{192,128},{1,65},{65,1},{129,193},{193,129... | collective-permute-start | bytes 122888 | tf_op jit(solution)/shard_map/ppermute | solution.py:604
  5.9 4.4 %collective-permute-start.1 = (f32[5,8,256]{2,1,0:T(8,128)S(1)}, f32[5,8,256]{2,1,0:T(8,128)S(1)}, u32[]{:S(2)}, u32[]{:S(2)}) collective-permute-start(f32[5,8,256]{2,1,0:T(8,128)S(1)} %get-tuple-element.37), channel_id=1, source_target_pairs={{0,192},{64,128},{128,64},{192,0},{1,193},{65,129},{129,65},{193,1... | collective-permute-start | bytes 122888 | tf_op jit(solution)/shard_map/ppermute | solution.py:604
  10.9 4.9 %collective-permute-start.8 = (f32[104,256]{1,0:T(8,128)S(1)}, f32[104,256]{1,0:T(8,128)S(1)}, u32[]{:S(2)}, u32[]{:S(2)}) collective-permute-start(f32[104,256]{1,0:T(8,128)S(1)} %get-tuple-element.48.own_maps.own_ref), channel_id=1, source_target_pairs={{0,192},{64,128},{128,64},{192,0},{1,193},{65,129},{129,65},{193,1... | collective-permute-start | bytes 319496 | tf_op jit(solution)/shard_map/ppermute | solution.py:604
  12.4 5.6 %collective-permute-start.7 = (f32[104,256]{1,0:T(8,128)S(1)}, f32[104,256]{1,0:T(8,128)S(1)}, u32[]{:S(2)}, u32[]{:S(2)}) collective-permute-start(f32[104,256]{1,0:T(8,128)S(1)} %get-tuple-element.48.own_maps.own_ref), channel_id=1, source_target_pairs={{0,128},{64,192},{128,0},{192,64},{1,129},{65,193},{129,1},{193,65... | collective-permute-start | bytes 319496 | tf_op jit(solution)/shard_map/ppermute | solution.py:604
  13.1 4.9 %collective-permute-start.5 = (f32[104,256]{1,0:T(8,128)S(1)}, f32[104,256]{1,0:T(8,128)S(1)}, u32[]{:S(2)}, u32[]{:S(2)}) collective-permute-start(f32[104,256]{1,0:T(8,128)S(1)} %get-tuple-element.48.own_maps.own_ref), channel_id=1, source_target_pairs={{0,64},{64,0},{128,192},{192,128},{1,65},{65,1},{129,193},{193,129... | collective-permute-start | bytes 319496 | tf_op jit(solution)/shard_map/ppermute | solution.py:604
  18.4 10.4 %collective-permute-start.9 = (f32[176,128]{1,0:T(8,128)S(1)}, f32[176,128]{1,0:T(8,128)S(1)}, u32[]{:S(2)}, u32[]{:S(2)}) collective-permute-start(f32[176,128]{1,0:T(8,128)S(1)} %get-tuple-element.54), channel_id=1, source_target_pairs={{0,1},{1,0},{2,3},{3,2},{4,5},{5,4},{6,7},{7,6},{8,9},{9,8},{10,11... | collective-permute-start | bytes 270344 | tf_op jit(solution)/shard_map/ppermute | solution.py:604
  28.8 5.8 %collective-permute-start.12 = (f32[176,128]{1,0:T(8,128)S(1)}, f32[176,128]{1,0:T(8,128)S(1)}, u32[]{:S(2)}, u32[]{:S(2)}) collective-permute-start(f32[176,128]{1,0:T(8,128)S(1)} %chip.1.refs_0_.q0_ref), channel_id=1, source_target_pairs={{0,6},{1,7},{2,4},{3,5},{4,2},{5,3},{6,0},{7,1},{8,14},{9,15},{10,... | collective-permute-start | bytes 270344 | tf_op jit(solution)/shard_map/ppermute | solution.py:604
  28.9 8.2 %collective-permute-start.11 = (f32[176,128]{1,0:T(8,128)S(1)}, f32[176,128]{1,0:T(8,128)S(1)}, u32[]{:S(2)}, u32[]{:S(2)}) collective-permute-start(f32[176,128]{1,0:T(8,128)S(1)} %chip.1.refs_0_.q0_ref), channel_id=1, source_target_pairs={{0,4},{1,5},{2,6},{3,7},{4,0},{5,1},{6,2},{7,3},{8,12},{9,13},{10,... | collective-permute-start | bytes 270344 | tf_op jit(solution)/shard_map/ppermute | solution.py:604
  29.0 8.9 %collective-permute-start.10 = (f32[176,128]{1,0:T(8,128)S(1)}, f32[176,128]{1,0:T(8,128)S(1)}, u32[]{:S(2)}, u32[]{:S(2)}) collective-permute-start(f32[176,128]{1,0:T(8,128)S(1)} %chip.1.refs_0_.q0_ref), channel_id=1, source_target_pairs={{0,2},{1,3},{2,0},{3,1},{4,6},{5,7},{6,4},{7,5},{8,10},{9,11},{10,... | collective-permute-start | bytes 270344 | tf_op jit(solution)/shard_map/ppermute | solution.py:604
  37.9 5.7 %collective-permute-start.13 = (f32[176,128]{1,0:T(8,128)S(1)}, f32[176,128]{1,0:T(8,128)S(1)}, u32[]{:S(2)}, u32[]{:S(2)}) collective-permute-start(f32[176,128]{1,0:T(8,128)S(1)} %quad.1.own_ref.own4_ref), channel_id=1, source_target_pairs={{0,12},{1,13},{2,14},{3,15},{4,8},{5,9},{6,10},{7,11},{8,4},{9,5},... | collective-permute-start | bytes 270344 | tf_op jit(solution)/shard_map/ppermute | solution.py:613
  38.4 9.4 %collective-permute-start.4 = (f32[5,32,256]{2,1,0:T(8,128)S(1)}, f32[5,32,256]{2,1,0:T(8,128)S(1)}, u32[]{:S(2)}, u32[]{:S(2)}) collective-permute-start(f32[5,32,256]{2,1,0:T(8,128)S(1)} %get-tuple-element.47.own_ref), channel_id=1, source_target_pairs={{0,64},{64,0},{128,192},{192,128},{1,65},{65,1},{129,193},{193,129... | collective-permute-start | bytes 491528 | tf_op jit(solution)/shard_map/ppermute | solution.py:604
  43.6 3.5 %collective-permute-start.14 = (f32[176,128]{1,0:T(8,128)S(1)}, f32[176,128]{1,0:T(8,128)S(1)}, u32[]{:S(2)}, u32[]{:S(2)}) collective-permute-start(f32[176,128]{1,0:T(8,128)S(1)} %ring.1.own_ref.own8_ref), channel_id=1, source_target_pairs={{0,16},{1,17},{2,18},{3,19},{4,20},{5,21},{6,22},{7,23},{8,24},{9,... | collective-permute-start | bytes 270344 | tf_op jit(solution)/shard_map/ppermute | solution.py:604
  47.1 4.2 %collective-permute-start.15 = (f32[88,128]{1,0:T(8,128)S(1)}, f32[88,128]{1,0:T(8,128)S(1)}, u32[]{:S(2)}, u32[]{:S(2)}) collective-permute-start(f32[88,128]{1,0:T(8,128)S(1)} %top.1.mine_ref), channel_id=1, source_target_pairs={{0,48},{1,49},{2,50},{3,51},{4,52},{5,53},{6,54},{7,55},{8,56},{9,... | collective-permute-start | bytes 135176 | tf_op jit(solution)/shard_map/ppermute | solution.py:604
  47.9 7.9 %collective-permute-start.6 = (f32[5,16,256]{2,1,0:T(8,128)S(1)}, f32[5,16,256]{2,1,0:T(8,128)S(1)}, u32[]{:S(2)}, u32[]{:S(2)}) collective-permute-start(f32[5,16,256]{2,1,0:T(8,128)S(1)} %plane_pair.1.mine2_ref), channel_id=1, source_target_pairs={{0,192},{64,128},{128,64},{192,0},{1,193},{65,129},{129,65},{193,1... | collective-permute-start | bytes 245768 | tf_op jit(solution)/shard_map/ppermute | solution.py:604
  51.5 5.3 %collective-permute-start.16 = (f32[160,128]{1,0:T(8,128)S(1)}, f32[160,128]{1,0:T(8,128)S(1)}, u32[]{:S(2)}, u32[]{:S(2)}) collective-permute-start(f32[160,128]{1,0:T(8,128)S(1)} %get-tuple-element.56), channel_id=1, source_target_pairs={{0,1},{1,0},{2,3},{3,2},{4,5},{5,4},{6,7},{7,6},{8,9},{9,8},{10,11... | collective-permute-start | bytes 245768 | tf_op jit(solution)/shard_map/ppermute | solution.py:604
where the time goes:
time: 57.8 us; the launch traced here: 57.7 us
  starting transfers between devices  30.1 us (52%)
  waiting for transfers between devices  20.5 us (35%)
  Pallas kernels  6.94 us (12%)
    ppermute x15, starting transfers between devices, swap(): return lax.ppermute(x, axis, [(i, i ^ flip) for i in range(size)])  30 us
    ppermute x15, waiting for transfers between devices, swap(): return lax.ppermute(x, axis, [(i, i ^ flip) for i in range(size)])  16 us
    pallas_call x13, Pallas kernels, call(): pl.pallas_call(kernel, out_shape=outs, in_specs=[pl.BlockSpec(memory_spac...  6.94 us
    ppermute x1, waiting for transfers between devices, across(): return lax.ppermute(x, 'plane', pairs)  4.49 us
  transfers between devices with their start and end apart: 17, of which 10 were waited for; matrix products, arithmetic and copies ran while one was open for 0% of the time, Pallas kernels for 6%

commit v1 on v0

--- a/solution.py
+++ b/solution.py
@@ -10,7 +10,7 @@
 HALF = NK // 2
 PLANE = NI * NJ
 TILE = (NJ, NK)
-MAPS = NV * 8
+MAPS = NV * 16
 
 
 def rows_of(shape):
@@ -85,20 +85,25 @@
 
 
 def prep_kernel(
-    f_hbm, c_hbm, x_hbm, m_hbm, w_ref,
-    c_ref, line_resp_ref, maps_ref, cross_resp_ref, halo_resp_ref, co_ref, g_ref, t_ref, x_ref,
-    f_ref, m_ref, sems,
+    x_hbm, m_hbm, w_ref, f_ref, c_ref,
+    half_ref, line_resp_ref, maps_ref, cross_resp_ref, halo_resp_ref, co_ref, g_ref, t_ref, x_ref,
+    m_ref, sems,
 ):
-    pairs = ((c_hbm, c_ref), (x_hbm, x_ref), (m_hbm, m_ref), (f_hbm, f_ref))
-    copies = [pltpu.make_async_copy(a, b, sems.at[n]) for n, (a, b) in enumerate(pairs)]
+    copies = [
+        pltpu.make_async_copy(x_hbm, x_ref, sems.at[0]),
+        pltpu.make_async_copy(m_hbm, m_ref, sems.at[1]),
+    ]
     for copy in copies:
         copy.start()
-    copies[0].wait()
+    even = place()[0] == 0
+    for v in range(NV):
+        for n in range(6):
+            c = c_ref[v, n]
+            half_ref[v, n] = jnp.where(even, c[:, :HALF], c[:, HALF:])
     line_coeffs_of(c_ref, line_resp_ref, maps_ref)
-    copies[1].wait()
+    for copy in copies:
+        copy.wait()
     cross_coeffs_of(x_ref, cross_resp_ref, halo_resp_ref, co_ref)
-    copies[2].wait()
-    copies[3].wait()
     local_source(w_ref, f_ref, m_ref, x_ref, g_ref, t_ref)
 
 
@@ -215,8 +220,8 @@
 
 
 def source_kernel(
-    g_in, t_in, ia_ref, ib_ref, ja_ref, jb_ref, c_ref, x_ref, halo_ref, maps_ref,
-    low_ref, high_ref, gi_ref, edge_ref, msg_ref, t_scr,
+    t_in, ia_ref, ib_ref, ja_ref, jb_ref, x_ref, halo_ref, co_ref,
+    low_ref, high_ref, gi_ref, keep_ref, send_ref, t_scr,
 ):
     p, q = lax.axis_index("line"), lax.axis_index("plane")
     even_line, even_plane = lax.rem(p, 2) == 0, lax.rem(q, 2) == 0
@@ -245,14 +250,43 @@
                 t = t + ends[0]
             if i == NI - 1:
                 t = t + ends[1]
-            t_scr[at, :] = t
-    local_sweeps(c_ref, t_scr, t_scr, edge_ref, msg_ref, small=True)
-    msg_ref[MAPS:, :] = maps_ref[...]
-
-
-def local_sweeps(c_ref, src_ref, tmp_ref, out_ref, msg_ref, small):
-    row = rows_of(TILE)
-    zero = jnp.zeros(TILE, F32)
+            for half in range(2):
+                t_scr[half, at, :] = t[:, half * HALF : half * HALF + HALF]
+        for n in range(2):
+            a, b = (t_scr[half, pl.ds(v * PLANE + n, NI, stride=NJ), :] for half in range(2))
+            at = slice(v * 32 + n * NI, v * 32 + n * NI + NI)
+            keep_ref[at, :] = jnp.where(even_plane, a, b)
+            send_ref[at, :] = jnp.where(even_plane, b, a)
+    a, b = co_ref[:, :HALF], co_ref[:, HALF:]
+    keep_ref[160:, :] = jnp.where(even_plane, a, b)
+    send_ref[160:, :] = jnp.where(even_plane, b, a)
+
+
+def layers_kernel(keep_ref, got_ref, c_ref, maps_ref, out_ref, msg_ref, t_scr):
+    even = place()[0] == 0
+    tile = (NJ, HALF)
+    row = rows_of(tile)
+    low, high = ordered(even, [keep_ref[...]], [got_ref[...]])
+    low, high = low[0], high[0]
+    for v in range(NV):
+        for i in range(NI):
+            a, b = v * 32 + i, v * 32 + NI + i
+            t_scr[v * PLANE + i * NJ : v * PLANE + i * NJ + NJ, :] = jnp.where(
+                row == 0,
+                low[a : a + 1],
+                jnp.where(row == 1, low[b : b + 1], jnp.where(row == 2, high[a : a + 1], high[b : b + 1])),
+            )
+    ends = local_sweeps(c_ref, t_scr, out_ref, out_ref)
+    for v in range(NV):
+        for n in range(2):
+            a, b = ends[v][2 * n : 2 * n + 2]
+            at = v * 16 + n * 8
+            msg_ref[at : at + 8, :] = jnp.where(row < 4, a, pltpu.roll(b, 4, 0))
+    msg_ref[MAPS:, :] = jnp.where(even, maps_ref[:, :HALF], maps_ref[:, HALF:])
+
+
+def local_sweeps(c_ref, src_ref, tmp_ref, out_ref):
+    zero = jnp.zeros((NJ, src_ref.shape[-1]), F32)
     one, two = [zero] * NV, [zero] * NV
     for i in range(NI):
         for v in range(NV):
@@ -267,26 +301,8 @@
             first, second, scale = (c_ref[v, n, i : i + 1, :] for n in range(3, 6))
             at = slice(v * PLANE + i * NJ, v * PLANE + i * NJ + NJ)
             one[v], two[v] = scale * tmp_ref[at, :] + first * one[v] + second * two[v], one[v]
-            if small:
-                for part in range(2):
-                    out_ref[part, at, :] = one[v][:, part * HALF : part * HALF + HALF]
-            else:
-                out_ref[at, :] = one[v]
-    for v in range(NV):
-        if small:
-            a, b, c, d = ends[v][0], ends[v][1], one[v], two[v]
-            msg_ref[v * 8 : v * 8 + 8, :] = jnp.where(
-                row < 2,
-                a,
-                jnp.where(
-                    row < 4,
-                    pltpu.roll(b, 2, 0),
-                    jnp.where(row < 6, pltpu.roll(c, 4, 0), pltpu.roll(d, 6, 0)),
-                ),
-            )
-        else:
-            for n, x in enumerate((ends[v][0], ends[v][1], one[v], two[v])):
-                msg_ref[v, n * NJ : n * NJ + NJ, :] = x
+            out_ref[at, :] = one[v]
+    return [ends[v] + (one[v], two[v]) for v in range(NV)]
 
 
 def planes_kernel(c_ref, g_ref, halo_ref, low_ref, high_ref, gi_ref, out_ref, msg_ref, g_scr):
@@ -300,11 +316,14 @@
             if i == NI - 1:
                 g = g + gi_ref[v, 1]
             g_scr[at, :] = g
-    local_sweeps(c_ref, g_scr, out_ref, out_ref, msg_ref, small=False)
-
-
-def maps_of(ref, v):
-    return ref[MAPS + v * 12 : MAPS + v * 12 + 12, :]
+    ends = local_sweeps(c_ref, g_scr, out_ref, out_ref)
+    for v in range(NV):
+        for n, x in enumerate(ends[v]):
+            msg_ref[v, n * NJ : n * NJ + NJ, :] = x
+
+
+def maps_of(ref, v, at=MAPS):
+    return ref[at + v * 12 : at + v * 12 + 12, :]
 
 
 def line_pair(p, own, got):
@@ -373,24 +392,19 @@
 
 
 def edges_kernel(
-    edge_ref, resp_ref, co_ref, own_ref, got1_ref, got2_ref, got3_ref,
-    keep_ref, send_ref, gamma_ref,
+    layers_ref, resp_ref, keep_ref, gotc_ref, own_ref, got1_ref, got2_ref, got3_ref,
+    low_ref, high_ref, chip_ref, maps_ref,
 ):
-    p = lax.axis_index("line")
-    even = place()[0] == 0
+    p, core = lax.axis_index("line"), place()[0]
     refs = (own_ref, got1_ref, got2_ref, got3_ref)
-
-    def put(at, x, y):
-        keep_ref[at, :] = jnp.where(even, x, y)
-        send_ref[at, :] = jnp.where(even, y, x)
-
     for v in range(NV):
         rows, maps = [], []
         for r in range(4):
-            rows.append(pick(p, [refs[r ^ own][v * 8 : v * 8 + 8, :] for own in range(4)]))
+            at = slice(v * 16, v * 16 + 16)
+            rows.append(pick(p, [refs[r ^ own][at, :] for own in range(4)]))
             maps.append(pick(p, [maps_of(refs[r ^ own], v) for own in range(4)]))
-        part = [[x[n * 2 : n * 2 + 2] for n in range(4)] for x in rows]
-        zero = jnp.zeros((2, NK), F32)
+        part = [[x[n * 4 : n * 4 + 4] for n in range(4)] for x in rows]
+        zero = jnp.zeros((4, HALF), F32)
         low = [(zero, zero), (part[0][0], part[0][1])]
         for r in (1, 2):
             low.append(l_after(maps[r], part[r][:2], low[r]))
@@ -399,32 +413,36 @@
             high[r - 1] = u_before(maps[r], part[r][2:], low[r], high[r])
         states = [pick(p, [x[t] for x in low]) for t in range(2)]
         states += [pick(p, [x[t] for x in high]) for t in range(2)]
-        for t in range(2):
-            parts = []
-            for half in range(2):
-                lane = slice(half * HALF, half * HALF + HALF)
-                x = edge_ref[half, pl.ds(v * PLANE + t, NI, stride=NJ), :]
-                for n in range(4):
-                    r = resp_ref[half, pl.ds(v * PLANE + n, NI, stride=NJ), :]
-                    x = x + r * states[n][t : t + 1, lane]
-                parts.append(x)
-            put(slice(v * 32 + t * 16, v * 32 + t * 16 + 16), *parts)
+        answers = [resp_ref[core, pl.ds(v * PLANE + n, NI, stride=NJ), :] for n in range(4)]
+        for t in range(4):
+            x = layers_ref[pl.ds(v * PLANE + t, NI, stride=NJ), :]
+            for n in range(4):
+                x = x + answers[n] * states[n][t : t + 1]
+            at = v * 32 + (t % 2) * NI
+            (low_ref, high_ref)[t // 2][at : at + NI, :] = x
+        maps_ref[v * 12 : v * 12 + 12, :] = maps_of(got1_ref, v)
         for n, x in enumerate(pair_gamma(maps[2], maps[3])):
-            gamma_ref[v * 4 + n : v * 4 + n + 1, :] = x
-    put(slice(160, 176), co_ref[:, :HALF], co_ref[:, HALF:])
-    gamma_ref[20:24, :] = jnp.zeros((4, NK), F32)
+            maps_ref[60 + v * 4 + n : 61 + v * 4 + n, :] = x
+    own, other = keep_ref[160:, :], gotc_ref[160:, :]
+    low_ref[160:, :] = jnp.where(core == 0, own, other)
+    high_ref[160:, :] = jnp.where(core == 0, other, own)
+    store(chip_ref, compose(load(low_ref), load(high_ref)))
 
 
 def last_gamma(ref, v):
-    return [ref[v * 4 + n : v * 4 + n + 1, :] for n in range(4)]
+    return [ref[60 + v * 4 + n : 61 + v * 4 + n, :] for n in range(4)]
 
 
 def big_parts(ref, maps_ref, v):
-    return [maps_of(maps_ref, v)] + [ref[v, n * NJ : n * NJ + NJ, :] for n in range(4)]
-
-
-def plane_pair_kernel(own_ref, got_ref, own_maps, got_maps, out_ref):
+    return [maps_of(maps_ref, v, 0)] + [ref[v, n * NJ : n * NJ + NJ, :] for n in range(4)]
+
+
+def plane_pair_kernel(own_ref, got_ref, own_maps, half_ref, other_ref, out_ref, got_maps):
     p = lax.axis_index("line")
+    even = place()[0] == 0
+    a, b = half_ref[...], other_ref[...]
+    got_maps[:, :HALF] = jnp.where(even, a, b)
+    got_maps[:, HALF:] = jnp.where(even, b, a)
     for v in range(NV):
         low, high = line_pair(p, big_parts(own_ref, own_maps, v), big_parts(got_ref, got_maps, v))
         a, b = pair_states(p, low, high)
@@ -433,14 +451,14 @@
 
 
 def solved_kernel(
-    local_ref, resp_ref, own_ref, got_ref, own_maps, got_maps, mine2_ref, got2_ref, last_ref, out_ref
+    local_ref, resp_ref, own_ref, got_ref, own_maps, got_maps, mine2_ref, got2_ref, out_ref
 ):
     p = lax.axis_index("line")
     for v in range(NV):
         low, high = line_pair(p, big_parts(own_ref, own_maps, v), big_parts(got_ref, got_maps, v))
         mine = (mine2_ref[v, :NJ, :], mine2_ref[v, NJ:, :])
         got = (got2_ref[v, :NJ, :], got2_ref[v, NJ:, :])
-        states = entering(p, low, high, mine, got, last_gamma(last_ref, v))
+        states = entering(p, low, high, mine, got, last_gamma(got_maps, v))
         for i in range(NI):
             at = v * PLANE + i * NJ
             for part in range(2):
@@ -501,10 +519,6 @@
     return lax.rem(z // n, 2) == 0
 
 
-def chip_kernel(keep_ref, got_ref, out_ref):
-    store(out_ref, compose(*ordered(place()[0] == 0, load(keep_ref), load(got_ref))))
-
-
 def members(refs):
     m = lax.rem(place()[1], 4)
     parts = [load(r) for r in refs]
@@ -516,10 +530,10 @@
 
 def quad_kernel(*refs):
     a, b, c, d = members(refs[:4])
-    store(refs[4], compose(compose(a, b), compose(c, d)))
-
-
-def ring_kernel(own_ref, got_ref, out_ref):
+    store(refs[-1], compose(compose(a, b), compose(c, d)))
+
+
+def ring_kernel(own_ref, got_ref, after_ref, out_ref):
     store(out_ref, compose(*ordered(bit_clear(place()[1], 4), load(own_ref), load(got_ref))))
 
 
@@ -546,7 +560,7 @@
 
 def down_kernel(
     mine_ref, got_ref, own8_ref, got8_ref, own4_ref, got4_ref,
-    q0_ref, q1_ref, q2_ref, q3_ref, own1_ref, got1_ref, keep_ref, send_ref,
+    q0_ref, q1_ref, q2_ref, q3_ref, low_ref, high_ref, after_ref, keep_ref, send_ref,
 ):
     core, z, y = place()
     upper = y >= 2
@@ -573,8 +587,7 @@
     f = [pick(m, [x[v] for x in fs]) for v in range(NV)]
     u = [pick(m, [x[v] for x in us]) for v in range(NV)]
     is_low = core == 0
-    low, high = ordered(is_low, load(own1_ref), load(got1_ref))
-    low, high = step_down(is_low, low, high, f, u)
+    low, high = step_down(is_low, load(low_ref), load(high_ref), f, u)
     put_states(keep_ref, choose(is_low, low, high))
     put_states(send_ref, choose(is_low, high, low))
 
@@ -632,57 +645,61 @@
     jb = lax.ppermute(jb, "plane", [(i, (i + 1 if i % 2 else i - 1) % 64) for i in range(64)])
 
     halves = (2, NV * PLANE, HALF)
-    c, line_resp, maps, cross_resp, halo_resp, co, g, t, x = call(
+    half, line_resp, maps, cross_resp, halo_resp, co, g, t, x = call(
         prep_kernel,
         [
-            line_coeffs.shape, halves, (64, NK), (NV, 2, NJ, NK), (NV, 4, NJ, NK), (16, NK),
-            flat, flat, cross_coeffs.shape,
+            line_coeffs.shape[:3] + (HALF,), halves, (64, NK), (NV, 2, NJ, NK), (NV, 4, NJ, NK),
+            (16, NK), flat, flat, cross_coeffs.shape,
         ],
-        f, line_coeffs, cross_coeffs, face_masks, w, in_hbm=4, name="prep", flops=10**7,
+        cross_coeffs, face_masks, w, f, line_coeffs, in_hbm=2, name="prep", flops=10**7,
         scratch=[
-            pltpu.VMEM(flat, F32),
             pltpu.VMEM(face_masks.shape, face_masks.dtype),
-            pltpu.SemaphoreType.DMA((4,)),
+            pltpu.SemaphoreType.DMA((2,)),
         ],
     )
-    j_low, j_high, gi, edge, small = call(
-        source_kernel, [j_face, j_face, (NV, 2, NJ, NK), halves, (MAPS + 64, NK)],
-        g, t, ia, ib, ja, jb, c, x, halo_resp, maps,
-        scratch=[pltpu.VMEM(flat, F32)], name="source",
+    msg = (176, HALF)
+    j_low, j_high, gi, keep, send = call(
+        source_kernel, [j_face, j_face, (NV, 2, NJ, NK), msg, msg],
+        t, ia, ib, ja, jb, x, halo_resp, co, scratch=[pltpu.VMEM(halves, F32)], name="source",
+    )
+    got = swap(send, "plane", 64, 1)
+    half_flat = (NV * PLANE, HALF)
+    layers, small = call(
+        layers_kernel, [half_flat, (MAPS + 64, HALF)], keep, got, half, maps,
+        scratch=[pltpu.VMEM(half_flat, F32)], name="layers",
     )
     smalls = [small] + [swap(small, "line", 4, d) for d in (1, 2, 3)]
+    low, high, chip, pair_maps = call(
+        edges_kernel, [msg, msg, msg, (80, HALF)],
+        layers, line_resp, keep, got, *smalls, name="edges",
+    )
+    quad = [chip] + [swap(chip, "plane", 64, d) for d in (2, 4, 6)]
 
     local, big = call(
-        planes_kernel, [flat, (NV, 32, NK)], c, g, halo_resp, j_low, j_high, gi,
+        planes_kernel, [flat, (NV, 32, NK)], line_coeffs, g, halo_resp, j_low, j_high, gi,
         scratch=[pltpu.VMEM(flat, F32)], name="planes", flops=10**7,
     )
     got_big = swap(big, "line", 4, 1)
-    last_big = call(
-        plane_pair_kernel, [(NV, 16, NK)], big, got_big, small, smalls[1], name="plane_pair"
-    )[0]
+    last_big, line_maps = call(
+        plane_pair_kernel, [(NV, 16, NK), (80, NK)],
+        big, got_big, maps, pair_maps, swap(pair_maps, "plane", 64, 1), name="plane_pair",
+    )
     got_last_big = swap(last_big, "line", 4, 3)
-
-    msg = (176, HALF)
-    keep, send, gamma = call(
-        edges_kernel, [msg, msg, (24, NK)], edge, line_resp, co, *smalls, name="edges"
-    )
     solved = call(
         solved_kernel, [flat],
-        local, line_resp, big, got_big, small, smalls[1], last_big, got_last_big, gamma,
+        local, line_resp, big, got_big, maps, line_maps, last_big, got_last_big,
         name="solved", flops=10**7,
     )[0]
-    got = swap(send, "plane", 64, 1)
-    own1 = call(chip_kernel, [msg], keep, got, name="chip")[0]
-    quad = [own1] + [swap(own1, "plane", 64, d) for d in (2, 4, 6)]
-    own4 = call(quad_kernel, [msg], *quad, name="quad")[0]
+
+    own4 = call(quad_kernel, [msg], *quad, big, name="quad")[0]
     got4 = across(own4)
-    own8 = call(ring_kernel, [msg], own4, got4, name="ring")[0]
+    own8 = call(ring_kernel, [msg], own4, got4, last_big, name="ring")[0]
     got8 = swap(own8, "plane", 64, 16)
     top = call(top_kernel, [(88, HALF)], own8, got8, name="top")[0]
     got_top = swap(top, "plane", 64, 48)
     mine, send = call(
         down_kernel, [(160, HALF)] * 2,
-        top, got_top, own8, got8, own4, got4, *quad, keep, got, name="down",
+        top, got_top, own8, got8, own4, got4, *quad, low, high, solved, name="down",
     )
     other = swap(send, "plane", 64, 1)
     out = call(

time: 57.8 us -> 55.8 us (0.965)
  waiting for transfers between devices: 20.5 us -> 12.8 us
  starting transfers between devices: 30.1 us -> 36.3 us
    ppermute x15 -> x16, starting transfers between devices: 30 us -> 35.8 us  [swap(): return lax.ppermute(x, axis, [(i, i ^ flip) for i in range(size)])]
    ppermute x15 -> x16, waiting for transfers between devices: 16 us -> 11.9 us  [swap(): return lax.ppermute(x, axis, [(i, i ^ flip) for i in range(size)])]
    ppermute x1, waiting for transfers between devices: 4.49 us -> 0.88 us  [across(): return lax.ppermute(x, 'plane', pairs)]
  transfers between devices with their start and end apart: 17 -> 18, of which waited for: 10 -> 10; matrix products, arithmetic and copies ran while one was open for 0% -> 0% of each run, Pallas kernels for 6% -> 6%
where the time goes in v1:
time: 55.8 us; the launch traced here: 55.7 us
  starting transfers between devices  36.3 us (65%)
  waiting for transfers between devices  12.8 us (23%)
  Pallas kernels  6.52 us (12%)
    ppermute x16, starting transfers between devices, swap(): return lax.ppermute(x, axis, [(i, i ^ flip) for i in range(size)])  35.8 us
    ppermute x16, waiting for transfers between devices, swap(): return lax.ppermute(x, axis, [(i, i ^ flip) for i in range(size)])  11.9 us
    pallas_call x13, Pallas kernels, call(): pl.pallas_call(kernel, out_shape=outs, in_specs=[pl.BlockSpec(memory_spac...  6.52 us
  transfers between devices with their start and end apart: 18, of which 10 were waited for; matrix products, arithmetic and copies ran while one was open for 0% of the time, Pallas kernels for 6%

profile of v1, /device:TPU:1, one launch (start us, length us, event | category | flops | bytes accessed | tf_op | source)
XLA Modules:
  0.0 55.7 jit_solution(4028085804369238067)
XLA Ops:
  0.0 1.6 %faces.1 = (f32[640,256]{1,0:T(8,128)S(1)}, f32[5,8,256]{2,1,0:T(8,128)S(1)}, f32[5,8,256]{2,1,0:T(8,128)S(1)}, f32[5,16,256]{2,1,0:T(8,128)S(1)}, f32[5,16,256]{2,1,0:T(8,128)S(1)}) custom-call(f32[640,256]{1,0:T(8,128)} %bitcast.5, f32[640,256]{1,0:T(8,128)} %bitcast.6), custom_call_target="tpu_custom_call" | custom-call | flops 1000 | bytes 1000 | tf_op jit(solution)/shard_map/faces/pallas_call | solution.py:31
  1.6 3.3 %collective-permute-start.2 = (f32[5,16,256]{2,1,0:T(8,128)S(1)}, f32[5,16,256]{2,1,0:T(8,128)S(1)}, u32[]{:S(2)}, u32[]{:S(2)}) collective-permute-start(f32[5,16,256]{2,1,0:T(8,128)S(1)} %get-tuple-element.42), channel_id=1, source_target_pairs={{0,1},{1,0},{2,3},{3,2},{4,5},{5,4},{6,7},{7,6},{8,9},{9,8},{10,11... | collective-permute-start | bytes 245768 | tf_op jit(solution)/shard_map/ppermute | solution.py:617
  4.9 1.1 %collective-permute-start = (f32[5,8,256]{2,1,0:T(8,128)S(1)}, f32[5,8,256]{2,1,0:T(8,128)S(1)}, u32[]{:S(2)}, u32[]{:S(2)}) collective-permute-start(f32[5,8,256]{2,1,0:T(8,128)S(1)} %get-tuple-element.40), channel_id=1, source_target_pairs={{0,64},{64,0},{128,192},{192,128},{1,65},{65,1},{129,193},{193,129... | collective-permute-start | bytes 122888 | tf_op jit(solution)/shard_map/ppermute | solution.py:617
  6.0 1.8 %collective-permute-start.1 = (f32[5,8,256]{2,1,0:T(8,128)S(1)}, f32[5,8,256]{2,1,0:T(8,128)S(1)}, u32[]{:S(2)}, u32[]{:S(2)}) collective-permute-start(f32[5,8,256]{2,1,0:T(8,128)S(1)} %get-tuple-element.41), channel_id=1, source_target_pairs={{0,192},{64,128},{128,64},{192,0},{1,193},{65,129},{129,65},{193,1... | collective-permute-start | bytes 122888 | tf_op jit(solution)/shard_map/ppermute | solution.py:617
  7.8 2.2 %prep.1 = (f32[5,6,16,128]{3,2,1,0:T(8,128)S(1)}, f32[2,640,128]{2,1,0:T(8,128)S(1)}, f32[64,256]{1,0:T(8,128)S(1)}, f32[5,2,8,256]{3,2,1,0:T(8,128)S(1)}, f32[5...) custom-call(f32[5,4,8,256]{3,2,1,0:T(8,128)} %x_hbm.1, ...), custom_call_target="tpu_custom_call" | custom-call | flops 10000000 | bytes 10000000 | tf_op jit(solution)/shard_map/prep/pallas_call | solution.py:31
  10.4 8.3 %collective-permute-start.5 = (f32[176,128]{1,0:T(8,128)S(1)}, f32[176,128]{1,0:T(8,128)S(1)}, u32[]{:S(2)}, u32[]{:S(2)}) collective-permute-start(f32[176,128]{1,0:T(8,128)S(1)} %get-tuple-element.54), channel_id=1, source_target_pairs={{0,1},{1,0},{2,3},{3,2},{4,5},{5,4},{6,7},{7,6},{8,9},{9,8},{10,11... | collective-permute-start | bytes 270344 | tf_op jit(solution)/shard_map/ppermute | solution.py:617
  18.7 0.9 %collective-permute-done.5.got_ref.gotc_ref = f32[176,128]{1,0:T(8,128)S(1)} collective-permute-done((f32[176,128]{1,0:T(8,128)S(1)}, f32[176,128]{1,0:T(8,128)S(1)}, u32[]{:S(2)}, u32[]{:S(2)}) %collective-permute-start.5) | collective-permute-done | bytes 90144 | tf_op jit(solution)/shard_map/ppermute | solution.py:617
  19.8 1.9 %collective-permute-start.8 = (f32[144,128]{1,0:T(8,128)S(1)}, f32[144,128]{1,0:T(8,128)S(1)}, u32[]{:S(2)}, u32[]{:S(2)}) collective-permute-start(f32[144,128]{1,0:T(8,128)S(1)} %get-tuple-element.57.own_ref), channel_id=1, source_target_pairs={{0,192},{64,128},{128,64},{192,0},{1,193},{65,129},{129,65},{193,1... | collective-permute-start | bytes 221192 | tf_op jit(solution)/shard_map/ppermute | solution.py:617
  21.7 1.4 %collective-permute-start.6 = (f32[144,128]{1,0:T(8,128)S(1)}, f32[144,128]{1,0:T(8,128)S(1)}, u32[]{:S(2)}, u32[]{:S(2)}) collective-permute-start(f32[144,128]{1,0:T(8,128)S(1)} %get-tuple-element.57.own_ref), channel_id=1, source_target_pairs={{0,64},{64,0},{128,192},{192,128},{1,65},{65,1},{129,193},{193,129... | collective-permute-start | bytes 221192 | tf_op jit(solution)/shard_map/ppermute | solution.py:617
  23.2 1.2 %collective-permute-done.8.got3_ref = f32[144,128]{1,0:T(8,128)S(1)} collective-permute-done((f32[144,128]{1,0:T(8,128)S(1)}, f32[144,128]{1,0:T(8,128)S(1)}, u32[]{:S(2)}, u32[]{:S(2)}) %collective-permute-start.8) | collective-permute-done | bytes 73760 | tf_op jit(solution)/shard_map/ppermute | solution.py:617
  24.3 2.1 %collective-permute-done.7.got2_ref = f32[144,128]{1,0:T(8,128)S(1)} collective-permute-done((f32[144,128]{1,0:T(8,128)S(1)}, f32[144,128]{1,0:T(8,128)S(1)}, u32[]{:S(2)}, u32[]{:S(2)}) %collective-permute-start.7) | collective-permute-done | bytes 73760 | tf_op jit(solution)/shard_map/ppermute | solution.py:617
  26.9 3.4 %collective-permute-start.11 = (f32[176,128]{1,0:T(8,128)S(1)}, f32[176,128]{1,0:T(8,128)S(1)}, u32[]{:S(2)}, u32[]{:S(2)}) collective-permute-start(f32[176,128]{1,0:T(8,128)S(1)} %get-tuple-element.62.refs_0_.q0_ref), channel_id=1, source_target_pairs={{0,2},{1,3},{2,0},{3,1},{4,6},{5,7},{6,4},{7,5},{8,10},{9,11},{10,... | collective-permute-start | bytes 270344 | tf_op jit(solution)/shard_map/ppermute | solution.py:617
  31.2 0.9 %collective-permute-done.13.refs_3_.q3_ref = f32[176,128]{1,0:T(8,128)S(1)} collective-permute-done((f32[176,128]{1,0:T(8,128)S(1)}, f32[176,128]{1,0:T(8,128)S(1)}, u32[]{:S(2)}, u32[]{:S(2)}) %collective-permute-start.13) | collective-permute-done | bytes 90144 | tf_op jit(solution)/shard_map/ppermute | solution.py:617
  32.1 0.9 %collective-permute-done.12.refs_2_.q2_ref = f32[176,128]{1,0:T(8,128)S(1)} collective-permute-done((f32[176,128]{1,0:T(8,128)S(1)}, f32[176,128]{1,0:T(8,128)S(1)}, u32[]{:S(2)}, u32[]{:S(2)}) %collective-permute-start.12) | collective-permute-done | bytes 90144 | tf_op jit(solution)/shard_map/ppermute | solution.py:617
  33.6 3.3 %collective-permute-start.9 = (f32[80,128]{1,0:T(8,128)S(1)}, f32[80,128]{1,0:T(8,128)S(1)}, u32[]{:S(2)}, u32[]{:S(2)}) collective-permute-start(f32[80,128]{1,0:T(8,128)S(1)} %get-tuple-element.58.half_ref), channel_id=1, source_target_pairs={{0,1},{1,0},{2,3},{3,2},{4,5},{5,4},{6,7},{7,6},{8,9},{9,8},{10,11... | collective-permute-start | bytes 122888 | tf_op jit(solution)/shard_map/ppermute | solution.py:617
  36.9 0.9 %collective-permute-done.9.other_ref = f32[80,128]{1,0:T(8,128)S(1)} collective-permute-done((f32[80,128]{1,0:T(8,128)S(1)}, f32[80,128]{1,0:T(8,128)S(1)}, u32[]{:S(2)}, u32[]{:S(2)}) %collective-permute-start.9) | collective-permute-done | bytes 40992 | tf_op jit(solution)/shard_map/ppermute | solution.py:617
  37.9 0.9 %collective-permute-done.14.got_ref.got4_ref = f32[176,128]{1,0:T(8,128)S(1)} collective-permute-done((f32[176,128]{1,0:T(8,128)S(1)}, f32[176,128]{1,0:T(8,128)S(1)}, u32[]{:S(2)}, u32[]{:S(2)}) %collective-permute-start.14) | collective-permute-done | bytes 90144 | tf_op jit(solution)/shard_map/ppermute | solution.py:626
  38.9 2.4 %collective-permute-start.10 = (f32[5,16,256]{2,1,0:T(8,128)S(1)}, f32[5,16,256]{2,1,0:T(8,128)S(1)}, u32[]{:S(2)}, u32[]{:S(2)}) collective-permute-start(f32[5,16,256]{2,1,0:T(8,128)S(1)} %get-tuple-element.60.mine2_ref.after_ref), channel_id=1, source_target_pairs={{0,192},{64,128},{128,64},{192,0},{1,193},{65,129},{129,65},{193,1... | collective-permute-start | bytes 245768 | tf_op jit(solution)/shard_map/ppermute | solution.py:617
  41.3 1.3 %collective-permute-done.15.got_ref.got8_ref = f32[176,128]{1,0:T(8,128)S(1)} collective-permute-done((f32[176,128]{1,0:T(8,128)S(1)}, f32[176,128]{1,0:T(8,128)S(1)}, u32[]{:S(2)}, u32[]{:S(2)}) %collective-permute-start.15) | collective-permute-done | bytes 90144 | tf_op jit(solution)/shard_map/ppermute | solution.py:617
  42.6 1.2 %collective-permute-start.16 = (f32[88,128]{1,0:T(8,128)S(1)}, f32[88,128]{1,0:T(8,128)S(1)}, u32[]{:S(2)}, u32[]{:S(2)}) collective-permute-start(f32[88,128]{1,0:T(8,128)S(1)} %top.1.mine_ref), channel_id=1, source_target_pairs={{0,48},{1,49},{2,50},{3,51},{4,52},{5,53},{6,54},{7,55},{8,56},{9,... | collective-permute-start | bytes 135176 | tf_op jit(solution)/shard_map/ppermute | solution.py:617
  44.1 2.7 %collective-permute-done.16.got_ref = f32[88,128]{1,0:T(8,128)S(1)} collective-permute-done((f32[88,128]{1,0:T(8,128)S(1)}, f32[88,128]{1,0:T(8,128)S(1)}, u32[]{:S(2)}, u32[]{:S(2)}) %collective-permute-start.16) | collective-permute-done | bytes 45088 | tf_op jit(solution)/shard_map/ppermute | solution.py:617
  47.0 6.9 %collective-permute-start.17 = (f32[160,128]{1,0:T(8,128)S(1)}, f32[160,128]{1,0:T(8,128)S(1)}, u32[]{:S(2)}, u32[]{:S(2)}) collective-permute-start(f32[160,128]{1,0:T(8,128)S(1)} %get-tuple-element.66), channel_id=1, source_target_pairs={{0,1},{1,0},{2,3},{3,2},{4,5},{5,4},{6,7},{7,6},{8,9},{9,8},{10,11... | collective-permute-start | bytes 245768 | tf_op jit(solution)/shard_map/ppermute | solution.py:617
  53.8 0.9 %collective-permute-done.17.other_ref = f32[160,128]{1,0:T(8,128)S(1)} collective-permute-done((f32[160,128]{1,0:T(8,128)S(1)}, f32[160,128]{1,0:T(8,128)S(1)}, u32[]{:S(2)}, u32[]{:S(2)}) %collective-permute-start.17) | collective-permute-done | bytes 81952 | tf_op jit(solution)/shard_map/ppermute | solution.py:617
  54.8 0.9 %final.1 = f32[640,256]{1,0:T(8,128)} custom-call(f32[640,256]{1,0:T(8,128)S(1)} %solved.1.after_ref.g_ref, f32[5,2,8,256]{3,2,1,0:T(8,128)S(1)} %get-tuple-element.61.resp_ref, f32[160,128]{1,0:T(8,128)S(1)} %get-tuple-element.65.mine_ref, f32[160,128]{1,0:T(8,128)S(1)} %collective-permute-done.17.other_ref), custom_call_target="tpu_custom_call" | custom-call | flops 1000 | bytes 1000 | tf_op jit(solution)/shard_map/final/pallas_call | solution.py:31
  (29 shorter events, 3.1 us)
Async XLA Ops:
  0.0 7.8 %copy-start = (f32[5,6,16,256]{3,2,1,0:T(8,128)S(1)}, f32[5,6,16,256]{3,2,1,0:T(8,128)}, u32[]{:S(2)}) copy-start(f32[5,6,16,256]{3,2,1,0:T(8,128)} %c_ref.3) | copy-start | bytes 1474564
  0.0 7.8 %copy-start.1 = (f32[5,16,8,256]{3,2,1,0:T(8,128)S(1)}, f32[5,16,8,256]{3,2,1,0:T(8,128)}, u32[]{:S(2)}) copy-start(f32[5,16,8,256]{3,2,1,0:T(8,128)} %param.7) | copy-start | bytes 1966084
  1.6 8.5 %collective-permute-start.2 = (f32[5,16,256]{2,1,0:T(8,128)S(1)}, f32[5,16,256]{2,1,0:T(8,128)S(1)}, u32[]{:S(2)}, u32[]{:S(2)}) collective-permute-start(f32[5,16,256]{2,1,0:T(8,128)S(1)} %get-tuple-element.42), channel_id=1, source_target_pairs={{0,1},{1,0},{2,3},{3,2},{4,5},{5,4},{6,7},{7,6},{8,9},{9,8},{10,11... | collective-permute-start | bytes 245768 | tf_op jit(solution)/shard_map/ppermute | solution.py:617
  4.9 5.2 %collective-permute-start.3 = (f32[5,16,256]{2,1,0:T(8,128)S(1)}, f32[5,16,256]{2,1,0:T(8,128)S(1)}, u32[]{:S(2)}, u32[]{:S(2)}) collective-permute-start(f32[5,16,256]{2,1,0:T(8,128)S(1)} %get-tuple-element.43), channel_id=1, source_target_pairs={{0,63},{1,2},{2,1},{3,4},{4,3},{5,6},{6,5},{7,8},{8,7},{9,10},{10,... | collective-permute-start | bytes 245768 | tf_op jit(solution)/shard_map/ppermute | solution.py:645
  4.9 5.1 %collective-permute-start = (f32[5,8,256]{2,1,0:T(8,128)S(1)}, f32[5,8,256]{2,1,0:T(8,128)S(1)}, u32[]{:S(2)}, u32[]{:S(2)}) collective-permute-start(f32[5,8,256]{2,1,0:T(8,128)S(1)} %get-tuple-element.40), channel_id=1, source_target_pairs={{0,64},{64,0},{128,192},{192,128},{1,65},{65,1},{129,193},{193,129... | collective-permute-start | bytes 122888 | tf_op jit(solution)/shard_map/ppermute | solution.py:617
  6.0 4.1 %collective-permute-start.1 = (f32[5,8,256]{2,1,0:T(8,128)S(1)}, f32[5,8,256]{2,1,0:T(8,128)S(1)}, u32[]{:S(2)}, u32[]{:S(2)}) collective-permute-start(f32[5,8,256]{2,1,0:T(8,128)S(1)} %get-tuple-element.41), channel_id=1, source_target_pairs={{0,192},{64,128},{128,64},{192,0},{1,193},{65,129},{129,65},{193,1... | collective-permute-start | bytes 122888 | tf_op jit(solution)/shard_map/ppermute | solution.py:617
  10.4 9.2 %collective-permute-start.5 = (f32[176,128]{1,0:T(8,128)S(1)}, f32[176,128]{1,0:T(8,128)S(1)}, u32[]{:S(2)}, u32[]{:S(2)}) collective-permute-start(f32[176,128]{1,0:T(8,128)S(1)} %get-tuple-element.54), channel_id=1, source_target_pairs={{0,1},{1,0},{2,3},{3,2},{4,5},{5,4},{6,7},{7,6},{8,9},{9,8},{10,11... | collective-permute-start | bytes 270344 | tf_op jit(solution)/shard_map/ppermute | solution.py:617
  19.8 4.5 %collective-permute-start.8 = (f32[144,128]{1,0:T(8,128)S(1)}, f32[144,128]{1,0:T(8,128)S(1)}, u32[]{:S(2)}, u32[]{:S(2)}) collective-permute-start(f32[144,128]{1,0:T(8,128)S(1)} %get-tuple-element.57.own_ref), channel_id=1, source_target_pairs={{0,192},{64,128},{128,64},{192,0},{1,193},{65,129},{129,65},{193,1... | collective-permute-start | bytes 221192 | tf_op jit(solution)/shard_map/ppermute | solution.py:617
  21.7 4.7 %collective-permute-start.7 = (f32[144,128]{1,0:T(8,128)S(1)}, f32[144,128]{1,0:T(8,128)S(1)}, u32[]{:S(2)}, u32[]{:S(2)}) collective-permute-start(f32[144,128]{1,0:T(8,128)S(1)} %get-tuple-element.57.own_ref), channel_id=1, source_target_pairs={{0,128},{64,192},{128,0},{192,64},{1,129},{65,193},{129,1},{193,65... | collective-permute-start | bytes 221192 | tf_op jit(solution)/shard_map/ppermute | solution.py:617
  21.7 4.7 %collective-permute-start.6 = (f32[144,128]{1,0:T(8,128)S(1)}, f32[144,128]{1,0:T(8,128)S(1)}, u32[]{:S(2)}, u32[]{:S(2)}) collective-permute-start(f32[144,128]{1,0:T(8,128)S(1)} %get-tuple-element.57.own_ref), channel_id=1, source_target_pairs={{0,64},{64,0},{128,192},{192,128},{1,65},{65,1},{129,193},{193,129... | collective-permute-start | bytes 221192 | tf_op jit(solution)/shard_map/ppermute | solution.py:617
  26.7 5.4 %collective-permute-start.13 = (f32[176,128]{1,0:T(8,128)S(1)}, f32[176,128]{1,0:T(8,128)S(1)}, u32[]{:S(2)}, u32[]{:S(2)}) collective-permute-start(f32[176,128]{1,0:T(8,128)S(1)} %get-tuple-element.62.refs_0_.q0_ref), channel_id=1, source_target_pairs={{0,6},{1,7},{2,4},{3,5},{4,2},{5,3},{6,0},{7,1},{8,14},{9,15},{10,... | collective-permute-start | bytes 270344 | tf_op jit(solution)/shard_map/ppermute | solution.py:617
  26.8 6.3 %collective-permute-start.12 = (f32[176,128]{1,0:T(8,128)S(1)}, f32[176,128]{1,0:T(8,128)S(1)}, u32[]{:S(2)}, u32[]{:S(2)}) collective-permute-start(f32[176,128]{1,0:T(8,128)S(1)} %get-tuple-element.62.refs_0_.q0_ref), channel_id=1, source_target_pairs={{0,4},{1,5},{2,6},{3,7},{4,0},{5,1},{6,2},{7,3},{8,12},{9,13},{10,... | collective-permute-start | bytes 270344 | tf_op jit(solution)/shard_map/ppermute | solution.py:617
  26.9 6.2 %collective-permute-start.11 = (f32[176,128]{1,0:T(8,128)S(1)}, f32[176,128]{1,0:T(8,128)S(1)}, u32[]{:S(2)}, u32[]{:S(2)}) collective-permute-start(f32[176,128]{1,0:T(8,128)S(1)} %get-tuple-element.62.refs_0_.q0_ref), channel_id=1, source_target_pairs={{0,2},{1,3},{2,0},{3,1},{4,6},{5,7},{6,4},{7,5},{8,10},{9,11},{10,... | collective-permute-start | bytes 270344 | tf_op jit(solution)/shard_map/ppermute | solution.py:617
  30.7 6.2 %collective-permute-start.4 = (f32[5,32,256]{2,1,0:T(8,128)S(1)}, f32[5,32,256]{2,1,0:T(8,128)S(1)}, u32[]{:S(2)}, u32[]{:S(2)}) collective-permute-start(f32[5,32,256]{2,1,0:T(8,128)S(1)} %get-tuple-element.51.own_ref.refs_4_), channel_id=1, source_target_pairs={{0,64},{64,0},{128,192},{192,128},{1,65},{65,1},{129,193},{193,129... | collective-permute-start | bytes 491528 | tf_op jit(solution)/shard_map/ppermute | solution.py:617
  33.2 5.6 %collective-permute-start.14 = (f32[176,128]{1,0:T(8,128)S(1)}, f32[176,128]{1,0:T(8,128)S(1)}, u32[]{:S(2)}, u32[]{:S(2)}) collective-permute-start(f32[176,128]{1,0:T(8,128)S(1)} %quad.1.own_ref.own4_ref), channel_id=1, source_target_pairs={{0,12},{1,13},{2,14},{3,15},{4,8},{5,9},{6,10},{7,11},{8,4},{9,5},... | collective-permute-start | bytes 270344 | tf_op jit(solution)/shard_map/ppermute | solution.py:626
  33.6 4.2 %collective-permute-start.9 = (f32[80,128]{1,0:T(8,128)S(1)}, f32[80,128]{1,0:T(8,128)S(1)}, u32[]{:S(2)}, u32[]{:S(2)}) collective-permute-start(f32[80,128]{1,0:T(8,128)S(1)} %get-tuple-element.58.half_ref), channel_id=1, source_target_pairs={{0,1},{1,0},{2,3},{3,2},{4,5},{5,4},{6,7},{7,6},{8,9},{9,8},{10,11... | collective-permute-start | bytes 122888 | tf_op jit(solution)/shard_map/ppermute | solution.py:617
  38.8 3.8 %collective-permute-start.15 = (f32[176,128]{1,0:T(8,128)S(1)}, f32[176,128]{1,0:T(8,128)S(1)}, u32[]{:S(2)}, u32[]{:S(2)}) collective-permute-start(f32[176,128]{1,0:T(8,128)S(1)} %ring.1.own_ref.own8_ref), channel_id=1, source_target_pairs={{0,16},{1,17},{2,18},{3,19},{4,20},{5,21},{6,22},{7,23},{8,24},{9,... | collective-permute-start | bytes 270344 | tf_op jit(solution)/shard_map/ppermute | solution.py:617
  38.9 4.9 %collective-permute-start.10 = (f32[5,16,256]{2,1,0:T(8,128)S(1)}, f32[5,16,256]{2,1,0:T(8,128)S(1)}, u32[]{:S(2)}, u32[]{:S(2)}) collective-permute-start(f32[5,16,256]{2,1,0:T(8,128)S(1)} %get-tuple-element.60.mine2_ref.after_ref), channel_id=1, source_target_pairs={{0,192},{64,128},{128,64},{192,0},{1,193},{65,129},{129,65},{193,1... | collective-permute-start | bytes 245768 | tf_op jit(solution)/shard_map/ppermute | solution.py:617
  42.6 4.2 %collective-permute-start.16 = (f32[88,128]{1,0:T(8,128)S(1)}, f32[88,128]{1,0:T(8,128)S(1)}, u32[]{:S(2)}, u32[]{:S(2)}) collective-permute-start(f32[88,128]{1,0:T(8,128)S(1)} %top.1.mine_ref), channel_id=1, source_target_pairs={{0,48},{1,49},{2,50},{3,51},{4,52},{5,53},{6,54},{7,55},{8,56},{9,... | collective-permute-start | bytes 135176 | tf_op jit(solution)/shard_map/ppermute | solution.py:617
  47.0 7.8 %collective-permute-start.17 = (f32[160,128]{1,0:T(8,128)S(1)}, f32[160,128]{1,0:T(8,128)S(1)}, u32[]{:S(2)}, u32[]{:S(2)}) collective-permute-start(f32[160,128]{1,0:T(8,128)S(1)} %get-tuple-element.66), channel_id=1, source_target_pairs={{0,1},{1,0},{2,3},{3,2},{4,5},{5,4},{6,7},{7,6},{8,9},{9,8},{10,11... | collective-permute-start | bytes 245768 | tf_op jit(solution)/shard_map/ppermute | solution.py:617

commit v2 on v1

--- a/solution.py
+++ b/solution.py
@@ -305,7 +305,9 @@
     return [ends[v] + (one[v], two[v]) for v in range(NV)]
 
 
-def planes_kernel(c_ref, g_ref, halo_ref, low_ref, high_ref, gi_ref, out_ref, msg_ref, g_scr):
+def planes_kernel(
+    c_ref, g_ref, halo_ref, low_ref, high_ref, gi_ref, maps_ref, out_ref, msg_ref, g_scr
+):
     for v in range(NV):
         a, b = halo_ref[v, 0], halo_ref[v, 1]
         for i in range(NI):
@@ -319,7 +321,8 @@
     ends = local_sweeps(c_ref, g_scr, out_ref, out_ref)
     for v in range(NV):
         for n, x in enumerate(ends[v]):
-            msg_ref[v, n * NJ : n * NJ + NJ, :] = x
+            msg_ref[v * 32 + n * NJ : v * 32 + n * NJ + NJ, :] = x
+    msg_ref[BIG:, :] = maps_ref[...]
 
 
 def maps_of(ref, v, at=MAPS):
@@ -393,7 +396,7 @@
 
 def edges_kernel(
     layers_ref, resp_ref, keep_ref, gotc_ref, own_ref, got1_ref, got2_ref, got3_ref,
-    low_ref, high_ref, chip_ref, maps_ref,
+    low_ref, high_ref, chip_ref,
 ):
     p, core = lax.axis_index("line"), place()[0]
     refs = (own_ref, got1_ref, got2_ref, got3_ref)
@@ -420,45 +423,48 @@
                 x = x + answers[n] * states[n][t : t + 1]
             at = v * 32 + (t % 2) * NI
             (low_ref, high_ref)[t // 2][at : at + NI, :] = x
-        maps_ref[v * 12 : v * 12 + 12, :] = maps_of(got1_ref, v)
-        for n, x in enumerate(pair_gamma(maps[2], maps[3])):
-            maps_ref[60 + v * 4 + n : 61 + v * 4 + n, :] = x
     own, other = keep_ref[160:, :], gotc_ref[160:, :]
     low_ref[160:, :] = jnp.where(core == 0, own, other)
     high_ref[160:, :] = jnp.where(core == 0, other, own)
     store(chip_ref, compose(load(low_ref), load(high_ref)))
 
 
+BIG = NV * 32
+LAST = NV * 16
+
+
+def big_parts(ref, v):
+    at = v * 32
+    return [maps_of(ref, v, BIG)] + [ref[at + n * NJ : at + n * NJ + NJ, :] for n in range(4)]
+
+
+def last_parts(ref, v):
+    at = v * 16
+    return ref[at : at + NJ, :], ref[at + NJ : at + 2 * NJ, :]
+
+
 def last_gamma(ref, v):
-    return [ref[60 + v * 4 + n : 61 + v * 4 + n, :] for n in range(4)]
-
-
-def big_parts(ref, maps_ref, v):
-    return [maps_of(maps_ref, v, 0)] + [ref[v, n * NJ : n * NJ + NJ, :] for n in range(4)]
-
-
-def plane_pair_kernel(own_ref, got_ref, own_maps, half_ref, other_ref, out_ref, got_maps):
+    return [ref[LAST + v * 4 + n : LAST + v * 4 + n + 1, :] for n in range(4)]
+
+
+def plane_pair_kernel(own_ref, got_ref, out_ref):
     p = lax.axis_index("line")
-    even = place()[0] == 0
-    a, b = half_ref[...], other_ref[...]
-    got_maps[:, :HALF] = jnp.where(even, a, b)
-    got_maps[:, HALF:] = jnp.where(even, b, a)
-    for v in range(NV):
-        low, high = line_pair(p, big_parts(own_ref, own_maps, v), big_parts(got_ref, got_maps, v))
+    for v in range(NV):
+        low, high = line_pair(p, big_parts(own_ref, v), big_parts(got_ref, v))
         a, b = pair_states(p, low, high)
-        out_ref[v, :NJ, :] = a
-        out_ref[v, NJ:, :] = b
-
-
-def solved_kernel(
-    local_ref, resp_ref, own_ref, got_ref, own_maps, got_maps, mine2_ref, got2_ref, out_ref
-):
+        out_ref[v * 16 : v * 16 + NJ, :] = a
+        out_ref[v * 16 + NJ : v * 16 + 2 * NJ, :] = b
+        for n, x in enumerate(pair_gamma(low[0], high[0])):
+            out_ref[LAST + v * 4 + n : LAST + v * 4 + n + 1, :] = x
+    out_ref[LAST + 20 :, :] = jnp.zeros((4, NK), F32)
+
+
+def solved_kernel(local_ref, resp_ref, own_ref, got_ref, mine2_ref, got2_ref, out_ref):
     p = lax.axis_index("line")
     for v in range(NV):
-        low, high = line_pair(p, big_parts(own_ref, own_maps, v), big_parts(got_ref, got_maps, v))
-        mine = (mine2_ref[v, :NJ, :], mine2_ref[v, NJ:, :])
-        got = (got2_ref[v, :NJ, :], got2_ref[v, NJ:, :])
-        states = entering(p, low, high, mine, got, last_gamma(got_maps, v))
+        low, high = line_pair(p, big_parts(own_ref, v), big_parts(got_ref, v))
+        mine, got = last_parts(mine2_ref, v), last_parts(got2_ref, v)
+        states = entering(p, low, high, mine, got, last_gamma(got2_ref, v))
         for i in range(NI):
             at = v * PLANE + i * NJ
             for part in range(2):
@@ -533,20 +539,16 @@
     store(refs[-1], compose(compose(a, b), compose(c, d)))
 
 
-def ring_kernel(own_ref, got_ref, after_ref, out_ref):
-    store(out_ref, compose(*ordered(bit_clear(place()[1], 4), load(own_ref), load(got_ref))))
-
-
-def top_kernel(own_ref, got_ref, out_ref):
-    y = place()[2]
-    agg = compose(*ordered(bit_clear(y, 1), load(own_ref), load(got_ref)))
-    for v in range(NV):
-        out_ref[v * NI : v * NI + NI, :] = jnp.where(y >= 2, agg[1][v], agg[0][v])
-    out_ref[80:85, :] = agg[4]
-    out_ref[85:88, :] = jnp.zeros((3, HALF), F32)
-
-
-def step_down(is_low, low, high, f, u):
+def ring_kernel(own_ref, got_ref, after_ref, out_ref, fore_ref):
+    agg = compose(*ordered(bit_clear(place()[1], 4), load(own_ref), load(got_ref)))
+    store(out_ref, agg)
+    last = place()[2] == 3
+    for v in range(NV):
+        fore_ref[v * NI : v * NI + NI, :] = jnp.where(last, agg[1][v], agg[0][v])
+    fore_ref[80:, :] = out_ref[160:, :]
+
+
+def step_down(low, high, f, u):
     f_high = f_after(low, f)
     u_low = g_before(high, f_high, u)
     return (f, u_low), (f_high, u)
@@ -559,24 +561,31 @@
 
 
 def down_kernel(
-    mine_ref, got_ref, own8_ref, got8_ref, own4_ref, got4_ref,
+    own_ref, one_ref, two_ref, three_ref, own4_ref, got4_ref,
     q0_ref, q1_ref, q2_ref, q3_ref, low_ref, high_ref, after_ref, keep_ref, send_ref,
 ):
     core, z, y = place()
-    upper = y >= 2
-    zero = jnp.zeros((NI, HALF), F32)
-    at = [slice(v * NI, v * NI + NI) for v in range(NV)]
-    f = [jnp.where(upper, got_ref[x, :], zero) for x in at]
-    u = [
-        jnp.where(upper, zero, got_ref[x, :] + got_ref[80 + v : 81 + v, :] * mine_ref[x, :])
-        for v, x in enumerate(at)
-    ]
-    for is_low, mine, got in (
-        (bit_clear(y, 1), own8_ref, got8_ref),
-        (bit_clear(z, 4), own4_ref, got4_ref),
-    ):
-        low, high = ordered(is_low, load(mine), load(got))
-        f, u = choose(is_low, *step_down(is_low, low, high, f, u))
+    own, two, three = (load(r) for r in (own_ref, two_ref, three_ref))
+    x = [one_ref[v * NI : v * NI + NI, :] for v in range(NV)]
+    one = (x, x, one_ref[80:85, :], one_ref[85:90, :], one_ref[90:95, :])
+
+    def sort(*groups):
+        return jax.tree.map(lambda *x: pick(y, x), *groups)
+
+    ups = (own, one, two, three), (three, own, one, two), (two, three, own, one)
+    ups = [sort(*group) for group in ups]
+    downs = [three, choose(y == 0, two, three), sort(one, two, three)]
+    zero = [jnp.zeros((NI, HALF), F32)] * NV
+    fs = [zero, ups[0][0]]
+    fs.append(f_after(ups[1], fs[1]))
+    fs.append(f_after(ups[2], fs[2]))
+    us = [None, None, None, zero]
+    for n in (3, 2, 1):
+        us[n - 1] = g_before(downs[n - 1], fs[n], us[n])
+    f, u = sort(*fs), sort(*us)
+    is_low = bit_clear(z, 4)
+    low, high = ordered(is_low, load(own4_ref), load(got4_ref))
+    f, u = choose(is_low, *step_down(low, high, f, u))
     parts = members((q0_ref, q1_ref, q2_ref, q3_ref))
     fs, us = [f], [None, None, None, u]
     for r in range(3):
@@ -587,7 +596,7 @@
     f = [pick(m, [x[v] for x in fs]) for v in range(NV)]
     u = [pick(m, [x[v] for x in us]) for v in range(NV)]
     is_low = core == 0
-    low, high = step_down(is_low, load(low_ref), load(high_ref), f, u)
+    low, high = step_down(load(low_ref), load(high_ref), f, u)
     put_states(keep_ref, choose(is_low, low, high))
     put_states(send_ref, choose(is_low, high, low))
 
@@ -615,6 +624,10 @@
 
 def swap(x, axis, size, flip):
     return lax.ppermute(x, axis, [(i, i ^ flip) for i in range(size)])
+
+
+def shift(x, axis, size, by):
+    return lax.ppermute(x, axis, [(i, (i + by) % size) for i in range(size)])
 
 
 def across(x):
@@ -669,37 +682,34 @@
         scratch=[pltpu.VMEM(half_flat, F32)], name="layers",
     )
     smalls = [small] + [swap(small, "line", 4, d) for d in (1, 2, 3)]
-    low, high, chip, pair_maps = call(
-        edges_kernel, [msg, msg, msg, (80, HALF)],
+    low, high, chip = call(
+        edges_kernel, [msg, msg, msg],
         layers, line_resp, keep, got, *smalls, name="edges",
     )
     quad = [chip] + [swap(chip, "plane", 64, d) for d in (2, 4, 6)]
 
     local, big = call(
-        planes_kernel, [flat, (NV, 32, NK)], line_coeffs, g, halo_resp, j_low, j_high, gi,
+        planes_kernel, [flat, (BIG + 64, NK)],
+        line_coeffs, g, halo_resp, j_low, j_high, gi, maps,
         scratch=[pltpu.VMEM(flat, F32)], name="planes", flops=10**7,
     )
     got_big = swap(big, "line", 4, 1)
-    last_big, line_maps = call(
-        plane_pair_kernel, [(NV, 16, NK), (80, NK)],
-        big, got_big, maps, pair_maps, swap(pair_maps, "plane", 64, 1), name="plane_pair",
-    )
+    last_big = call(plane_pair_kernel, [(LAST + 24, NK)], big, got_big, name="plane_pair")[0]
     got_last_big = swap(last_big, "line", 4, 3)
     solved = call(
-        solved_kernel, [flat],
-        local, line_resp, big, got_big, maps, line_maps, last_big, got_last_big,
+        solved_kernel, [flat], local, line_resp, big, got_big, last_big, got_last_big,
         name="solved", flops=10**7,
     )[0]
 
     own4 = call(quad_kernel, [msg], *quad, big, name="quad")[0]
     got4 = across(own4)
-    own8 = call(ring_kernel, [msg], own4, got4, last_big, name="ring")[0]
-    got8 = swap(own8, "plane", 64, 16)
-    top = call(top_kernel, [(88, HALF)], own8, got8, name="top")[0]
-    got_top = swap(top, "plane", 64, 48)
+    ring, fore = call(ring_kernel, [msg, (96, HALF)], own4, got4, last_big, name="ring")
+    y1, y2, y3 = (
+        shift(fore, "plane", 64, 16), shift(ring, "plane", 64, 32), shift(ring, "plane", 64, 48)
+    )
     mine, send = call(
         down_kernel, [(160, HALF)] * 2,
-        top, got_top, own8, got8, own4, got4, *quad, low, high, solved, name="down",
+        ring, y1, y2, y3, own4, got4, *quad, low, high, solved, name="down",
     )
     other = swap(send, "plane", 64, 1)
     out = call(

time: 55.8 us -> 53.4 us (0.957)
  starting transfers between devices: 36.3 us -> 31.6 us
  waiting for transfers between devices: 12.8 us -> 15 us
    ppermute x16 -> x13, starting transfers between devices: 35.8 us -> 29.8 us  [swap(): return lax.ppermute(x, axis, [(i, i ^ flip) for i in range(size)])]
    ppermute x16 -> x13, waiting for transfers between devices: 11.9 us -> 7.43 us  [swap(): return lax.ppermute(x, axis, [(i, i ^ flip) for i in range(size)])]
    ppermute x0 -> x3, waiting for transfers between devices: none -> 4.15 us  [shift(): return lax.ppermute(x, axis, [(i, (i + by) % size) for i in range(size)])]
    ppermute x1, waiting for transfers between devices: 0.88 us -> 3.4 us  [across(): return lax.ppermute(x, 'plane', pairs)]
    ppermute x0 -> x3, starting transfers between devices: none -> 1.79 us  [shift(): return lax.ppermute(x, axis, [(i, (i + by) % size) for i in range(size)])]
    pallas_call x13 -> x12, Pallas kernels: 6.52 us -> 6.54 us  [call(): pl.pallas_call(kernel, out_shape=outs, in_specs=[pl.BlockSpec(memory_spac...]
  transfers between devices with their start and end apart: 18 -> 18, of which waited for: 10 -> 8; matrix products, arithmetic and copies ran while one was open for 0% -> 0% of each run, Pallas kernels for 6% -> 6%
where the time goes in v2:
time: 53.4 us; the launch traced here: 53.3 us
  starting transfers between devices  31.6 us (59%)
  waiting for transfers between devices  15 us (28%)
  Pallas kernels  6.54 us (12%)
    ppermute x13, starting transfers between devices, swap(): return lax.ppermute(x, axis, [(i, i ^ flip) for i in range(size)])  29.8 us
    ppermute x13, waiting for transfers between devices, swap(): return lax.ppermute(x, axis, [(i, i ^ flip) for i in range(size)])  7.43 us
    pallas_call x12, Pallas kernels, call(): pl.pallas_call(kernel, out_shape=outs, in_specs=[pl.BlockSpec(memory_spac...  6.54 us
    ppermute x3, waiting for transfers between devices, shift(): return lax.ppermute(x, axis, [(i, (i + by) % size) for i in range(size)])  4.15 us
    ppermute x1, waiting for transfers between devices, across(): return lax.ppermute(x, 'plane', pairs)  3.4 us
    ppermute x3, starting transfers between devices, shift(): return lax.ppermute(x, axis, [(i, (i + by) % size) for i in range(size)])  1.79 us
  transfers between devices with their start and end apart: 18, of which 8 were waited for; matrix products, arithmetic and copies ran while one was open for 0% of the time, Pallas kernels for 6%

profile of v2, /device:TPU:1, one launch (start us, length us, event | category | flops | bytes accessed | tf_op | source)
XLA Modules:
  0.0 53.3 jit_solution(17457968188141478507)
XLA Ops:
  0.0 1.6 %faces.1 = (f32[640,256]{1,0:T(8,128)S(1)}, f32[5,8,256]{2,1,0:T(8,128)S(1)}, f32[5,8,256]{2,1,0:T(8,128)S(1)}, f32[5,16,256]{2,1,0:T(8,128)S(1)}, f32[5,16,256]{2,1,0:T(8,128)S(1)}) custom-call(f32[640,256]{1,0:T(8,128)} %bitcast.5, f32[640,256]{1,0:T(8,128)} %bitcast.6), custom_call_target="tpu_custom_call" | custom-call | flops 1000 | bytes 1000 | tf_op jit(solution)/shard_map/faces/pallas_call | solution.py:31
  1.6 3.3 %collective-permute-start.2 = (f32[5,16,256]{2,1,0:T(8,128)S(1)}, f32[5,16,256]{2,1,0:T(8,128)S(1)}, u32[]{:S(2)}, u32[]{:S(2)}) collective-permute-start(f32[5,16,256]{2,1,0:T(8,128)S(1)} %get-tuple-element.41), channel_id=1, source_target_pairs={{0,1},{1,0},{2,3},{3,2},{4,5},{5,4},{6,7},{7,6},{8,9},{9,8},{10,11... | collective-permute-start | bytes 245768 | tf_op jit(solution)/shard_map/ppermute | solution.py:626
  4.9 1.1 %collective-permute-start = (f32[5,8,256]{2,1,0:T(8,128)S(1)}, f32[5,8,256]{2,1,0:T(8,128)S(1)}, u32[]{:S(2)}, u32[]{:S(2)}) collective-permute-start(f32[5,8,256]{2,1,0:T(8,128)S(1)} %get-tuple-element.39), channel_id=1, source_target_pairs={{0,64},{64,0},{128,192},{192,128},{1,65},{65,1},{129,193},{193,129... | collective-permute-start | bytes 122888 | tf_op jit(solution)/shard_map/ppermute | solution.py:626
  6.0 1.8 %collective-permute-start.1 = (f32[5,8,256]{2,1,0:T(8,128)S(1)}, f32[5,8,256]{2,1,0:T(8,128)S(1)}, u32[]{:S(2)}, u32[]{:S(2)}) collective-permute-start(f32[5,8,256]{2,1,0:T(8,128)S(1)} %get-tuple-element.40), channel_id=1, source_target_pairs={{0,192},{64,128},{128,64},{192,0},{1,193},{65,129},{129,65},{193,1... | collective-permute-start | bytes 122888 | tf_op jit(solution)/shard_map/ppermute | solution.py:626
  7.8 2.2 %prep.1 = (f32[5,6,16,128]{3,2,1,0:T(8,128)S(1)}, f32[2,640,128]{2,1,0:T(8,128)S(1)}, f32[64,256]{1,0:T(8,128)S(1)}, f32[5,2,8,256]{3,2,1,0:T(8,128)S(1)}, f32[5...) custom-call(f32[5,4,8,256]{3,2,1,0:T(8,128)} %x_hbm.1, ...), custom_call_target="tpu_custom_call" | custom-call | flops 10000000 | bytes 10000000 | tf_op jit(solution)/shard_map/prep/pallas_call | solution.py:31
  10.4 8.3 %collective-permute-start.6 = (f32[176,128]{1,0:T(8,128)S(1)}, f32[176,128]{1,0:T(8,128)S(1)}, u32[]{:S(2)}, u32[]{:S(2)}) collective-permute-start(f32[176,128]{1,0:T(8,128)S(1)} %get-tuple-element.54), channel_id=1, source_target_pairs={{0,1},{1,0},{2,3},{3,2},{4,5},{5,4},{6,7},{7,6},{8,9},{9,8},{10,11... | collective-permute-start | bytes 270344 | tf_op jit(solution)/shard_map/ppermute | solution.py:626
  18.7 0.9 %collective-permute-done.6.got_ref.gotc_ref = f32[176,128]{1,0:T(8,128)S(1)} collective-permute-done((f32[176,128]{1,0:T(8,128)S(1)}, f32[176,128]{1,0:T(8,128)S(1)}, u32[]{:S(2)}, u32[]{:S(2)}) %collective-permute-start.6) | collective-permute-done | bytes 90144 | tf_op jit(solution)/shard_map/ppermute | solution.py:626
  19.8 1.9 %collective-permute-start.9 = (f32[144,128]{1,0:T(8,128)S(1)}, f32[144,128]{1,0:T(8,128)S(1)}, u32[]{:S(2)}, u32[]{:S(2)}) collective-permute-start(f32[144,128]{1,0:T(8,128)S(1)} %get-tuple-element.57.own_ref), channel_id=1, source_target_pairs={{0,192},{64,128},{128,64},{192,0},{1,193},{65,129},{129,65},{193,1... | collective-permute-start | bytes 221192 | tf_op jit(solution)/shard_map/ppermute | solution.py:626
  21.7 1.4 %collective-permute-start.7 = (f32[144,128]{1,0:T(8,128)S(1)}, f32[144,128]{1,0:T(8,128)S(1)}, u32[]{:S(2)}, u32[]{:S(2)}) collective-permute-start(f32[144,128]{1,0:T(8,128)S(1)} %get-tuple-element.57.own_ref), channel_id=1, source_target_pairs={{0,64},{64,0},{128,192},{192,128},{1,65},{65,1},{129,193},{193,129... | collective-permute-start | bytes 221192 | tf_op jit(solution)/shard_map/ppermute | solution.py:626
  23.2 0.4 planes.1
  23.7 0.7 %collective-permute-done.9.got3_ref = f32[144,128]{1,0:T(8,128)S(1)} collective-permute-done((f32[144,128]{1,0:T(8,128)S(1)}, f32[144,128]{1,0:T(8,128)S(1)}, u32[]{:S(2)}, u32[]{:S(2)}) %collective-permute-start.9) | collective-permute-done | bytes 73760 | tf_op jit(solution)/shard_map/ppermute | solution.py:626
  24.3 2.1 %collective-permute-done.8.got2_ref = f32[144,128]{1,0:T(8,128)S(1)} collective-permute-done((f32[144,128]{1,0:T(8,128)S(1)}, f32[144,128]{1,0:T(8,128)S(1)}, u32[]{:S(2)}, u32[]{:S(2)}) %collective-permute-start.8) | collective-permute-done | bytes 73760 | tf_op jit(solution)/shard_map/ppermute | solution.py:626
  26.9 3.4 %collective-permute-start.10 = (f32[176,128]{1,0:T(8,128)S(1)}, f32[176,128]{1,0:T(8,128)S(1)}, u32[]{:S(2)}, u32[]{:S(2)}) collective-permute-start(f32[176,128]{1,0:T(8,128)S(1)} %get-tuple-element.58.refs_0_.q0_ref), channel_id=1, source_target_pairs={{0,2},{1,3},{2,0},{3,1},{4,6},{5,7},{6,4},{7,5},{8,10},{9,11},{10,... | collective-permute-start | bytes 270344 | tf_op jit(solution)/shard_map/ppermute | solution.py:626
  30.3 1.8 %collective-permute-done.12.refs_3_.q3_ref = f32[176,128]{1,0:T(8,128)S(1)} collective-permute-done((f32[176,128]{1,0:T(8,128)S(1)}, f32[176,128]{1,0:T(8,128)S(1)}, u32[]{:S(2)}, u32[]{:S(2)}) %collective-permute-start.12) | collective-permute-done | bytes 90144 | tf_op jit(solution)/shard_map/ppermute | solution.py:626
  32.1 0.9 %collective-permute-done.11.refs_2_.q2_ref = f32[176,128]{1,0:T(8,128)S(1)} collective-permute-done((f32[176,128]{1,0:T(8,128)S(1)}, f32[176,128]{1,0:T(8,128)S(1)}, u32[]{:S(2)}, u32[]{:S(2)}) %collective-permute-start.11) | collective-permute-done | bytes 90144 | tf_op jit(solution)/shard_map/ppermute | solution.py:626
  33.5 1.9 %collective-permute-start.5 = (f32[104,256]{1,0:T(8,128)S(1)}, f32[104,256]{1,0:T(8,128)S(1)}, u32[]{:S(2)}, u32[]{:S(2)}) collective-permute-start(f32[104,256]{1,0:T(8,128)S(1)} %plane_pair.1.mine2_ref.after_ref), channel_id=1, source_target_pairs={{0,192},{64,128},{128,64},{192,0},{1,193},{65,129},{129,65},{193,1... | collective-permute-start | bytes 319496 | tf_op jit(solution)/shard_map/ppermute | solution.py:626
  35.4 3.4 %collective-permute-done.13.got_ref.got4_ref = f32[176,128]{1,0:T(8,128)S(1)} collective-permute-done((f32[176,128]{1,0:T(8,128)S(1)}, f32[176,128]{1,0:T(8,128)S(1)}, u32[]{:S(2)}, u32[]{:S(2)}) %collective-permute-start.13) | collective-permute-done | bytes 90144 | tf_op jit(solution)/shard_map/ppermute | solution.py:639
  38.8 0.8 %collective-permute-start.16 = (f32[176,128]{1,0:T(8,128)S(1)}, f32[176,128]{1,0:T(8,128)S(1)}, u32[]{:S(2)}, u32[]{:S(2)}) collective-permute-start(f32[176,128]{1,0:T(8,128)S(1)} %get-tuple-element.59.own_ref), channel_id=1, source_target_pairs={{0,48},{1,49},{2,50},{3,51},{4,52},{5,53},{6,54},{7,55},{8,56},{9,... | collective-permute-start | bytes 270344 | tf_op jit(solution)/shard_map/ppermute | solution.py:630
  39.6 0.3 collective-permute-start.15
  39.9 0.7 %collective-permute-start.14 = (f32[96,128]{1,0:T(8,128)S(1)}, f32[96,128]{1,0:T(8,128)S(1)}, u32[]{:S(2)}, u32[]{:S(2)}) collective-permute-start(f32[96,128]{1,0:T(8,128)S(1)} %get-tuple-element.60), channel_id=1, source_target_pairs={{0,16},{1,17},{2,18},{3,19},{4,20},{5,21},{6,22},{7,23},{8,24},{9,... | collective-permute-start | bytes 147464 | tf_op jit(solution)/shard_map/ppermute | solution.py:630
  40.9 4.1 %collective-permute-done.14.one_ref = f32[96,128]{1,0:T(8,128)S(1)} collective-permute-done((f32[96,128]{1,0:T(8,128)S(1)}, f32[96,128]{1,0:T(8,128)S(1)}, u32[]{:S(2)}, u32[]{:S(2)}) %collective-permute-start.14) | collective-permute-done | bytes 49184 | tf_op jit(solution)/shard_map/ppermute | solution.py:630
  45.3 6.2 %collective-permute-start.17 = (f32[160,128]{1,0:T(8,128)S(1)}, f32[160,128]{1,0:T(8,128)S(1)}, u32[]{:S(2)}, u32[]{:S(2)}) collective-permute-start(f32[160,128]{1,0:T(8,128)S(1)} %get-tuple-element.64), channel_id=1, source_target_pairs={{0,1},{1,0},{2,3},{3,2},{4,5},{5,4},{6,7},{7,6},{8,9},{9,8},{10,11... | collective-permute-start | bytes 245768 | tf_op jit(solution)/shard_map/ppermute | solution.py:626
  51.5 0.9 %collective-permute-done.17.other_ref = f32[160,128]{1,0:T(8,128)S(1)} collective-permute-done((f32[160,128]{1,0:T(8,128)S(1)}, f32[160,128]{1,0:T(8,128)S(1)}, u32[]{:S(2)}, u32[]{:S(2)}) %collective-permute-start.17) | collective-permute-done | bytes 81952 | tf_op jit(solution)/shard_map/ppermute | solution.py:626
  52.4 0.9 %final.1 = f32[640,256]{1,0:T(8,128)} custom-call(f32[640,256]{1,0:T(8,128)S(1)} %solved.1.after_ref.g_ref, f32[5,2,8,256]{3,2,1,0:T(8,128)S(1)} %get-tuple-element.52.resp_ref, f32[160,128]{1,0:T(8,128)S(1)} %get-tuple-element.63.mine_ref, f32[160,128]{1,0:T(8,128)S(1)} %collective-permute-done.17.other_ref), custom_call_target="tpu_custom_call" | custom-call | flops 1000 | bytes 1000 | tf_op jit(solution)/shard_map/final/pallas_call | solution.py:31
  (28 shorter events, 1.9 us)
Async XLA Ops:
  0.0 7.8 %copy-start = (f32[5,6,16,256]{3,2,1,0:T(8,128)S(1)}, f32[5,6,16,256]{3,2,1,0:T(8,128)}, u32[]{:S(2)}) copy-start(f32[5,6,16,256]{3,2,1,0:T(8,128)} %c_ref.3) | copy-start | bytes 1474564
  0.0 7.8 %copy-start.1 = (f32[5,16,8,256]{3,2,1,0:T(8,128)S(1)}, f32[5,16,8,256]{3,2,1,0:T(8,128)}, u32[]{:S(2)}) copy-start(f32[5,16,8,256]{3,2,1,0:T(8,128)} %param.7) | copy-start | bytes 1966084
  1.6 8.5 %collective-permute-start.2 = (f32[5,16,256]{2,1,0:T(8,128)S(1)}, f32[5,16,256]{2,1,0:T(8,128)S(1)}, u32[]{:S(2)}, u32[]{:S(2)}) collective-permute-start(f32[5,16,256]{2,1,0:T(8,128)S(1)} %get-tuple-element.41), channel_id=1, source_target_pairs={{0,1},{1,0},{2,3},{3,2},{4,5},{5,4},{6,7},{7,6},{8,9},{9,8},{10,11... | collective-permute-start | bytes 245768 | tf_op jit(solution)/shard_map/ppermute | solution.py:626
  4.9 5.2 %collective-permute-start.3 = (f32[5,16,256]{2,1,0:T(8,128)S(1)}, f32[5,16,256]{2,1,0:T(8,128)S(1)}, u32[]{:S(2)}, u32[]{:S(2)}) collective-permute-start(f32[5,16,256]{2,1,0:T(8,128)S(1)} %get-tuple-element.42), channel_id=1, source_target_pairs={{0,63},{1,2},{2,1},{3,4},{4,3},{5,6},{6,5},{7,8},{8,7},{9,10},{10,... | collective-permute-start | bytes 245768 | tf_op jit(solution)/shard_map/ppermute | solution.py:658
  4.9 5.1 %collective-permute-start = (f32[5,8,256]{2,1,0:T(8,128)S(1)}, f32[5,8,256]{2,1,0:T(8,128)S(1)}, u32[]{:S(2)}, u32[]{:S(2)}) collective-permute-start(f32[5,8,256]{2,1,0:T(8,128)S(1)} %get-tuple-element.39), channel_id=1, source_target_pairs={{0,64},{64,0},{128,192},{192,128},{1,65},{65,1},{129,193},{193,129... | collective-permute-start | bytes 122888 | tf_op jit(solution)/shard_map/ppermute | solution.py:626
  6.0 4.1 %collective-permute-start.1 = (f32[5,8,256]{2,1,0:T(8,128)S(1)}, f32[5,8,256]{2,1,0:T(8,128)S(1)}, u32[]{:S(2)}, u32[]{:S(2)}) collective-permute-start(f32[5,8,256]{2,1,0:T(8,128)S(1)} %get-tuple-element.40), channel_id=1, source_target_pairs={{0,192},{64,128},{128,64},{192,0},{1,193},{65,129},{129,65},{193,1... | collective-permute-start | bytes 122888 | tf_op jit(solution)/shard_map/ppermute | solution.py:626
  10.4 9.2 %collective-permute-start.6 = (f32[176,128]{1,0:T(8,128)S(1)}, f32[176,128]{1,0:T(8,128)S(1)}, u32[]{:S(2)}, u32[]{:S(2)}) collective-permute-start(f32[176,128]{1,0:T(8,128)S(1)} %get-tuple-element.54), channel_id=1, source_target_pairs={{0,1},{1,0},{2,3},{3,2},{4,5},{5,4},{6,7},{7,6},{8,9},{9,8},{10,11... | collective-permute-start | bytes 270344 | tf_op jit(solution)/shard_map/ppermute | solution.py:626
  19.8 4.5 %collective-permute-start.9 = (f32[144,128]{1,0:T(8,128)S(1)}, f32[144,128]{1,0:T(8,128)S(1)}, u32[]{:S(2)}, u32[]{:S(2)}) collective-permute-start(f32[144,128]{1,0:T(8,128)S(1)} %get-tuple-element.57.own_ref), channel_id=1, source_target_pairs={{0,192},{64,128},{128,64},{192,0},{1,193},{65,129},{129,65},{193,1... | collective-permute-start | bytes 221192 | tf_op jit(solution)/shard_map/ppermute | solution.py:626
  21.7 4.7 %collective-permute-start.8 = (f32[144,128]{1,0:T(8,128)S(1)}, f32[144,128]{1,0:T(8,128)S(1)}, u32[]{:S(2)}, u32[]{:S(2)}) collective-permute-start(f32[144,128]{1,0:T(8,128)S(1)} %get-tuple-element.57.own_ref), channel_id=1, source_target_pairs={{0,128},{64,192},{128,0},{192,64},{1,129},{65,193},{129,1},{193,65... | collective-permute-start | bytes 221192 | tf_op jit(solution)/shard_map/ppermute | solution.py:626
  21.7 4.7 %collective-permute-start.7 = (f32[144,128]{1,0:T(8,128)S(1)}, f32[144,128]{1,0:T(8,128)S(1)}, u32[]{:S(2)}, u32[]{:S(2)}) collective-permute-start(f32[144,128]{1,0:T(8,128)S(1)} %get-tuple-element.57.own_ref), channel_id=1, source_target_pairs={{0,64},{64,0},{128,192},{192,128},{1,65},{65,1},{129,193},{193,129... | collective-permute-start | bytes 221192 | tf_op jit(solution)/shard_map/ppermute | solution.py:626
  23.5 9.7 %collective-permute-start.4 = (f32[224,256]{1,0:T(8,128)S(1)}, f32[224,256]{1,0:T(8,128)S(1)}, u32[]{:S(2)}, u32[]{:S(2)}) collective-permute-start(f32[224,256]{1,0:T(8,128)S(1)} %get-tuple-element.51.own_ref.refs_4_), channel_id=1, source_target_pairs={{0,64},{64,0},{128,192},{192,128},{1,65},{65,1},{129,193},{193,129... | collective-permute-start | bytes 688136 | tf_op jit(solution)/shard_map/ppermute | solution.py:626
  26.7 5.4 %collective-permute-start.12 = (f32[176,128]{1,0:T(8,128)S(1)}, f32[176,128]{1,0:T(8,128)S(1)}, u32[]{:S(2)}, u32[]{:S(2)}) collective-permute-start(f32[176,128]{1,0:T(8,128)S(1)} %get-tuple-element.58.refs_0_.q0_ref), channel_id=1, source_target_pairs={{0,6},{1,7},{2,4},{3,5},{4,2},{5,3},{6,0},{7,1},{8,14},{9,15},{10,... | collective-permute-start | bytes 270344 | tf_op jit(solution)/shard_map/ppermute | solution.py:626
  26.8 6.3 %collective-permute-start.11 = (f32[176,128]{1,0:T(8,128)S(1)}, f32[176,128]{1,0:T(8,128)S(1)}, u32[]{:S(2)}, u32[]{:S(2)}) collective-permute-start(f32[176,128]{1,0:T(8,128)S(1)} %get-tuple-element.58.refs_0_.q0_ref), channel_id=1, source_target_pairs={{0,4},{1,5},{2,6},{3,7},{4,0},{5,1},{6,2},{7,3},{8,12},{9,13},{10,... | collective-permute-start | bytes 270344 | tf_op jit(solution)/shard_map/ppermute | solution.py:626
  26.9 6.2 %collective-permute-start.10 = (f32[176,128]{1,0:T(8,128)S(1)}, f32[176,128]{1,0:T(8,128)S(1)}, u32[]{:S(2)}, u32[]{:S(2)}) collective-permute-start(f32[176,128]{1,0:T(8,128)S(1)} %get-tuple-element.58.refs_0_.q0_ref), channel_id=1, source_target_pairs={{0,2},{1,3},{2,0},{3,1},{4,6},{5,7},{6,4},{7,5},{8,10},{9,11},{10,... | collective-permute-start | bytes 270344 | tf_op jit(solution)/shard_map/ppermute | solution.py:626
  33.1 5.6 %collective-permute-start.13 = (f32[176,128]{1,0:T(8,128)S(1)}, f32[176,128]{1,0:T(8,128)S(1)}, u32[]{:S(2)}, u32[]{:S(2)}) collective-permute-start(f32[176,128]{1,0:T(8,128)S(1)} %quad.1.own_ref.own4_ref), channel_id=1, source_target_pairs={{0,12},{1,13},{2,14},{3,15},{4,8},{5,9},{6,10},{7,11},{8,4},{9,5},... | collective-permute-start | bytes 270344 | tf_op jit(solution)/shard_map/ppermute | solution.py:639
  33.5 7.2 %collective-permute-start.5 = (f32[104,256]{1,0:T(8,128)S(1)}, f32[104,256]{1,0:T(8,128)S(1)}, u32[]{:S(2)}, u32[]{:S(2)}) collective-permute-start(f32[104,256]{1,0:T(8,128)S(1)} %plane_pair.1.mine2_ref.after_ref), channel_id=1, source_target_pairs={{0,192},{64,128},{128,64},{192,0},{1,193},{65,129},{129,65},{193,1... | collective-permute-start | bytes 319496 | tf_op jit(solution)/shard_map/ppermute | solution.py:626
  38.8 6.2 %collective-permute-start.16 = (f32[176,128]{1,0:T(8,128)S(1)}, f32[176,128]{1,0:T(8,128)S(1)}, u32[]{:S(2)}, u32[]{:S(2)}) collective-permute-start(f32[176,128]{1,0:T(8,128)S(1)} %get-tuple-element.59.own_ref), channel_id=1, source_target_pairs={{0,48},{1,49},{2,50},{3,51},{4,52},{5,53},{6,54},{7,55},{8,56},{9,... | collective-permute-start | bytes 270344 | tf_op jit(solution)/shard_map/ppermute | solution.py:630
  39.6 5.4 %collective-permute-start.15 = (f32[176,128]{1,0:T(8,128)S(1)}, f32[176,128]{1,0:T(8,128)S(1)}, u32[]{:S(2)}, u32[]{:S(2)}) collective-permute-start(f32[176,128]{1,0:T(8,128)S(1)} %get-tuple-element.59.own_ref), channel_id=1, source_target_pairs={{0,32},{1,33},{2,34},{3,35},{4,36},{5,37},{6,38},{7,39},{8,40},{9,... | collective-permute-start | bytes 270344 | tf_op jit(solution)/shard_map/ppermute | solution.py:630
  39.9 5.1 %collective-permute-start.14 = (f32[96,128]{1,0:T(8,128)S(1)}, f32[96,128]{1,0:T(8,128)S(1)}, u32[]{:S(2)}, u32[]{:S(2)}) collective-permute-start(f32[96,128]{1,0:T(8,128)S(1)} %get-tuple-element.60), channel_id=1, source_target_pairs={{0,16},{1,17},{2,18},{3,19},{4,20},{5,21},{6,22},{7,23},{8,24},{9,... | collective-permute-start | bytes 147464 | tf_op jit(solution)/shard_map/ppermute | solution.py:630
  45.3 7.1 %collective-permute-start.17 = (f32[160,128]{1,0:T(8,128)S(1)}, f32[160,128]{1,0:T(8,128)S(1)}, u32[]{:S(2)}, u32[]{:S(2)}) collective-permute-start(f32[160,128]{1,0:T(8,128)S(1)} %get-tuple-element.64), channel_id=1, source_target_pairs={{0,1},{1,0},{2,3},{3,2},{4,5},{5,4},{6,7},{7,6},{8,9},{9,8},{10,11... | collective-permute-start | bytes 245768 | tf_op jit(solution)/shard_map/ppermute | solution.py:626

commit v3 on v2

--- a/solution.py
+++ b/solution.py
@@ -86,7 +86,7 @@
 
 def prep_kernel(
     x_hbm, m_hbm, w_ref, f_ref, c_ref,
-    half_ref, line_resp_ref, maps_ref, cross_resp_ref, halo_resp_ref, co_ref, g_ref, t_ref, x_ref,
+    half_ref, line_resp_ref, maps_ref, cross_resp_ref, halo_resp_ref, weight_ref, co_ref, s_ref, t_ref, x_ref,
     m_ref, sems,
 ):
     copies = [
@@ -103,8 +103,8 @@
     line_coeffs_of(c_ref, line_resp_ref, maps_ref)
     for copy in copies:
         copy.wait()
-    cross_coeffs_of(x_ref, cross_resp_ref, halo_resp_ref, co_ref)
-    local_source(w_ref, f_ref, m_ref, x_ref, g_ref, t_ref)
+    cross_coeffs_of(x_ref, cross_resp_ref, halo_resp_ref, weight_ref, co_ref)
+    local_source(w_ref, f_ref, m_ref, weight_ref, s_ref, t_ref)
 
 
 def line_coeffs_of(c_ref, resp_ref, msg_ref):
@@ -160,7 +160,7 @@
     return x
 
 
-def cross_coeffs_of(x_ref, resp_ref, halo_ref, co_ref):
+def cross_coeffs_of(x_ref, resp_ref, halo_ref, weight_ref, co_ref):
     row = rows_of(TILE)
     co_ref[15:, :] = jnp.zeros((1, NK), F32)
     for v in range(NV):
@@ -171,22 +171,27 @@
         b_resp = scan_down(jnp.where(row == NJ - 1, bc, 0.0), dn)
         resp_ref[v, 0] = g_resp
         resp_ref[v, 1] = b_resp
+        following = down_steps(pltpu.roll(fc, NJ - 1, 0))
+        before = up_steps(pltpu.roll(bc, 1, 0))
+        phi = fd * scan_down(jnp.where(row == NJ - 1, 1.0, 0.0), following)
+        beta = fd * scan_down(bd * scan_up(jnp.where(row == 0, 1.0, 0.0), before), following)
+        weight_ref[v, 0] = phi
+        weight_ref[v, 1] = beta
         for n, at, half in ((0, 0, 0.5), (1, NJ - 1, -0.5)):
-            f = scan_up(jnp.where(row == at, half * fd, 0.0), up)
-            g = scan_down(bd * f, dn)
-            halo_ref[v, n] = g
-            halo_ref[v, n + 2] = edge_rows(f, g)
+            halo_ref[v, n] = half * jnp.where(row < 4, phi[at : at + 1], beta[at : at + 1])
         co_ref[v : v + 1, :] = f_resp[NJ - 1 : NJ]
         co_ref[NV + v : NV + v + 1, :] = b_resp[0:1]
         co_ref[2 * NV + v : 2 * NV + v + 1, :] = g_resp[0:1]
 
 
-def edge_rows(f, g):
-    row = rows_of(TILE)
-    return jnp.where(row == 0, pltpu.roll(f, 1, 0), pltpu.roll(g, 1, 0))
-
-
-def local_source(w_ref, f_ref, m_ref, x_ref, g_ref, t_ref):
+def edge_rows(weight_ref, v, s):
+    a, b = weight_ref[v, 0] * s, weight_ref[v, 1] * s
+    x = jnp.where(rows_of(TILE) < 4, a + pltpu.roll(a, 4, 0), b + pltpu.roll(b, 4, 0))
+    x = x + pltpu.roll(x, NJ - 1, 0)
+    return x + pltpu.roll(x, NJ - 2, 0)
+
+
+def local_source(w_ref, f_ref, m_ref, weight_ref, s_ref, t_ref):
     p = lax.axis_index("line")
     row, lane = rows_of(TILE), lanes_of(TILE)
     zero = jnp.zeros(TILE, F32)
@@ -197,8 +202,6 @@
         base = pl.multiple_of(v * PLANE, PLANE)
         at = [pl.ds(base + i * NJ, NJ) for i in range(NI)]
         w = [w_ref[at[i], :] for i in range(NI)]
-        fd, bd = x_ref[v, 1], x_ref[v, 3]
-        up, dn = up_steps(x_ref[v, 0]), down_steps(x_ref[v, 2])
         for i in range(NI):
             x = w[i]
             before = low_mask * x if i == 0 else w[i - 1]
@@ -210,18 +213,16 @@
             s = f_ref[at[i], :] + 0.5 * (
                 (before - after) + (j_before - j_after) + (k_before - k_after)
             )
-            f = scan_up(fd * s, up)
-            g = scan_down(bd * f, dn)
-            g_ref[at[i], :] = g
-            t_ref[at[i], :] = edge_rows(f, g)
+            s_ref[at[i], :] = s
+            t_ref[at[i], :] = edge_rows(weight_ref, v, s)
         return 0
 
     lax.fori_loop(0, NV, step, 0)
 
 
 def source_kernel(
-    t_in, ia_ref, ib_ref, ja_ref, jb_ref, x_ref, halo_ref, co_ref,
-    low_ref, high_ref, gi_ref, keep_ref, send_ref, t_scr,
+    t_in, ia_ref, ib_ref, ja_ref, jb_ref, halo_ref, weight_ref, co_ref,
+    low_ref, high_ref, face_ref, keep_ref, send_ref, t_scr,
 ):
     p, q = lax.axis_index("line"), lax.axis_index("plane")
     even_line, even_plane = lax.rem(p, 2) == 0, lax.rem(q, 2) == 0
@@ -234,15 +235,11 @@
         j_high = jnp.where(q == 63, 0.0, jnp.where(even_plane, ja, jb))
         low_ref[v] = j_low
         high_ref[v] = j_high
-        fd, bd = x_ref[v, 1], x_ref[v, 3]
-        up, dn = up_steps(x_ref[v, 0]), down_steps(x_ref[v, 2])
         ends = []
         for n, face in enumerate((0.5 * low, -0.5 * high)):
-            f = scan_up(fd * face, up)
-            g = scan_down(bd * f, dn)
-            gi_ref[v, n] = g
-            ends.append(edge_rows(f, g))
-        a, b = halo_ref[v, 2], halo_ref[v, 3]
+            face_ref[v, n] = face
+            ends.append(edge_rows(weight_ref, v, face))
+        a, b = halo_ref[v, 0], halo_ref[v, 1]
         for i in range(NI):
             at = slice(v * PLANE + i * NJ, v * PLANE + i * NJ + NJ)
             t = t_in[at, :] + a * j_low[i : i + 1] + b * j_high[i : i + 1]
@@ -253,7 +250,7 @@
             for half in range(2):
                 t_scr[half, at, :] = t[:, half * HALF : half * HALF + HALF]
         for n in range(2):
-            a, b = (t_scr[half, pl.ds(v * PLANE + n, NI, stride=NJ), :] for half in range(2))
+            a, b = (t_scr[half, pl.ds(v * PLANE + 4 * n, NI, stride=NJ), :] for half in range(2))
             at = slice(v * 32 + n * NI, v * 32 + n * NI + NI)
             keep_ref[at, :] = jnp.where(even_plane, a, b)
             send_ref[at, :] = jnp.where(even_plane, b, a)
@@ -306,18 +303,21 @@
 
 
 def planes_kernel(
-    c_ref, g_ref, halo_ref, low_ref, high_ref, gi_ref, maps_ref, out_ref, msg_ref, g_scr
+    c_ref, x_ref, s_ref, low_ref, high_ref, face_ref, maps_ref, out_ref, msg_ref, g_scr
 ):
-    for v in range(NV):
-        a, b = halo_ref[v, 0], halo_ref[v, 1]
+    row = rows_of(TILE)
+    for v in range(NV):
+        fd, bd = x_ref[v, 1], x_ref[v, 3]
+        up, dn = up_steps(x_ref[v, 0]), down_steps(x_ref[v, 2])
         for i in range(NI):
             at = slice(v * PLANE + i * NJ, v * PLANE + i * NJ + NJ)
-            g = g_ref[at, :] + a * low_ref[v, i : i + 1, :] + b * high_ref[v, i : i + 1, :]
-            if i == 0:
-                g = g + gi_ref[v, 0]
-            if i == NI - 1:
-                g = g + gi_ref[v, 1]
-            g_scr[at, :] = g
+            low, high = low_ref[v, i : i + 1, :], high_ref[v, i : i + 1, :]
+            s = s_ref[at, :] + jnp.where(
+                row == 0, 0.5 * low, jnp.where(row == NJ - 1, -0.5 * high, 0.0)
+            )
+            if i in (0, NI - 1):
+                s = s + face_ref[v, 0 if i == 0 else 1]
+            g_scr[at, :] = scan_down(bd * scan_up(fd * s, up), dn)
     ends = local_sweeps(c_ref, g_scr, out_ref, out_ref)
     for v in range(NV):
         for n, x in enumerate(ends[v]):
@@ -561,7 +561,7 @@
 
 
 def down_kernel(
-    own_ref, one_ref, two_ref, three_ref, own4_ref, got4_ref,
+    own_ref, one_ref, three_ref, two_ref, own4_ref, got4_ref,
     q0_ref, q1_ref, q2_ref, q3_ref, low_ref, high_ref, after_ref, keep_ref, send_ref,
 ):
     core, z, y = place()
@@ -626,6 +626,12 @@
     return lax.ppermute(x, axis, [(i, i ^ flip) for i in range(size)])
 
 
+def everyone(x, partner):
+    places = [(p, q) for p in range(4) for q in range(64)]
+    pairs = [(p * 64 + q, partner(p, q)) for p, q in places]
+    return lax.ppermute(x, ("line", "plane"), [(n, p * 64 + q) for n, (p, q) in pairs])
+
+
 def shift(x, axis, size, by):
     return lax.ppermute(x, axis, [(i, (i + by) % size) for i in range(size)])
 
@@ -653,16 +659,16 @@
         ],
     )
     ia = swap(ia, "line", 4, 1)
-    ib = swap(ib, "line", 4, 3)
+    ib = everyone(ib, lambda p, q: (3 - p, q) if p in (1, 2) else (p, q ^ 1))
     ja = swap(ja, "plane", 64, 1)
-    jb = lax.ppermute(jb, "plane", [(i, (i + 1 if i % 2 else i - 1) % 64) for i in range(64)])
+    jb = everyone(jb, lambda p, q: (p ^ 1, q) if q in (0, 63) else (p, q + 1 if q % 2 else q - 1))
 
     halves = (2, NV * PLANE, HALF)
-    half, line_resp, maps, cross_resp, halo_resp, co, g, t, x = call(
+    half, line_resp, maps, cross_resp, halo_resp, weights, co, s, t, x = call(
         prep_kernel,
         [
-            line_coeffs.shape[:3] + (HALF,), halves, (64, NK), (NV, 2, NJ, NK), (NV, 4, NJ, NK),
-            (16, NK), flat, flat, cross_coeffs.shape,
+            line_coeffs.shape[:3] + (HALF,), halves, (64, NK), (NV, 2, NJ, NK), (NV, 2, NJ, NK),
+            (NV, 2, NJ, NK), (16, NK), flat, flat, cross_coeffs.shape,
         ],
         cross_coeffs, face_masks, w, f, line_coeffs, in_hbm=2, name="prep", flops=10**7,
         scratch=[
@@ -671,9 +677,9 @@
         ],
     )
     msg = (176, HALF)
-    j_low, j_high, gi, keep, send = call(
+    j_low, j_high, faces, keep, send = call(
         source_kernel, [j_face, j_face, (NV, 2, NJ, NK), msg, msg],
-        t, ia, ib, ja, jb, x, halo_resp, co, scratch=[pltpu.VMEM(halves, F32)], name="source",
+        t, ia, ib, ja, jb, halo_resp, weights, co, scratch=[pltpu.VMEM(halves, F32)], name="source",
     )
     got = swap(send, "plane", 64, 1)
     half_flat = (NV * PLANE, HALF)
@@ -690,7 +696,7 @@
 
     local, big = call(
         planes_kernel, [flat, (BIG + 64, NK)],
-        line_coeffs, g, halo_resp, j_low, j_high, gi, maps,
+        line_coeffs, x, s, j_low, j_high, faces, maps,
         scratch=[pltpu.VMEM(flat, F32)], name="planes", flops=10**7,
     )
     got_big = swap(big, "line", 4, 1)
@@ -709,7 +715,7 @@
     )
     mine, send = call(
         down_kernel, [(160, HALF)] * 2,
-        ring, y1, y2, y3, own4, got4, *quad, low, high, solved, name="down",
+        ring, y1, y3, y2, own4, got4, *quad, low, high, solved, name="down",
     )
     other = swap(send, "plane", 64, 1)
     out = call(

time: 53.4 us -> 51.8 us (0.970)
  starting transfers between devices: 31.6 us -> 29.6 us
    ppermute x13 -> x12, starting transfers between devices: 29.8 us -> 23.2 us  [swap(): return lax.ppermute(x, axis, [(i, i ^ flip) for i in range(size)])]
    ppermute x13 -> x12, waiting for transfers between devices: 7.43 us -> 10.5 us  [swap(): return lax.ppermute(x, axis, [(i, i ^ flip) for i in range(size)])]
    ppermute x3, starting transfers between devices: 1.79 us -> 3.71 us  [shift(): return lax.ppermute(x, axis, [(i, (i + by) % size) for i in range(size)])]
    ppermute x1, waiting for transfers between devices: 3.4 us -> 1.56 us  [across(): return lax.ppermute(x, 'plane', pairs)]
    ppermute x1, starting transfers between devices: 0.09 us -> 1.67 us  [across(): return lax.ppermute(x, 'plane', pairs)]
    ppermute x1 -> x2, starting transfers between devices: 0.01 us -> 1.03 us  [everyone(): lax.ppermute(x, ('line', 'plane'), [(n, p * 64 + q) for n, (p, q) in pairs])]
    ppermute x3, waiting for transfers between devices: 4.15 us -> 3.2 us  [shift(): return lax.ppermute(x, axis, [(i, (i + by) % size) for i in range(size)])]
  transfers between devices with their start and end apart: 18 -> 18, of which waited for: 8 -> 9; matrix products, arithmetic and copies ran while one was open for 0% -> 0% of each run, Pallas kernels for 6% -> 7%
where the time goes in v3:
time: 51.8 us; the launch traced here: 51.7 us
  starting transfers between devices  29.6 us (57%)
  waiting for transfers between devices  15.4 us (30%)
  Pallas kernels  6.58 us (13%)
    ppermute x12, starting transfers between devices, swap(): return lax.ppermute(x, axis, [(i, i ^ flip) for i in range(size)])  23.2 us
    ppermute x12, waiting for transfers between devices, swap(): return lax.ppermute(x, axis, [(i, i ^ flip) for i in range(size)])  10.5 us
    pallas_call x12, Pallas kernels, call(): pl.pallas_call(kernel, out_shape=outs, in_specs=[pl.BlockSpec(memory_spac...  6.58 us
    ppermute x3, starting transfers between devices, shift(): return lax.ppermute(x, axis, [(i, (i + by) % size) for i in range(size)])  3.71 us
    ppermute x3, waiting for transfers between devices, shift(): return lax.ppermute(x, axis, [(i, (i + by) % size) for i in range(size)])  3.2 us
    ppermute x1, starting transfers between devices, across(): return lax.ppermute(x, 'plane', pairs)  1.67 us
    ppermute x1, waiting for transfers between devices, across(): return lax.ppermute(x, 'plane', pairs)  1.56 us
  transfers between devices with their start and end apart: 18, of which 9 were waited for; matrix products, arithmetic and copies ran while one was open for 0% of the time, Pallas kernels for 7%

profile of v3, /device:TPU:1, one launch (start us, length us, event | category | flops | bytes accessed | tf_op | source)
XLA Modules:
  0.0 51.7 jit_solution(3263858932069235017)
XLA Ops:
  0.0 1.6 %faces.1 = (f32[640,256]{1,0:T(8,128)S(1)}, f32[5,8,256]{2,1,0:T(8,128)S(1)}, f32[5,8,256]{2,1,0:T(8,128)S(1)}, f32[5,16,256]{2,1,0:T(8,128)S(1)}, f32[5,16,256]{2,1,0:T(8,128)S(1)}) custom-call(f32[640,256]{1,0:T(8,128)} %bitcast.5, f32[640,256]{1,0:T(8,128)} %bitcast.6), custom_call_target="tpu_custom_call" | custom-call | flops 1000 | bytes 1000 | tf_op jit(solution)/shard_map/faces/pallas_call | solution.py:31
  1.6 3.3 %collective-permute-start.2 = (f32[5,16,256]{2,1,0:T(8,128)S(1)}, f32[5,16,256]{2,1,0:T(8,128)S(1)}, u32[]{:S(2)}, u32[]{:S(2)}) collective-permute-start(f32[5,16,256]{2,1,0:T(8,128)S(1)} %get-tuple-element.42), channel_id=1, source_target_pairs={{0,1},{1,0},{2,3},{3,2},{4,5},{5,4},{6,7},{7,6},{8,9},{9,8},{10,11... | collective-permute-start | bytes 245768 | tf_op jit(solution)/shard_map/ppermute | solution.py:626
  4.9 1.1 %collective-permute-start = (f32[5,8,256]{2,1,0:T(8,128)S(1)}, f32[5,8,256]{2,1,0:T(8,128)S(1)}, u32[]{:S(2)}, u32[]{:S(2)}) collective-permute-start(f32[5,8,256]{2,1,0:T(8,128)S(1)} %get-tuple-element.40), channel_id=1, source_target_pairs={{0,64},{64,0},{128,192},{192,128},{1,65},{65,1},{129,193},{193,129... | collective-permute-start | bytes 122888 | tf_op jit(solution)/shard_map/ppermute | solution.py:626
  6.0 1.0 %collective-permute-start.1 = (f32[5,8,256]{2,1,0:T(8,128)S(1)}, f32[5,8,256]{2,1,0:T(8,128)S(1)}, u32[]{:S(2)}, u32[]{:S(2)}) collective-permute-start(f32[5,8,256]{2,1,0:T(8,128)S(1)} %get-tuple-element.41), channel_id=1, source_target_pairs={{0,1},{1,0},{2,3},{3,2},{4,5},{5,4},{6,7},{7,6},{8,9},{9,8},{10,11... | collective-permute-start | bytes 122888 | tf_op jit(solution)/shard_map/ppermute | solution.py:632
  7.0 1.9 %prep.1 = (f32[5,6,16,128]{3,2,1,0:T(8,128)S(1)}, f32[2,640,128]{2,1,0:T(8,128)S(1)}, f32[64,256]{1,0:T(8,128)S(1)}, f32[5,2,8,256]{3,2,1,0:T(8,128)S(1)}, f32[5...) custom-call(f32[5,4,8,256]{3,2,1,0:T(8,128)} %x_hbm.1, ...), custom_call_target="tpu_custom_call" | custom-call | flops 10000000 | bytes 10000000 | tf_op jit(solution)/shard_map/prep/pallas_call | solution.py:31
  9.3 0.9 %collective-permute-start.6 = (f32[176,128]{1,0:T(8,128)S(1)}, f32[176,128]{1,0:T(8,128)S(1)}, u32[]{:S(2)}, u32[]{:S(2)}) collective-permute-start(f32[176,128]{1,0:T(8,128)S(1)} %get-tuple-element.56), channel_id=1, source_target_pairs={{0,1},{1,0},{2,3},{3,2},{4,5},{5,4},{6,7},{7,6},{8,9},{9,8},{10,11... | collective-permute-start | bytes 270344 | tf_op jit(solution)/shard_map/ppermute | solution.py:626
  10.2 0.9 %collective-permute-done.6.got_ref.gotc_ref = f32[176,128]{1,0:T(8,128)S(1)} collective-permute-done((f32[176,128]{1,0:T(8,128)S(1)}, f32[176,128]{1,0:T(8,128)S(1)}, u32[]{:S(2)}, u32[]{:S(2)}) %collective-permute-start.6) | collective-permute-done | bytes 90144 | tf_op jit(solution)/shard_map/ppermute | solution.py:626
  11.4 1.1 %collective-permute-start.9 = (f32[144,128]{1,0:T(8,128)S(1)}, f32[144,128]{1,0:T(8,128)S(1)}, u32[]{:S(2)}, u32[]{:S(2)}) collective-permute-start(f32[144,128]{1,0:T(8,128)S(1)} %get-tuple-element.59.own_ref), channel_id=1, source_target_pairs={{0,192},{64,128},{128,64},{192,0},{1,193},{65,129},{129,65},{193,1... | collective-permute-start | bytes 221192 | tf_op jit(solution)/shard_map/ppermute | solution.py:626
  12.5 1.8 %collective-permute-start.8 = (f32[144,128]{1,0:T(8,128)S(1)}, f32[144,128]{1,0:T(8,128)S(1)}, u32[]{:S(2)}, u32[]{:S(2)}) collective-permute-start(f32[144,128]{1,0:T(8,128)S(1)} %get-tuple-element.59.own_ref), channel_id=1, source_target_pairs={{0,128},{64,192},{128,0},{192,64},{1,129},{65,193},{129,1},{193,65... | collective-permute-start | bytes 221192 | tf_op jit(solution)/shard_map/ppermute | solution.py:626
  14.7 0.8 %planes.1 = (f32[640,256]{1,0:T(8,128)S(1)}, f32[224,256]{1,0:T(8,128)S(1)}) custom-call(f32[5,6,16,256]{3,2,1,0:T(8,128)S(1)} %copy-done, f32[5,4,8,256]{3,2,1,0:T(8,128)S(1)} %get-tuple-element.37.x_ref, f32[640,256]{1,0:T(8,128)S(1)} %get-tuple-element.38.s_ref, f32[5,16,256]{2,1,0:T(8,128)S(1)} %get-tuple-element.47.low_ref, ...), custom_call_target="tpu_custom_call" | custom-call | flops 10000000 | bytes 10000000 | tf_op jit(solution)/shard_map/planes/pallas_call | solution.py:31
  15.6 1.0 %collective-permute-start.4 = (f32[224,256]{1,0:T(8,128)S(1)}, f32[224,256]{1,0:T(8,128)S(1)}, u32[]{:S(2)}, u32[]{:S(2)}) collective-permute-start(f32[224,256]{1,0:T(8,128)S(1)} %get-tuple-element.53.own_ref.refs_4_), channel_id=1, source_target_pairs={{0,64},{64,0},{128,192},{192,128},{1,65},{65,1},{129,193},{193,129... | collective-permute-start | bytes 688136 | tf_op jit(solution)/shard_map/ppermute | solution.py:626
  17.3 1.1 %collective-permute-done.7.got1_ref = f32[144,128]{1,0:T(8,128)S(1)} collective-permute-done((f32[144,128]{1,0:T(8,128)S(1)}, f32[144,128]{1,0:T(8,128)S(1)}, u32[]{:S(2)}, u32[]{:S(2)}) %collective-permute-start.7) | collective-permute-done | bytes 73760 | tf_op jit(solution)/shard_map/ppermute | solution.py:626
  18.6 4.5 %collective-permute-start.12 = (f32[176,128]{1,0:T(8,128)S(1)}, f32[176,128]{1,0:T(8,128)S(1)}, u32[]{:S(2)}, u32[]{:S(2)}) collective-permute-start(f32[176,128]{1,0:T(8,128)S(1)} %get-tuple-element.60.refs_0_.q0_ref), channel_id=1, source_target_pairs={{0,6},{1,7},{2,4},{3,5},{4,2},{5,3},{6,0},{7,1},{8,14},{9,15},{10,... | collective-permute-start | bytes 270344 | tf_op jit(solution)/shard_map/ppermute | solution.py:626
  23.5 1.6 %collective-permute-done.12.refs_3_.q3_ref = f32[176,128]{1,0:T(8,128)S(1)} collective-permute-done((f32[176,128]{1,0:T(8,128)S(1)}, f32[176,128]{1,0:T(8,128)S(1)}, u32[]{:S(2)}, u32[]{:S(2)}) %collective-permute-start.12) | collective-permute-done | bytes 90144 | tf_op jit(solution)/shard_map/ppermute | solution.py:626
  25.1 5.4 %collective-permute-done.11.refs_2_.q2_ref = f32[176,128]{1,0:T(8,128)S(1)} collective-permute-done((f32[176,128]{1,0:T(8,128)S(1)}, f32[176,128]{1,0:T(8,128)S(1)}, u32[]{:S(2)}, u32[]{:S(2)}) %collective-permute-start.11) | collective-permute-done | bytes 90144 | tf_op jit(solution)/shard_map/ppermute | solution.py:626
  30.5 1.7 %collective-permute-start.13 = (f32[176,128]{1,0:T(8,128)S(1)}, f32[176,128]{1,0:T(8,128)S(1)}, u32[]{:S(2)}, u32[]{:S(2)}) collective-permute-start(f32[176,128]{1,0:T(8,128)S(1)} %quad.1.own_ref.own4_ref), channel_id=1, source_target_pairs={{0,12},{1,13},{2,14},{3,15},{4,8},{5,9},{6,10},{7,11},{8,4},{9,5},... | collective-permute-start | bytes 270344 | tf_op jit(solution)/shard_map/ppermute | solution.py:645
  32.4 2.2 %collective-permute-start.5 = (f32[104,256]{1,0:T(8,128)S(1)}, f32[104,256]{1,0:T(8,128)S(1)}, u32[]{:S(2)}, u32[]{:S(2)}) collective-permute-start(f32[104,256]{1,0:T(8,128)S(1)} %plane_pair.1.mine2_ref.after_ref), channel_id=1, source_target_pairs={{0,192},{64,128},{128,64},{192,0},{1,193},{65,129},{129,65},{193,1... | collective-permute-start | bytes 319496 | tf_op jit(solution)/shard_map/ppermute | solution.py:626
  34.5 1.6 %collective-permute-done.13.got_ref.got4_ref = f32[176,128]{1,0:T(8,128)S(1)} collective-permute-done((f32[176,128]{1,0:T(8,128)S(1)}, f32[176,128]{1,0:T(8,128)S(1)}, u32[]{:S(2)}, u32[]{:S(2)}) %collective-permute-start.13) | collective-permute-done | bytes 90144 | tf_op jit(solution)/shard_map/ppermute | solution.py:645
  36.1 2.2 %collective-permute-start.16 = (f32[176,128]{1,0:T(8,128)S(1)}, f32[176,128]{1,0:T(8,128)S(1)}, u32[]{:S(2)}, u32[]{:S(2)}) collective-permute-start(f32[176,128]{1,0:T(8,128)S(1)} %get-tuple-element.61.own_ref), channel_id=1, source_target_pairs={{0,32},{1,33},{2,34},{3,35},{4,36},{5,37},{6,38},{7,39},{8,40},{9,... | collective-permute-start | bytes 270344 | tf_op jit(solution)/shard_map/ppermute | solution.py:636
  38.4 0.8 %collective-permute-start.15 = (f32[176,128]{1,0:T(8,128)S(1)}, f32[176,128]{1,0:T(8,128)S(1)}, u32[]{:S(2)}, u32[]{:S(2)}) collective-permute-start(f32[176,128]{1,0:T(8,128)S(1)} %get-tuple-element.61.own_ref), channel_id=1, source_target_pairs={{0,48},{1,49},{2,50},{3,51},{4,52},{5,53},{6,54},{7,55},{8,56},{9,... | collective-permute-start | bytes 270344 | tf_op jit(solution)/shard_map/ppermute | solution.py:636
  40.1 3.2 %collective-permute-done.14.one_ref = f32[96,128]{1,0:T(8,128)S(1)} collective-permute-done((f32[96,128]{1,0:T(8,128)S(1)}, f32[96,128]{1,0:T(8,128)S(1)}, u32[]{:S(2)}, u32[]{:S(2)}) %collective-permute-start.14) | collective-permute-done | bytes 49184 | tf_op jit(solution)/shard_map/ppermute | solution.py:636
  43.5 6.4 %collective-permute-start.17 = (f32[160,128]{1,0:T(8,128)S(1)}, f32[160,128]{1,0:T(8,128)S(1)}, u32[]{:S(2)}, u32[]{:S(2)}) collective-permute-start(f32[160,128]{1,0:T(8,128)S(1)} %get-tuple-element.66), channel_id=1, source_target_pairs={{0,1},{1,0},{2,3},{3,2},{4,5},{5,4},{6,7},{7,6},{8,9},{9,8},{10,11... | collective-permute-start | bytes 245768 | tf_op jit(solution)/shard_map/ppermute | solution.py:626
  49.9 0.9 %collective-permute-done.17.other_ref = f32[160,128]{1,0:T(8,128)S(1)} collective-permute-done((f32[160,128]{1,0:T(8,128)S(1)}, f32[160,128]{1,0:T(8,128)S(1)}, u32[]{:S(2)}, u32[]{:S(2)}) %collective-permute-start.17) | collective-permute-done | bytes 81952 | tf_op jit(solution)/shard_map/ppermute | solution.py:626
  50.8 0.9 %final.1 = f32[640,256]{1,0:T(8,128)} custom-call(f32[640,256]{1,0:T(8,128)S(1)} %solved.1.after_ref.g_ref, f32[5,2,8,256]{3,2,1,0:T(8,128)S(1)} %get-tuple-element.54.resp_ref, f32[160,128]{1,0:T(8,128)S(1)} %get-tuple-element.65.mine_ref, f32[160,128]{1,0:T(8,128)S(1)} %collective-permute-done.17.other_ref), custom_call_target="tpu_custom_call" | custom-call | flops 1000 | bytes 1000 | tf_op jit(solution)/shard_map/final/pallas_call | solution.py:31
  (28 shorter events, 3.8 us)
Async XLA Ops:
  0.0 7.0 %copy-start = (f32[5,6,16,256]{3,2,1,0:T(8,128)S(1)}, f32[5,6,16,256]{3,2,1,0:T(8,128)}, u32[]{:S(2)}) copy-start(f32[5,6,16,256]{3,2,1,0:T(8,128)} %c_ref.3) | copy-start | bytes 1474564
  0.0 7.0 %copy-start.1 = (f32[5,16,8,256]{3,2,1,0:T(8,128)S(1)}, f32[5,16,8,256]{3,2,1,0:T(8,128)}, u32[]{:S(2)}) copy-start(f32[5,16,8,256]{3,2,1,0:T(8,128)} %param.7) | copy-start | bytes 1966084
  1.6 7.4 %collective-permute-start.2 = (f32[5,16,256]{2,1,0:T(8,128)S(1)}, f32[5,16,256]{2,1,0:T(8,128)S(1)}, u32[]{:S(2)}, u32[]{:S(2)}) collective-permute-start(f32[5,16,256]{2,1,0:T(8,128)S(1)} %get-tuple-element.42), channel_id=1, source_target_pairs={{0,1},{1,0},{2,3},{3,2},{4,5},{5,4},{6,7},{7,6},{8,9},{9,8},{10,11... | collective-permute-start | bytes 245768 | tf_op jit(solution)/shard_map/ppermute | solution.py:626
  4.9 4.2 %collective-permute-start.3 = (f32[5,16,256]{2,1,0:T(8,128)S(1)}, f32[5,16,256]{2,1,0:T(8,128)S(1)}, u32[]{:S(2)}, u32[]{:S(2)}) collective-permute-start(f32[5,16,256]{2,1,0:T(8,128)S(1)} %get-tuple-element.43), channel_id=1, source_target_pairs={{0,64},{1,2},{2,1},{3,4},{4,3},{5,6},{6,5},{7,8},{8,7},{9,10},{10,... | collective-permute-start | bytes 245768 | tf_op jit(solution)/shard_map/ppermute | solution.py:632
  4.9 4.0 %collective-permute-start = (f32[5,8,256]{2,1,0:T(8,128)S(1)}, f32[5,8,256]{2,1,0:T(8,128)S(1)}, u32[]{:S(2)}, u32[]{:S(2)}) collective-permute-start(f32[5,8,256]{2,1,0:T(8,128)S(1)} %get-tuple-element.40), channel_id=1, source_target_pairs={{0,64},{64,0},{128,192},{192,128},{1,65},{65,1},{129,193},{193,129... | collective-permute-start | bytes 122888 | tf_op jit(solution)/shard_map/ppermute | solution.py:626
  6.0 2.9 %collective-permute-start.1 = (f32[5,8,256]{2,1,0:T(8,128)S(1)}, f32[5,8,256]{2,1,0:T(8,128)S(1)}, u32[]{:S(2)}, u32[]{:S(2)}) collective-permute-start(f32[5,8,256]{2,1,0:T(8,128)S(1)} %get-tuple-element.41), channel_id=1, source_target_pairs={{0,1},{1,0},{2,3},{3,2},{4,5},{5,4},{6,7},{7,6},{8,9},{9,8},{10,11... | collective-permute-start | bytes 122888 | tf_op jit(solution)/shard_map/ppermute | solution.py:632
  9.3 1.9 %collective-permute-start.6 = (f32[176,128]{1,0:T(8,128)S(1)}, f32[176,128]{1,0:T(8,128)S(1)}, u32[]{:S(2)}, u32[]{:S(2)}) collective-permute-start(f32[176,128]{1,0:T(8,128)S(1)} %get-tuple-element.56), channel_id=1, source_target_pairs={{0,1},{1,0},{2,3},{3,2},{4,5},{5,4},{6,7},{7,6},{8,9},{9,8},{10,11... | collective-permute-start | bytes 270344 | tf_op jit(solution)/shard_map/ppermute | solution.py:626
  11.4 5.2 %collective-permute-start.9 = (f32[144,128]{1,0:T(8,128)S(1)}, f32[144,128]{1,0:T(8,128)S(1)}, u32[]{:S(2)}, u32[]{:S(2)}) collective-permute-start(f32[144,128]{1,0:T(8,128)S(1)} %get-tuple-element.59.own_ref), channel_id=1, source_target_pairs={{0,192},{64,128},{128,64},{192,0},{1,193},{65,129},{129,65},{193,1... | collective-permute-start | bytes 221192 | tf_op jit(solution)/shard_map/ppermute | solution.py:626
  12.5 4.8 %collective-permute-start.8 = (f32[144,128]{1,0:T(8,128)S(1)}, f32[144,128]{1,0:T(8,128)S(1)}, u32[]{:S(2)}, u32[]{:S(2)}) collective-permute-start(f32[144,128]{1,0:T(8,128)S(1)} %get-tuple-element.59.own_ref), channel_id=1, source_target_pairs={{0,128},{64,192},{128,0},{192,64},{1,129},{65,193},{129,1},{193,65... | collective-permute-start | bytes 221192 | tf_op jit(solution)/shard_map/ppermute | solution.py:626
  14.2 4.1 %collective-permute-start.7 = (f32[144,128]{1,0:T(8,128)S(1)}, f32[144,128]{1,0:T(8,128)S(1)}, u32[]{:S(2)}, u32[]{:S(2)}) collective-permute-start(f32[144,128]{1,0:T(8,128)S(1)} %get-tuple-element.59.own_ref), channel_id=1, source_target_pairs={{0,64},{64,0},{128,192},{192,128},{1,65},{65,1},{129,193},{193,129... | collective-permute-start | bytes 221192 | tf_op jit(solution)/shard_map/ppermute | solution.py:626
  15.6 16.6 %collective-permute-start.4 = (f32[224,256]{1,0:T(8,128)S(1)}, f32[224,256]{1,0:T(8,128)S(1)}, u32[]{:S(2)}, u32[]{:S(2)}) collective-permute-start(f32[224,256]{1,0:T(8,128)S(1)} %get-tuple-element.53.own_ref.refs_4_), channel_id=1, source_target_pairs={{0,64},{64,0},{128,192},{192,128},{1,65},{65,1},{129,193},{193,129... | collective-permute-start | bytes 688136 | tf_op jit(solution)/shard_map/ppermute | solution.py:626
  18.6 6.5 %collective-permute-start.12 = (f32[176,128]{1,0:T(8,128)S(1)}, f32[176,128]{1,0:T(8,128)S(1)}, u32[]{:S(2)}, u32[]{:S(2)}) collective-permute-start(f32[176,128]{1,0:T(8,128)S(1)} %get-tuple-element.60.refs_0_.q0_ref), channel_id=1, source_target_pairs={{0,6},{1,7},{2,4},{3,5},{4,2},{5,3},{6,0},{7,1},{8,14},{9,15},{10,... | collective-permute-start | bytes 270344 | tf_op jit(solution)/shard_map/ppermute | solution.py:626
  23.1 7.3 %collective-permute-start.11 = (f32[176,128]{1,0:T(8,128)S(1)}, f32[176,128]{1,0:T(8,128)S(1)}, u32[]{:S(2)}, u32[]{:S(2)}) collective-permute-start(f32[176,128]{1,0:T(8,128)S(1)} %get-tuple-element.60.refs_0_.q0_ref), channel_id=1, source_target_pairs={{0,4},{1,5},{2,6},{3,7},{4,0},{5,1},{6,2},{7,3},{8,12},{9,13},{10,... | collective-permute-start | bytes 270344 | tf_op jit(solution)/shard_map/ppermute | solution.py:626
  23.1 7.3 %collective-permute-start.10 = (f32[176,128]{1,0:T(8,128)S(1)}, f32[176,128]{1,0:T(8,128)S(1)}, u32[]{:S(2)}, u32[]{:S(2)}) collective-permute-start(f32[176,128]{1,0:T(8,128)S(1)} %get-tuple-element.60.refs_0_.q0_ref), channel_id=1, source_target_pairs={{0,2},{1,3},{2,0},{3,1},{4,6},{5,7},{6,4},{7,5},{8,10},{9,11},{10,... | collective-permute-start | bytes 270344 | tf_op jit(solution)/shard_map/ppermute | solution.py:626
  30.5 5.6 %collective-permute-start.13 = (f32[176,128]{1,0:T(8,128)S(1)}, f32[176,128]{1,0:T(8,128)S(1)}, u32[]{:S(2)}, u32[]{:S(2)}) collective-permute-start(f32[176,128]{1,0:T(8,128)S(1)} %quad.1.own_ref.own4_ref), channel_id=1, source_target_pairs={{0,12},{1,13},{2,14},{3,15},{4,8},{5,9},{6,10},{7,11},{8,4},{9,5},... | collective-permute-start | bytes 270344 | tf_op jit(solution)/shard_map/ppermute | solution.py:645
  32.4 7.5 %collective-permute-start.5 = (f32[104,256]{1,0:T(8,128)S(1)}, f32[104,256]{1,0:T(8,128)S(1)}, u32[]{:S(2)}, u32[]{:S(2)}) collective-permute-start(f32[104,256]{1,0:T(8,128)S(1)} %plane_pair.1.mine2_ref.after_ref), channel_id=1, source_target_pairs={{0,192},{64,128},{128,64},{192,0},{1,193},{65,129},{129,65},{193,1... | collective-permute-start | bytes 319496 | tf_op jit(solution)/shard_map/ppermute | solution.py:626
  36.1 7.2 %collective-permute-start.16 = (f32[176,128]{1,0:T(8,128)S(1)}, f32[176,128]{1,0:T(8,128)S(1)}, u32[]{:S(2)}, u32[]{:S(2)}) collective-permute-start(f32[176,128]{1,0:T(8,128)S(1)} %get-tuple-element.61.own_ref), channel_id=1, source_target_pairs={{0,32},{1,33},{2,34},{3,35},{4,36},{5,37},{6,38},{7,39},{8,40},{9,... | collective-permute-start | bytes 270344 | tf_op jit(solution)/shard_map/ppermute | solution.py:636
  38.4 4.9 %collective-permute-start.15 = (f32[176,128]{1,0:T(8,128)S(1)}, f32[176,128]{1,0:T(8,128)S(1)}, u32[]{:S(2)}, u32[]{:S(2)}) collective-permute-start(f32[176,128]{1,0:T(8,128)S(1)} %get-tuple-element.61.own_ref), channel_id=1, source_target_pairs={{0,48},{1,49},{2,50},{3,51},{4,52},{5,53},{6,54},{7,55},{8,56},{9,... | collective-permute-start | bytes 270344 | tf_op jit(solution)/shard_map/ppermute | solution.py:636
  39.2 4.2 %collective-permute-start.14 = (f32[96,128]{1,0:T(8,128)S(1)}, f32[96,128]{1,0:T(8,128)S(1)}, u32[]{:S(2)}, u32[]{:S(2)}) collective-permute-start(f32[96,128]{1,0:T(8,128)S(1)} %get-tuple-element.62), channel_id=1, source_target_pairs={{0,16},{1,17},{2,18},{3,19},{4,20},{5,21},{6,22},{7,23},{8,24},{9,... | collective-permute-start | bytes 147464 | tf_op jit(solution)/shard_map/ppermute | solution.py:636
  43.5 7.3 %collective-permute-start.17 = (f32[160,128]{1,0:T(8,128)S(1)}, f32[160,128]{1,0:T(8,128)S(1)}, u32[]{:S(2)}, u32[]{:S(2)}) collective-permute-start(f32[160,128]{1,0:T(8,128)S(1)} %get-tuple-element.66), channel_id=1, source_target_pairs={{0,1},{1,0},{2,3},{3,2},{4,5},{5,4},{6,7},{7,6},{8,9},{9,8},{10,11... | collective-permute-start | bytes 245768 | tf_op jit(solution)/shard_map/ppermute | solution.py:626

commit v4 on v3

--- a/solution.py
+++ b/solution.py
@@ -22,7 +22,7 @@
 
 
 def call(kernel, outs, *args, scratch=(), in_hbm=0, out_hbm=False, name=None, flops=1000):
-    outs = [jax.ShapeDtypeStruct(s, F32) for s in outs]
+    outs = [s if isinstance(s, jax.ShapeDtypeStruct) else jax.ShapeDtypeStruct(s, F32) for s in outs]
     args = [
         pltpu.with_memory_space_constraint(x, pltpu.HBM) if n < in_hbm else x
         for n, x in enumerate(args)
@@ -53,7 +53,8 @@
 
 
 def faces_kernel(
-    a_hbm, e_hbm, w_ref, ia_ref, ib_ref, ja_ref, jb_ref, a_scr, e_scr, scr, sems
+    a_hbm, e_hbm, x_hbm, m_hbm,
+    w_ref, ia_ref, ib_ref, ja_ref, jb_ref, x_ref, m_ref, a_scr, e_scr, scr, sems, more_sems,
 ):
     even_line = lax.rem(lax.axis_index("line"), 2) == 0
     even_plane = lax.rem(lax.axis_index("plane"), 2) == 0
@@ -66,6 +67,12 @@
     for v in range(NV):
         for n in range(2):
             fetch(v, n).start()
+    more = [
+        pltpu.make_async_copy(x_hbm, x_ref, more_sems.at[0]),
+        pltpu.make_async_copy(m_hbm, m_ref, more_sems.at[1]),
+    ]
+    for copy in more:
+        copy.start()
     for v in range(NV):
         for n in range(2):
             fetch(v, n).wait()
@@ -82,27 +89,20 @@
             high = scr[v, part, pl.ds(NJ - 1, NI, stride=NJ), :]
             ja_ref[v, :, lane] = jnp.where(even_plane, high, low)
             jb_ref[v, :, lane] = jnp.where(even_plane, low, high)
+    for copy in more:
+        copy.wait()
 
 
 def prep_kernel(
-    x_hbm, m_hbm, w_ref, f_ref, c_ref,
-    half_ref, line_resp_ref, maps_ref, cross_resp_ref, halo_resp_ref, weight_ref, co_ref, s_ref, t_ref, x_ref,
-    m_ref, sems,
+    x_ref, m_ref, w_ref, f_ref, c_ref,
+    half_ref, line_resp_ref, maps_ref, cross_resp_ref, halo_resp_ref, weight_ref, co_ref, s_ref, t_ref,
 ):
-    copies = [
-        pltpu.make_async_copy(x_hbm, x_ref, sems.at[0]),
-        pltpu.make_async_copy(m_hbm, m_ref, sems.at[1]),
-    ]
-    for copy in copies:
-        copy.start()
     even = place()[0] == 0
     for v in range(NV):
         for n in range(6):
             c = c_ref[v, n]
             half_ref[v, n] = jnp.where(even, c[:, :HALF], c[:, HALF:])
     line_coeffs_of(c_ref, line_resp_ref, maps_ref)
-    for copy in copies:
-        copy.wait()
     cross_coeffs_of(x_ref, cross_resp_ref, halo_resp_ref, weight_ref, co_ref)
     local_source(w_ref, f_ref, m_ref, weight_ref, s_ref, t_ref)
 
@@ -649,13 +649,16 @@
     flat = (NV * PLANE, NK)
     a, f, e = (x.reshape(flat) for x in (adjoint, forcing, eigen_values))
     i_face, j_face = (NV, NJ, NK), (NV, NI, NK)
-    w, ia, ib, ja, jb = call(
-        faces_kernel, [flat, i_face, i_face, j_face, j_face], a, e, in_hbm=2, name="faces",
+    masks = jax.ShapeDtypeStruct(face_masks.shape, face_masks.dtype)
+    w, ia, ib, ja, jb, x, m = call(
+        faces_kernel, [flat, i_face, i_face, j_face, j_face, cross_coeffs.shape, masks],
+        a, e, cross_coeffs, face_masks, in_hbm=4, name="faces",
         scratch=[
             pltpu.VMEM(flat, F32),
             pltpu.VMEM(flat, F32),
             pltpu.VMEM((NV, 2, PLANE, HALF), F32),
             pltpu.SemaphoreType.DMA((NV, 2)),
+            pltpu.SemaphoreType.DMA((2,)),
         ],
     )
     ia = swap(ia, "line", 4, 1)
@@ -664,17 +667,13 @@
     jb = everyone(jb, lambda p, q: (p ^ 1, q) if q in (0, 63) else (p, q + 1 if q % 2 else q - 1))
 
     halves = (2, NV * PLANE, HALF)
-    half, line_resp, maps, cross_resp, halo_resp, weights, co, s, t, x = call(
+    half, line_resp, maps, cross_resp, halo_resp, weights, co, s, t = call(
         prep_kernel,
         [
             line_coeffs.shape[:3] + (HALF,), halves, (64, NK), (NV, 2, NJ, NK), (NV, 2, NJ, NK),
-            (NV, 2, NJ, NK), (16, NK), flat, flat, cross_coeffs.shape,
+            (NV, 2, NJ, NK), (16, NK), flat, flat,
         ],
-        cross_coeffs, face_masks, w, f, line_coeffs, in_hbm=2, name="prep", flops=10**7,
-        scratch=[
-            pltpu.VMEM(face_masks.shape, face_masks.dtype),
-            pltpu.SemaphoreType.DMA((2,)),
-        ],
+        x, m, w, f, line_coeffs, name="prep", flops=10**7,
     )
     msg = (176, HALF)
     j_low, j_high, faces, keep, send = call(

time: 51.8 us -> 51.5 us (level)
  Pallas kernels: 6.58 us -> 5.97 us
    ppermute x12, starting transfers between devices: 23.2 us -> 22.2 us  [swap(): return lax.ppermute(x, axis, [(i, i ^ flip) for i in range(size)])]
    ppermute x2, waiting for transfers between devices: 0.13 us -> 0.8 us  [everyone(): lax.ppermute(x, ('line', 'plane'), [(n, p * 64 + q) for n, (p, q) in pairs])]
    pallas_call x12, Pallas kernels: 6.58 us -> 5.97 us  [call(): pl.pallas_call(kernel, out_shape=outs, in_specs=[pl.BlockSpec(memory_spac...]
    ppermute x3, starting transfers between devices: 3.71 us -> 4.25 us  [shift(): return lax.ppermute(x, axis, [(i, (i + by) % size) for i in range(size)])]
  transfers between devices with their start and end apart: 18 -> 18, of which waited for: 9 -> 9; matrix products, arithmetic and copies ran while one was open for 0% -> 0% of each run, Pallas kernels for 7% -> 5%
where the time goes in v4:
time: 51.5 us; the launch traced here: 51.4 us
  starting transfers between devices  29.6 us (57%)
  waiting for transfers between devices  15.7 us (30%)
  Pallas kernels  5.97 us (12%)
    ppermute x12, starting transfers between devices, swap(): return lax.ppermute(x, axis, [(i, i ^ flip) for i in range(size)])  22.2 us
    ppermute x12, waiting for transfers between devices, swap(): return lax.ppermute(x, axis, [(i, i ^ flip) for i in range(size)])  10.6 us
    pallas_call x12, Pallas kernels, call(): pl.pallas_call(kernel, out_shape=outs, in_specs=[pl.BlockSpec(memory_spac...  5.97 us
    ppermute x3, starting transfers between devices, shift(): return lax.ppermute(x, axis, [(i, (i + by) % size) for i in range(size)])  4.25 us
    ppermute x3, waiting for transfers between devices, shift(): return lax.ppermute(x, axis, [(i, (i + by) % size) for i in range(size)])  3.2 us
    ppermute x1, starting transfers between devices, across(): return lax.ppermute(x, 'plane', pairs)  2.11 us
    ppermute x1, waiting for transfers between devices, across(): return lax.ppermute(x, 'plane', pairs)  1.12 us
    ppermute x2, starting transfers between devices, everyone(): lax.ppermute(x, ('line', 'plane'), [(n, p * 64 + q) for n, (p, q) in pairs])  1.03 us
  transfers between devices with their start and end apart: 18, of which 9 were waited for; matrix products, arithmetic and copies ran while one was open for 0% of the time, Pallas kernels for 5%

profile of v4, /device:TPU:1, one launch (start us, length us, event | category | flops | bytes accessed | tf_op | source)
XLA Modules:
  0.0 51.4 jit_solution(11769062908471503788)
XLA Ops:
  0.0 1.6 %faces.1 = (f32[640,256]{1,0:T(8,128)S(1)}, f32[5,8,256]{2,1,0:T(8,128)S(1)}, f32[5,8,256]{2,1,0:T(8,128)S(1)}, f32[5,16,256]{2,1,0:T(8,128)S(1)}, f32[5,16,256]...) custom-call(f32[640,256]{1,0:T(8,128)} %bitcast.5, f32[640,256]{1,0:T(8,128)} %bitcast.6, ...), custom_call_target="tpu_custom_call" | custom-call | flops 1000 | bytes 1000 | tf_op jit(solution)/shard_map/faces/pallas_call | solution.py:31
  1.7 3.3 %collective-permute-start.2 = (f32[5,16,256]{2,1,0:T(8,128)S(1)}, f32[5,16,256]{2,1,0:T(8,128)S(1)}, u32[]{:S(2)}, u32[]{:S(2)}) collective-permute-start(f32[5,16,256]{2,1,0:T(8,128)S(1)} %get-tuple-element.44), channel_id=1, source_target_pairs={{0,1},{1,0},{2,3},{3,2},{4,5},{5,4},{6,7},{7,6},{8,9},{9,8},{10,11... | collective-permute-start | bytes 245768 | tf_op jit(solution)/shard_map/ppermute | solution.py:626
  5.0 1.1 %collective-permute-start = (f32[5,8,256]{2,1,0:T(8,128)S(1)}, f32[5,8,256]{2,1,0:T(8,128)S(1)}, u32[]{:S(2)}, u32[]{:S(2)}) collective-permute-start(f32[5,8,256]{2,1,0:T(8,128)S(1)} %get-tuple-element.42), channel_id=1, source_target_pairs={{0,64},{64,0},{128,192},{192,128},{1,65},{65,1},{129,193},{193,129... | collective-permute-start | bytes 122888 | tf_op jit(solution)/shard_map/ppermute | solution.py:626
  6.1 1.0 %collective-permute-start.1 = (f32[5,8,256]{2,1,0:T(8,128)S(1)}, f32[5,8,256]{2,1,0:T(8,128)S(1)}, u32[]{:S(2)}, u32[]{:S(2)}) collective-permute-start(f32[5,8,256]{2,1,0:T(8,128)S(1)} %get-tuple-element.43), channel_id=1, source_target_pairs={{0,1},{1,0},{2,3},{3,2},{4,5},{5,4},{6,7},{7,6},{8,9},{9,8},{10,11... | collective-permute-start | bytes 122888 | tf_op jit(solution)/shard_map/ppermute | solution.py:632
  7.1 1.2 %prep.1 = (f32[5,6,16,128]{3,2,1,0:T(8,128)S(1)}, f32[2,640,128]{2,1,0:T(8,128)S(1)}, f32[64,256]{1,0:T(8,128)S(1)}, f32[5,2,8,256]{3,2,1,0:T(8,128)S(1)}, f32[5...) custom-call(f32[5,4,8,256]{3,2,1,0:T(8,128)S(1)} %get-tuple-element., ...), custom_call_target="tpu_custom_call" | custom-call | flops 10000000 | bytes 10000000 | tf_op jit(solution)/shard_map/prep/pallas_call | solution.py:31
  8.3 0.8 %collective-permute-done.3.jb_ref = f32[5,16,256]{2,1,0:T(8,128)S(1)} collective-permute-done((f32[5,16,256]{2,1,0:T(8,128)S(1)}, f32[5,16,256]{2,1,0:T(8,128)S(1)}, u32[]{:S(2)}, u32[]{:S(2)}) %collective-permute-start.3) | collective-permute-done | bytes 81952 | tf_op jit(solution)/shard_map/ppermute | solution.py:632
  9.4 0.9 %collective-permute-start.6 = (f32[176,128]{1,0:T(8,128)S(1)}, f32[176,128]{1,0:T(8,128)S(1)}, u32[]{:S(2)}, u32[]{:S(2)}) collective-permute-start(f32[176,128]{1,0:T(8,128)S(1)} %get-tuple-element.58), channel_id=1, source_target_pairs={{0,1},{1,0},{2,3},{3,2},{4,5},{5,4},{6,7},{7,6},{8,9},{9,8},{10,11... | collective-permute-start | bytes 270344 | tf_op jit(solution)/shard_map/ppermute | solution.py:626
  10.3 0.9 %collective-permute-done.6.got_ref.gotc_ref = f32[176,128]{1,0:T(8,128)S(1)} collective-permute-done((f32[176,128]{1,0:T(8,128)S(1)}, f32[176,128]{1,0:T(8,128)S(1)}, u32[]{:S(2)}, u32[]{:S(2)}) %collective-permute-start.6) | collective-permute-done | bytes 90144 | tf_op jit(solution)/shard_map/ppermute | solution.py:626
  11.4 1.1 %collective-permute-start.9 = (f32[144,128]{1,0:T(8,128)S(1)}, f32[144,128]{1,0:T(8,128)S(1)}, u32[]{:S(2)}, u32[]{:S(2)}) collective-permute-start(f32[144,128]{1,0:T(8,128)S(1)} %get-tuple-element.61.own_ref), channel_id=1, source_target_pairs={{0,192},{64,128},{128,64},{192,0},{1,193},{65,129},{129,65},{193,1... | collective-permute-start | bytes 221192 | tf_op jit(solution)/shard_map/ppermute | solution.py:626
  12.5 1.8 %collective-permute-start.8 = (f32[144,128]{1,0:T(8,128)S(1)}, f32[144,128]{1,0:T(8,128)S(1)}, u32[]{:S(2)}, u32[]{:S(2)}) collective-permute-start(f32[144,128]{1,0:T(8,128)S(1)} %get-tuple-element.61.own_ref), channel_id=1, source_target_pairs={{0,128},{64,192},{128,0},{192,64},{1,129},{65,193},{129,1},{193,65... | collective-permute-start | bytes 221192 | tf_op jit(solution)/shard_map/ppermute | solution.py:626
  14.8 0.8 %planes.1 = (f32[640,256]{1,0:T(8,128)S(1)}, f32[224,256]{1,0:T(8,128)S(1)}) custom-call(f32[5,6,16,256]{3,2,1,0:T(8,128)S(1)} %copy-done, f32[5,4,8,256]{3,2,1,0:T(8,128)S(1)} %get-tuple-element.37.x_ref, f32[640,256]{1,0:T(8,128)S(1)} %get-tuple-element.40.s_ref, f32[5,16,256]{2,1,0:T(8,128)S(1)} %get-tuple-element.49.low_ref, ...), custom_call_target="tpu_custom_call" | custom-call | flops 10000000 | bytes 10000000 | tf_op jit(solution)/shard_map/planes/pallas_call | solution.py:31
  15.6 1.0 %collective-permute-start.4 = (f32[224,256]{1,0:T(8,128)S(1)}, f32[224,256]{1,0:T(8,128)S(1)}, u32[]{:S(2)}, u32[]{:S(2)}) collective-permute-start(f32[224,256]{1,0:T(8,128)S(1)} %get-tuple-element.55.own_ref.refs_4_), channel_id=1, source_target_pairs={{0,64},{64,0},{128,192},{192,128},{1,65},{65,1},{129,193},{193,129... | collective-permute-start | bytes 688136 | tf_op jit(solution)/shard_map/ppermute | solution.py:626
  17.3 1.1 %collective-permute-done.7.got1_ref = f32[144,128]{1,0:T(8,128)S(1)} collective-permute-done((f32[144,128]{1,0:T(8,128)S(1)}, f32[144,128]{1,0:T(8,128)S(1)}, u32[]{:S(2)}, u32[]{:S(2)}) %collective-permute-start.7) | collective-permute-done | bytes 73760 | tf_op jit(solution)/shard_map/ppermute | solution.py:626
  18.6 4.1 %collective-permute-start.12 = (f32[176,128]{1,0:T(8,128)S(1)}, f32[176,128]{1,0:T(8,128)S(1)}, u32[]{:S(2)}, u32[]{:S(2)}) collective-permute-start(f32[176,128]{1,0:T(8,128)S(1)} %get-tuple-element.62.refs_0_.q0_ref), channel_id=1, source_target_pairs={{0,6},{1,7},{2,4},{3,5},{4,2},{5,3},{6,0},{7,1},{8,14},{9,15},{10,... | collective-permute-start | bytes 270344 | tf_op jit(solution)/shard_map/ppermute | solution.py:626
  23.1 1.5 %collective-permute-done.12.refs_3_.q3_ref = f32[176,128]{1,0:T(8,128)S(1)} collective-permute-done((f32[176,128]{1,0:T(8,128)S(1)}, f32[176,128]{1,0:T(8,128)S(1)}, u32[]{:S(2)}, u32[]{:S(2)}) %collective-permute-start.12) | collective-permute-done | bytes 90144 | tf_op jit(solution)/shard_map/ppermute | solution.py:626
  24.6 5.4 %collective-permute-done.11.refs_2_.q2_ref = f32[176,128]{1,0:T(8,128)S(1)} collective-permute-done((f32[176,128]{1,0:T(8,128)S(1)}, f32[176,128]{1,0:T(8,128)S(1)}, u32[]{:S(2)}, u32[]{:S(2)}) %collective-permute-start.11) | collective-permute-done | bytes 90144 | tf_op jit(solution)/shard_map/ppermute | solution.py:626
  30.1 2.1 %collective-permute-start.13 = (f32[176,128]{1,0:T(8,128)S(1)}, f32[176,128]{1,0:T(8,128)S(1)}, u32[]{:S(2)}, u32[]{:S(2)}) collective-permute-start(f32[176,128]{1,0:T(8,128)S(1)} %quad.1.own_ref.own4_ref), channel_id=1, source_target_pairs={{0,12},{1,13},{2,14},{3,15},{4,8},{5,9},{6,10},{7,11},{8,4},{9,5},... | collective-permute-start | bytes 270344 | tf_op jit(solution)/shard_map/ppermute | solution.py:645
  32.4 2.2 %collective-permute-start.5 = (f32[104,256]{1,0:T(8,128)S(1)}, f32[104,256]{1,0:T(8,128)S(1)}, u32[]{:S(2)}, u32[]{:S(2)}) collective-permute-start(f32[104,256]{1,0:T(8,128)S(1)} %plane_pair.1.mine2_ref.after_ref), channel_id=1, source_target_pairs={{0,192},{64,128},{128,64},{192,0},{1,193},{65,129},{129,65},{193,1... | collective-permute-start | bytes 319496 | tf_op jit(solution)/shard_map/ppermute | solution.py:626
  34.6 1.1 %collective-permute-done.13.got_ref.got4_ref = f32[176,128]{1,0:T(8,128)S(1)} collective-permute-done((f32[176,128]{1,0:T(8,128)S(1)}, f32[176,128]{1,0:T(8,128)S(1)}, u32[]{:S(2)}, u32[]{:S(2)}) %collective-permute-start.13) | collective-permute-done | bytes 90144 | tf_op jit(solution)/shard_map/ppermute | solution.py:645
  35.8 2.8 %collective-permute-start.16 = (f32[176,128]{1,0:T(8,128)S(1)}, f32[176,128]{1,0:T(8,128)S(1)}, u32[]{:S(2)}, u32[]{:S(2)}) collective-permute-start(f32[176,128]{1,0:T(8,128)S(1)} %get-tuple-element.63.own_ref), channel_id=1, source_target_pairs={{0,32},{1,33},{2,34},{3,35},{4,36},{5,37},{6,38},{7,39},{8,40},{9,... | collective-permute-start | bytes 270344 | tf_op jit(solution)/shard_map/ppermute | solution.py:636
  40.3 3.2 %collective-permute-done.14.one_ref = f32[96,128]{1,0:T(8,128)S(1)} collective-permute-done((f32[96,128]{1,0:T(8,128)S(1)}, f32[96,128]{1,0:T(8,128)S(1)}, u32[]{:S(2)}, u32[]{:S(2)}) %collective-permute-start.14) | collective-permute-done | bytes 49184 | tf_op jit(solution)/shard_map/ppermute | solution.py:636
  43.7 5.9 %collective-permute-start.17 = (f32[160,128]{1,0:T(8,128)S(1)}, f32[160,128]{1,0:T(8,128)S(1)}, u32[]{:S(2)}, u32[]{:S(2)}) collective-permute-start(f32[160,128]{1,0:T(8,128)S(1)} %get-tuple-element.68), channel_id=1, source_target_pairs={{0,1},{1,0},{2,3},{3,2},{4,5},{5,4},{6,7},{7,6},{8,9},{9,8},{10,11... | collective-permute-start | bytes 245768 | tf_op jit(solution)/shard_map/ppermute | solution.py:626
  49.5 0.9 %collective-permute-done.17.other_ref = f32[160,128]{1,0:T(8,128)S(1)} collective-permute-done((f32[160,128]{1,0:T(8,128)S(1)}, f32[160,128]{1,0:T(8,128)S(1)}, u32[]{:S(2)}, u32[]{:S(2)}) %collective-permute-start.17) | collective-permute-done | bytes 81952 | tf_op jit(solution)/shard_map/ppermute | solution.py:626
  50.5 0.9 %final.1 = f32[640,256]{1,0:T(8,128)} custom-call(f32[640,256]{1,0:T(8,128)S(1)} %solved.1.after_ref.g_ref, f32[5,2,8,256]{3,2,1,0:T(8,128)S(1)} %get-tuple-element.56.resp_ref, f32[160,128]{1,0:T(8,128)S(1)} %get-tuple-element.67.mine_ref, f32[160,128]{1,0:T(8,128)S(1)} %collective-permute-done.17.other_ref), custom_call_target="tpu_custom_call" | custom-call | flops 1000 | bytes 1000 | tf_op jit(solution)/shard_map/final/pallas_call | solution.py:31
  (28 shorter events, 4.5 us)
Async XLA Ops:
  0.0 7.1 %copy-start = (f32[5,6,16,256]{3,2,1,0:T(8,128)S(1)}, f32[5,6,16,256]{3,2,1,0:T(8,128)}, u32[]{:S(2)}) copy-start(f32[5,6,16,256]{3,2,1,0:T(8,128)} %c_ref.3) | copy-start | bytes 1474564
  0.0 7.1 %copy-start.1 = (f32[5,16,8,256]{3,2,1,0:T(8,128)S(1)}, f32[5,16,8,256]{3,2,1,0:T(8,128)}, u32[]{:S(2)}) copy-start(f32[5,16,8,256]{3,2,1,0:T(8,128)} %param.7) | copy-start | bytes 1966084
  1.7 6.7 %collective-permute-start.2 = (f32[5,16,256]{2,1,0:T(8,128)S(1)}, f32[5,16,256]{2,1,0:T(8,128)S(1)}, u32[]{:S(2)}, u32[]{:S(2)}) collective-permute-start(f32[5,16,256]{2,1,0:T(8,128)S(1)} %get-tuple-element.44), channel_id=1, source_target_pairs={{0,1},{1,0},{2,3},{3,2},{4,5},{5,4},{6,7},{7,6},{8,9},{9,8},{10,11... | collective-permute-start | bytes 245768 | tf_op jit(solution)/shard_map/ppermute | solution.py:626
  5.0 4.2 %collective-permute-start.3 = (f32[5,16,256]{2,1,0:T(8,128)S(1)}, f32[5,16,256]{2,1,0:T(8,128)S(1)}, u32[]{:S(2)}, u32[]{:S(2)}) collective-permute-start(f32[5,16,256]{2,1,0:T(8,128)S(1)} %get-tuple-element.45), channel_id=1, source_target_pairs={{0,64},{1,2},{2,1},{3,4},{4,3},{5,6},{6,5},{7,8},{8,7},{9,10},{10,... | collective-permute-start | bytes 245768 | tf_op jit(solution)/shard_map/ppermute | solution.py:632
  5.0 3.3 %collective-permute-start = (f32[5,8,256]{2,1,0:T(8,128)S(1)}, f32[5,8,256]{2,1,0:T(8,128)S(1)}, u32[]{:S(2)}, u32[]{:S(2)}) collective-permute-start(f32[5,8,256]{2,1,0:T(8,128)S(1)} %get-tuple-element.42), channel_id=1, source_target_pairs={{0,64},{64,0},{128,192},{192,128},{1,65},{65,1},{129,193},{193,129... | collective-permute-start | bytes 122888 | tf_op jit(solution)/shard_map/ppermute | solution.py:626
  6.1 2.2 %collective-permute-start.1 = (f32[5,8,256]{2,1,0:T(8,128)S(1)}, f32[5,8,256]{2,1,0:T(8,128)S(1)}, u32[]{:S(2)}, u32[]{:S(2)}) collective-permute-start(f32[5,8,256]{2,1,0:T(8,128)S(1)} %get-tuple-element.43), channel_id=1, source_target_pairs={{0,1},{1,0},{2,3},{3,2},{4,5},{5,4},{6,7},{7,6},{8,9},{9,8},{10,11... | collective-permute-start | bytes 122888 | tf_op jit(solution)/shard_map/ppermute | solution.py:632
  9.4 1.9 %collective-permute-start.6 = (f32[176,128]{1,0:T(8,128)S(1)}, f32[176,128]{1,0:T(8,128)S(1)}, u32[]{:S(2)}, u32[]{:S(2)}) collective-permute-start(f32[176,128]{1,0:T(8,128)S(1)} %get-tuple-element.58), channel_id=1, source_target_pairs={{0,1},{1,0},{2,3},{3,2},{4,5},{5,4},{6,7},{7,6},{8,9},{9,8},{10,11... | collective-permute-start | bytes 270344 | tf_op jit(solution)/shard_map/ppermute | solution.py:626
  11.4 5.2 %collective-permute-start.9 = (f32[144,128]{1,0:T(8,128)S(1)}, f32[144,128]{1,0:T(8,128)S(1)}, u32[]{:S(2)}, u32[]{:S(2)}) collective-permute-start(f32[144,128]{1,0:T(8,128)S(1)} %get-tuple-element.61.own_ref), channel_id=1, source_target_pairs={{0,192},{64,128},{128,64},{192,0},{1,193},{65,129},{129,65},{193,1... | collective-permute-start | bytes 221192 | tf_op jit(solution)/shard_map/ppermute | solution.py:626
  12.5 4.8 %collective-permute-start.8 = (f32[144,128]{1,0:T(8,128)S(1)}, f32[144,128]{1,0:T(8,128)S(1)}, u32[]{:S(2)}, u32[]{:S(2)}) collective-permute-start(f32[144,128]{1,0:T(8,128)S(1)} %get-tuple-element.61.own_ref), channel_id=1, source_target_pairs={{0,128},{64,192},{128,0},{192,64},{1,129},{65,193},{129,1},{193,65... | collective-permute-start | bytes 221192 | tf_op jit(solution)/shard_map/ppermute | solution.py:626
  14.3 4.1 %collective-permute-start.7 = (f32[144,128]{1,0:T(8,128)S(1)}, f32[144,128]{1,0:T(8,128)S(1)}, u32[]{:S(2)}, u32[]{:S(2)}) collective-permute-start(f32[144,128]{1,0:T(8,128)S(1)} %get-tuple-element.61.own_ref), channel_id=1, source_target_pairs={{0,64},{64,0},{128,192},{192,128},{1,65},{65,1},{129,193},{193,129... | collective-permute-start | bytes 221192 | tf_op jit(solution)/shard_map/ppermute | solution.py:626
  15.6 16.6 %collective-permute-start.4 = (f32[224,256]{1,0:T(8,128)S(1)}, f32[224,256]{1,0:T(8,128)S(1)}, u32[]{:S(2)}, u32[]{:S(2)}) collective-permute-start(f32[224,256]{1,0:T(8,128)S(1)} %get-tuple-element.55.own_ref.refs_4_), channel_id=1, source_target_pairs={{0,64},{64,0},{128,192},{192,128},{1,65},{65,1},{129,193},{193,129... | collective-permute-start | bytes 688136 | tf_op jit(solution)/shard_map/ppermute | solution.py:626
  18.6 6.0 %collective-permute-start.12 = (f32[176,128]{1,0:T(8,128)S(1)}, f32[176,128]{1,0:T(8,128)S(1)}, u32[]{:S(2)}, u32[]{:S(2)}) collective-permute-start(f32[176,128]{1,0:T(8,128)S(1)} %get-tuple-element.62.refs_0_.q0_ref), channel_id=1, source_target_pairs={{0,6},{1,7},{2,4},{3,5},{4,2},{5,3},{6,0},{7,1},{8,14},{9,15},{10,... | collective-permute-start | bytes 270344 | tf_op jit(solution)/shard_map/ppermute | solution.py:626
  22.7 7.4 %collective-permute-start.11 = (f32[176,128]{1,0:T(8,128)S(1)}, f32[176,128]{1,0:T(8,128)S(1)}, u32[]{:S(2)}, u32[]{:S(2)}) collective-permute-start(f32[176,128]{1,0:T(8,128)S(1)} %get-tuple-element.62.refs_0_.q0_ref), channel_id=1, source_target_pairs={{0,4},{1,5},{2,6},{3,7},{4,0},{5,1},{6,2},{7,3},{8,12},{9,13},{10,... | collective-permute-start | bytes 270344 | tf_op jit(solution)/shard_map/ppermute | solution.py:626
  22.7 7.4 %collective-permute-start.10 = (f32[176,128]{1,0:T(8,128)S(1)}, f32[176,128]{1,0:T(8,128)S(1)}, u32[]{:S(2)}, u32[]{:S(2)}) collective-permute-start(f32[176,128]{1,0:T(8,128)S(1)} %get-tuple-element.62.refs_0_.q0_ref), channel_id=1, source_target_pairs={{0,2},{1,3},{2,0},{3,1},{4,6},{5,7},{6,4},{7,5},{8,10},{9,11},{10,... | collective-permute-start | bytes 270344 | tf_op jit(solution)/shard_map/ppermute | solution.py:626
  30.1 5.6 %collective-permute-start.13 = (f32[176,128]{1,0:T(8,128)S(1)}, f32[176,128]{1,0:T(8,128)S(1)}, u32[]{:S(2)}, u32[]{:S(2)}) collective-permute-start(f32[176,128]{1,0:T(8,128)S(1)} %quad.1.own_ref.own4_ref), channel_id=1, source_target_pairs={{0,12},{1,13},{2,14},{3,15},{4,8},{5,9},{6,10},{7,11},{8,4},{9,5},... | collective-permute-start | bytes 270344 | tf_op jit(solution)/shard_map/ppermute | solution.py:645
  32.4 7.6 %collective-permute-start.5 = (f32[104,256]{1,0:T(8,128)S(1)}, f32[104,256]{1,0:T(8,128)S(1)}, u32[]{:S(2)}, u32[]{:S(2)}) collective-permute-start(f32[104,256]{1,0:T(8,128)S(1)} %plane_pair.1.mine2_ref.after_ref), channel_id=1, source_target_pairs={{0,192},{64,128},{128,64},{192,0},{1,193},{65,129},{129,65},{193,1... | collective-permute-start | bytes 319496 | tf_op jit(solution)/shard_map/ppermute | solution.py:626
  35.8 7.7 %collective-permute-start.16 = (f32[176,128]{1,0:T(8,128)S(1)}, f32[176,128]{1,0:T(8,128)S(1)}, u32[]{:S(2)}, u32[]{:S(2)}) collective-permute-start(f32[176,128]{1,0:T(8,128)S(1)} %get-tuple-element.63.own_ref), channel_id=1, source_target_pairs={{0,32},{1,33},{2,34},{3,35},{4,36},{5,37},{6,38},{7,39},{8,40},{9,... | collective-permute-start | bytes 270344 | tf_op jit(solution)/shard_map/ppermute | solution.py:636
  38.6 4.9 %collective-permute-start.15 = (f32[176,128]{1,0:T(8,128)S(1)}, f32[176,128]{1,0:T(8,128)S(1)}, u32[]{:S(2)}, u32[]{:S(2)}) collective-permute-start(f32[176,128]{1,0:T(8,128)S(1)} %get-tuple-element.63.own_ref), channel_id=1, source_target_pairs={{0,48},{1,49},{2,50},{3,51},{4,52},{5,53},{6,54},{7,55},{8,56},{9,... | collective-permute-start | bytes 270344 | tf_op jit(solution)/shard_map/ppermute | solution.py:636
  39.3 4.2 %collective-permute-start.14 = (f32[96,128]{1,0:T(8,128)S(1)}, f32[96,128]{1,0:T(8,128)S(1)}, u32[]{:S(2)}, u32[]{:S(2)}) collective-permute-start(f32[96,128]{1,0:T(8,128)S(1)} %get-tuple-element.64), channel_id=1, source_target_pairs={{0,16},{1,17},{2,18},{3,19},{4,20},{5,21},{6,22},{7,23},{8,24},{9,... | collective-permute-start | bytes 147464 | tf_op jit(solution)/shard_map/ppermute | solution.py:636
  43.7 6.8 %collective-permute-start.17 = (f32[160,128]{1,0:T(8,128)S(1)}, f32[160,128]{1,0:T(8,128)S(1)}, u32[]{:S(2)}, u32[]{:S(2)}) collective-permute-start(f32[160,128]{1,0:T(8,128)S(1)} %get-tuple-element.68), channel_id=1, source_target_pairs={{0,1},{1,0},{2,3},{3,2},{4,5},{5,4},{6,7},{7,6},{8,9},{9,8},{10,11... | collective-permute-start | bytes 245768 | tf_op jit(solution)/shard_map/ppermute | solution.py:626

commit v5 on v4

--- a/solution.py
+++ b/solution.py
@@ -60,12 +60,12 @@
     even_plane = lax.rem(lax.axis_index("plane"), 2) == 0
 
     def fetch(v, n):
-        src, dst = ((a_hbm, a_scr), (e_hbm, e_scr))[n]
-        at = pl.ds(v * PLANE, PLANE)
+        src, dst = ((a_hbm, a_scr), (e_hbm, e_scr))[n % 2]
+        at = pl.ds(v * PLANE + n // 2 * (PLANE // 2), PLANE // 2)
         return pltpu.make_async_copy(src.at[at], dst.at[at], sems.at[v, n])
 
     for v in range(NV):
-        for n in range(2):
+        for n in range(4):
             fetch(v, n).start()
     more = [
         pltpu.make_async_copy(x_hbm, x_ref, more_sems.at[0]),
@@ -74,7 +74,7 @@
     for copy in more:
         copy.start()
     for v in range(NV):
-        for n in range(2):
+        for n in range(4):
             fetch(v, n).wait()
         base = v * PLANE
         for part in range(2):
@@ -657,7 +657,7 @@
             pltpu.VMEM(flat, F32),
             pltpu.VMEM(flat, F32),
             pltpu.VMEM((NV, 2, PLANE, HALF), F32),
-            pltpu.SemaphoreType.DMA((NV, 2)),
+            pltpu.SemaphoreType.DMA((NV, 4)),
             pltpu.SemaphoreType.DMA((2,)),
         ],
     )

time: 51.5 us -> 51.5 us (level)
  no operation moved by 1% of the time
where the time goes in v5:
time: 51.5 us; the launch traced here: 51.4 us
  starting transfers between devices  29.6 us (57%)
  waiting for transfers between devices  15.7 us (30%)
  Pallas kernels  6.01 us (12%)
    ppermute x12, starting transfers between devices, swap(): return lax.ppermute(x, axis, [(i, i ^ flip) for i in range(size)])  22.2 us
    ppermute x12, waiting for transfers between devices, swap(): return lax.ppermute(x, axis, [(i, i ^ flip) for i in range(size)])  10.6 us
    pallas_call x12, Pallas kernels, call(): pl.pallas_call(kernel, out_shape=outs, in_specs=[pl.BlockSpec(memory_spac...  6.01 us
    ppermute x3, starting transfers between devices, shift(): return lax.ppermute(x, axis, [(i, (i + by) % size) for i in range(size)])  4.25 us
    ppermute x3, waiting for transfers between devices, shift(): return lax.ppermute(x, axis, [(i, (i + by) % size) for i in range(size)])  3.2 us
    ppermute x1, starting transfers between devices, across(): return lax.ppermute(x, 'plane', pairs)  2.11 us
    ppermute x1, waiting for transfers between devices, across(): return lax.ppermute(x, 'plane', pairs)  1.12 us
    ppermute x2, starting transfers between devices, everyone(): lax.ppermute(x, ('line', 'plane'), [(n, p * 64 + q) for n, (p, q) in pairs])  1.03 us
  transfers between devices with their start and end apart: 18, of which 9 were waited for; matrix products, arithmetic and copies ran while one was open for 0% of the time, Pallas kernels for 5%

profile of v5, /device:TPU:1, one launch (start us, length us, event | category | flops | bytes accessed | tf_op | source)
XLA Modules:
  0.0 51.4 jit_solution(18303404615563940278)
XLA Ops:
  0.0 1.7 %faces.1 = (f32[640,256]{1,0:T(8,128)S(1)}, f32[5,8,256]{2,1,0:T(8,128)S(1)}, f32[5,8,256]{2,1,0:T(8,128)S(1)}, f32[5,16,256]{2,1,0:T(8,128)S(1)}, f32[5,16,256]...) custom-call(f32[640,256]{1,0:T(8,128)} %bitcast.5, f32[640,256]{1,0:T(8,128)} %bitcast.6, ...), custom_call_target="tpu_custom_call" | custom-call | flops 1000 | bytes 1000 | tf_op jit(solution)/shard_map/faces/pallas_call | solution.py:31
  1.7 3.3 %collective-permute-start.2 = (f32[5,16,256]{2,1,0:T(8,128)S(1)}, f32[5,16,256]{2,1,0:T(8,128)S(1)}, u32[]{:S(2)}, u32[]{:S(2)}) collective-permute-start(f32[5,16,256]{2,1,0:T(8,128)S(1)} %get-tuple-element.44), channel_id=1, source_target_pairs={{0,1},{1,0},{2,3},{3,2},{4,5},{5,4},{6,7},{7,6},{8,9},{9,8},{10,11... | collective-permute-start | bytes 245768 | tf_op jit(solution)/shard_map/ppermute | solution.py:626
  5.0 1.1 %collective-permute-start = (f32[5,8,256]{2,1,0:T(8,128)S(1)}, f32[5,8,256]{2,1,0:T(8,128)S(1)}, u32[]{:S(2)}, u32[]{:S(2)}) collective-permute-start(f32[5,8,256]{2,1,0:T(8,128)S(1)} %get-tuple-element.42), channel_id=1, source_target_pairs={{0,64},{64,0},{128,192},{192,128},{1,65},{65,1},{129,193},{193,129... | collective-permute-start | bytes 122888 | tf_op jit(solution)/shard_map/ppermute | solution.py:626
  6.1 1.0 %collective-permute-start.1 = (f32[5,8,256]{2,1,0:T(8,128)S(1)}, f32[5,8,256]{2,1,0:T(8,128)S(1)}, u32[]{:S(2)}, u32[]{:S(2)}) collective-permute-start(f32[5,8,256]{2,1,0:T(8,128)S(1)} %get-tuple-element.43), channel_id=1, source_target_pairs={{0,1},{1,0},{2,3},{3,2},{4,5},{5,4},{6,7},{7,6},{8,9},{9,8},{10,11... | collective-permute-start | bytes 122888 | tf_op jit(solution)/shard_map/ppermute | solution.py:632
  7.2 1.2 %prep.1 = (f32[5,6,16,128]{3,2,1,0:T(8,128)S(1)}, f32[2,640,128]{2,1,0:T(8,128)S(1)}, f32[64,256]{1,0:T(8,128)S(1)}, f32[5,2,8,256]{3,2,1,0:T(8,128)S(1)}, f32[5...) custom-call(f32[5,4,8,256]{3,2,1,0:T(8,128)S(1)} %get-tuple-element., ...), custom_call_target="tpu_custom_call" | custom-call | flops 10000000 | bytes 10000000 | tf_op jit(solution)/shard_map/prep/pallas_call | solution.py:31
  8.4 0.8 %collective-permute-done.3.jb_ref = f32[5,16,256]{2,1,0:T(8,128)S(1)} collective-permute-done((f32[5,16,256]{2,1,0:T(8,128)S(1)}, f32[5,16,256]{2,1,0:T(8,128)S(1)}, u32[]{:S(2)}, u32[]{:S(2)}) %collective-permute-start.3) | collective-permute-done | bytes 81952 | tf_op jit(solution)/shard_map/ppermute | solution.py:632
  9.4 0.9 %collective-permute-start.6 = (f32[176,128]{1,0:T(8,128)S(1)}, f32[176,128]{1,0:T(8,128)S(1)}, u32[]{:S(2)}, u32[]{:S(2)}) collective-permute-start(f32[176,128]{1,0:T(8,128)S(1)} %get-tuple-element.58), channel_id=1, source_target_pairs={{0,1},{1,0},{2,3},{3,2},{4,5},{5,4},{6,7},{7,6},{8,9},{9,8},{10,11... | collective-permute-start | bytes 270344 | tf_op jit(solution)/shard_map/ppermute | solution.py:626
  10.3 0.9 %collective-permute-done.6.got_ref.gotc_ref = f32[176,128]{1,0:T(8,128)S(1)} collective-permute-done((f32[176,128]{1,0:T(8,128)S(1)}, f32[176,128]{1,0:T(8,128)S(1)}, u32[]{:S(2)}, u32[]{:S(2)}) %collective-permute-start.6) | collective-permute-done | bytes 90144 | tf_op jit(solution)/shard_map/ppermute | solution.py:626
  11.5 1.1 %collective-permute-start.9 = (f32[144,128]{1,0:T(8,128)S(1)}, f32[144,128]{1,0:T(8,128)S(1)}, u32[]{:S(2)}, u32[]{:S(2)}) collective-permute-start(f32[144,128]{1,0:T(8,128)S(1)} %get-tuple-element.61.own_ref), channel_id=1, source_target_pairs={{0,192},{64,128},{128,64},{192,0},{1,193},{65,129},{129,65},{193,1... | collective-permute-start | bytes 221192 | tf_op jit(solution)/shard_map/ppermute | solution.py:626
  12.6 1.8 %collective-permute-start.8 = (f32[144,128]{1,0:T(8,128)S(1)}, f32[144,128]{1,0:T(8,128)S(1)}, u32[]{:S(2)}, u32[]{:S(2)}) collective-permute-start(f32[144,128]{1,0:T(8,128)S(1)} %get-tuple-element.61.own_ref), channel_id=1, source_target_pairs={{0,128},{64,192},{128,0},{192,64},{1,129},{65,193},{129,1},{193,65... | collective-permute-start | bytes 221192 | tf_op jit(solution)/shard_map/ppermute | solution.py:626
  14.8 0.8 %planes.1 = (f32[640,256]{1,0:T(8,128)S(1)}, f32[224,256]{1,0:T(8,128)S(1)}) custom-call(f32[5,6,16,256]{3,2,1,0:T(8,128)S(1)} %copy-done, f32[5,4,8,256]{3,2,1,0:T(8,128)S(1)} %get-tuple-element.37.x_ref, f32[640,256]{1,0:T(8,128)S(1)} %get-tuple-element.40.s_ref, f32[5,16,256]{2,1,0:T(8,128)S(1)} %get-tuple-element.49.low_ref, ...), custom_call_target="tpu_custom_call" | custom-call | flops 10000000 | bytes 10000000 | tf_op jit(solution)/shard_map/planes/pallas_call | solution.py:31
  15.7 1.0 %collective-permute-start.4 = (f32[224,256]{1,0:T(8,128)S(1)}, f32[224,256]{1,0:T(8,128)S(1)}, u32[]{:S(2)}, u32[]{:S(2)}) collective-permute-start(f32[224,256]{1,0:T(8,128)S(1)} %get-tuple-element.55.own_ref.refs_4_), channel_id=1, source_target_pairs={{0,64},{64,0},{128,192},{192,128},{1,65},{65,1},{129,193},{193,129... | collective-permute-start | bytes 688136 | tf_op jit(solution)/shard_map/ppermute | solution.py:626
  17.4 1.1 %collective-permute-done.7.got1_ref = f32[144,128]{1,0:T(8,128)S(1)} collective-permute-done((f32[144,128]{1,0:T(8,128)S(1)}, f32[144,128]{1,0:T(8,128)S(1)}, u32[]{:S(2)}, u32[]{:S(2)}) %collective-permute-start.7) | collective-permute-done | bytes 73760 | tf_op jit(solution)/shard_map/ppermute | solution.py:626
  18.7 4.1 %collective-permute-start.12 = (f32[176,128]{1,0:T(8,128)S(1)}, f32[176,128]{1,0:T(8,128)S(1)}, u32[]{:S(2)}, u32[]{:S(2)}) collective-permute-start(f32[176,128]{1,0:T(8,128)S(1)} %get-tuple-element.62.refs_0_.q0_ref), channel_id=1, source_target_pairs={{0,6},{1,7},{2,4},{3,5},{4,2},{5,3},{6,0},{7,1},{8,14},{9,15},{10,... | collective-permute-start | bytes 270344 | tf_op jit(solution)/shard_map/ppermute | solution.py:626
  23.1 1.5 %collective-permute-done.12.refs_3_.q3_ref = f32[176,128]{1,0:T(8,128)S(1)} collective-permute-done((f32[176,128]{1,0:T(8,128)S(1)}, f32[176,128]{1,0:T(8,128)S(1)}, u32[]{:S(2)}, u32[]{:S(2)}) %collective-permute-start.12) | collective-permute-done | bytes 90144 | tf_op jit(solution)/shard_map/ppermute | solution.py:626
  24.6 5.4 %collective-permute-done.11.refs_2_.q2_ref = f32[176,128]{1,0:T(8,128)S(1)} collective-permute-done((f32[176,128]{1,0:T(8,128)S(1)}, f32[176,128]{1,0:T(8,128)S(1)}, u32[]{:S(2)}, u32[]{:S(2)}) %collective-permute-start.11) | collective-permute-done | bytes 90144 | tf_op jit(solution)/shard_map/ppermute | solution.py:626
  30.2 2.1 %collective-permute-start.13 = (f32[176,128]{1,0:T(8,128)S(1)}, f32[176,128]{1,0:T(8,128)S(1)}, u32[]{:S(2)}, u32[]{:S(2)}) collective-permute-start(f32[176,128]{1,0:T(8,128)S(1)} %quad.1.own_ref.own4_ref), channel_id=1, source_target_pairs={{0,12},{1,13},{2,14},{3,15},{4,8},{5,9},{6,10},{7,11},{8,4},{9,5},... | collective-permute-start | bytes 270344 | tf_op jit(solution)/shard_map/ppermute | solution.py:645
  32.5 2.2 %collective-permute-start.5 = (f32[104,256]{1,0:T(8,128)S(1)}, f32[104,256]{1,0:T(8,128)S(1)}, u32[]{:S(2)}, u32[]{:S(2)}) collective-permute-start(f32[104,256]{1,0:T(8,128)S(1)} %plane_pair.1.mine2_ref.after_ref), channel_id=1, source_target_pairs={{0,192},{64,128},{128,64},{192,0},{1,193},{65,129},{129,65},{193,1... | collective-permute-start | bytes 319496 | tf_op jit(solution)/shard_map/ppermute | solution.py:626
  34.6 1.1 %collective-permute-done.13.got_ref.got4_ref = f32[176,128]{1,0:T(8,128)S(1)} collective-permute-done((f32[176,128]{1,0:T(8,128)S(1)}, f32[176,128]{1,0:T(8,128)S(1)}, u32[]{:S(2)}, u32[]{:S(2)}) %collective-permute-start.13) | collective-permute-done | bytes 90144 | tf_op jit(solution)/shard_map/ppermute | solution.py:645
  35.8 2.8 %collective-permute-start.16 = (f32[176,128]{1,0:T(8,128)S(1)}, f32[176,128]{1,0:T(8,128)S(1)}, u32[]{:S(2)}, u32[]{:S(2)}) collective-permute-start(f32[176,128]{1,0:T(8,128)S(1)} %get-tuple-element.63.own_ref), channel_id=1, source_target_pairs={{0,32},{1,33},{2,34},{3,35},{4,36},{5,37},{6,38},{7,39},{8,40},{9,... | collective-permute-start | bytes 270344 | tf_op jit(solution)/shard_map/ppermute | solution.py:636
  40.3 3.2 %collective-permute-done.14.one_ref = f32[96,128]{1,0:T(8,128)S(1)} collective-permute-done((f32[96,128]{1,0:T(8,128)S(1)}, f32[96,128]{1,0:T(8,128)S(1)}, u32[]{:S(2)}, u32[]{:S(2)}) %collective-permute-start.14) | collective-permute-done | bytes 49184 | tf_op jit(solution)/shard_map/ppermute | solution.py:636
  43.7 5.9 %collective-permute-start.17 = (f32[160,128]{1,0:T(8,128)S(1)}, f32[160,128]{1,0:T(8,128)S(1)}, u32[]{:S(2)}, u32[]{:S(2)}) collective-permute-start(f32[160,128]{1,0:T(8,128)S(1)} %get-tuple-element.68), channel_id=1, source_target_pairs={{0,1},{1,0},{2,3},{3,2},{4,5},{5,4},{6,7},{7,6},{8,9},{9,8},{10,11... | collective-permute-start | bytes 245768 | tf_op jit(solution)/shard_map/ppermute | solution.py:626
  49.6 0.9 %collective-permute-done.17.other_ref = f32[160,128]{1,0:T(8,128)S(1)} collective-permute-done((f32[160,128]{1,0:T(8,128)S(1)}, f32[160,128]{1,0:T(8,128)S(1)}, u32[]{:S(2)}, u32[]{:S(2)}) %collective-permute-start.17) | collective-permute-done | bytes 81952 | tf_op jit(solution)/shard_map/ppermute | solution.py:626
  50.5 0.9 %final.1 = f32[640,256]{1,0:T(8,128)} custom-call(f32[640,256]{1,0:T(8,128)S(1)} %solved.1.after_ref.g_ref, f32[5,2,8,256]{3,2,1,0:T(8,128)S(1)} %get-tuple-element.56.resp_ref, f32[160,128]{1,0:T(8,128)S(1)} %get-tuple-element.67.mine_ref, f32[160,128]{1,0:T(8,128)S(1)} %collective-permute-done.17.other_ref), custom_call_target="tpu_custom_call" | custom-call | flops 1000 | bytes 1000 | tf_op jit(solution)/shard_map/final/pallas_call | solution.py:31
  (28 shorter events, 4.5 us)
Async XLA Ops:
  0.0 7.2 %copy-start = (f32[5,6,16,256]{3,2,1,0:T(8,128)S(1)}, f32[5,6,16,256]{3,2,1,0:T(8,128)}, u32[]{:S(2)}) copy-start(f32[5,6,16,256]{3,2,1,0:T(8,128)} %c_ref.3) | copy-start | bytes 1474564
  0.0 7.2 %copy-start.1 = (f32[5,16,8,256]{3,2,1,0:T(8,128)S(1)}, f32[5,16,8,256]{3,2,1,0:T(8,128)}, u32[]{:S(2)}) copy-start(f32[5,16,8,256]{3,2,1,0:T(8,128)} %param.7) | copy-start | bytes 1966084
  1.7 6.7 %collective-permute-start.2 = (f32[5,16,256]{2,1,0:T(8,128)S(1)}, f32[5,16,256]{2,1,0:T(8,128)S(1)}, u32[]{:S(2)}, u32[]{:S(2)}) collective-permute-start(f32[5,16,256]{2,1,0:T(8,128)S(1)} %get-tuple-element.44), channel_id=1, source_target_pairs={{0,1},{1,0},{2,3},{3,2},{4,5},{5,4},{6,7},{7,6},{8,9},{9,8},{10,11... | collective-permute-start | bytes 245768 | tf_op jit(solution)/shard_map/ppermute | solution.py:626
  5.0 4.2 %collective-permute-start.3 = (f32[5,16,256]{2,1,0:T(8,128)S(1)}, f32[5,16,256]{2,1,0:T(8,128)S(1)}, u32[]{:S(2)}, u32[]{:S(2)}) collective-permute-start(f32[5,16,256]{2,1,0:T(8,128)S(1)} %get-tuple-element.45), channel_id=1, source_target_pairs={{0,64},{1,2},{2,1},{3,4},{4,3},{5,6},{6,5},{7,8},{8,7},{9,10},{10,... | collective-permute-start | bytes 245768 | tf_op jit(solution)/shard_map/ppermute | solution.py:632
  5.0 3.3 %collective-permute-start = (f32[5,8,256]{2,1,0:T(8,128)S(1)}, f32[5,8,256]{2,1,0:T(8,128)S(1)}, u32[]{:S(2)}, u32[]{:S(2)}) collective-permute-start(f32[5,8,256]{2,1,0:T(8,128)S(1)} %get-tuple-element.42), channel_id=1, source_target_pairs={{0,64},{64,0},{128,192},{192,128},{1,65},{65,1},{129,193},{193,129... | collective-permute-start | bytes 122888 | tf_op jit(solution)/shard_map/ppermute | solution.py:626
  6.1 2.2 %collective-permute-start.1 = (f32[5,8,256]{2,1,0:T(8,128)S(1)}, f32[5,8,256]{2,1,0:T(8,128)S(1)}, u32[]{:S(2)}, u32[]{:S(2)}) collective-permute-start(f32[5,8,256]{2,1,0:T(8,128)S(1)} %get-tuple-element.43), channel_id=1, source_target_pairs={{0,1},{1,0},{2,3},{3,2},{4,5},{5,4},{6,7},{7,6},{8,9},{9,8},{10,11... | collective-permute-start | bytes 122888 | tf_op jit(solution)/shard_map/ppermute | solution.py:632
  9.4 1.9 %collective-permute-start.6 = (f32[176,128]{1,0:T(8,128)S(1)}, f32[176,128]{1,0:T(8,128)S(1)}, u32[]{:S(2)}, u32[]{:S(2)}) collective-permute-start(f32[176,128]{1,0:T(8,128)S(1)} %get-tuple-element.58), channel_id=1, source_target_pairs={{0,1},{1,0},{2,3},{3,2},{4,5},{5,4},{6,7},{7,6},{8,9},{9,8},{10,11... | collective-permute-start | bytes 270344 | tf_op jit(solution)/shard_map/ppermute | solution.py:626
  11.5 5.2 %collective-permute-start.9 = (f32[144,128]{1,0:T(8,128)S(1)}, f32[144,128]{1,0:T(8,128)S(1)}, u32[]{:S(2)}, u32[]{:S(2)}) collective-permute-start(f32[144,128]{1,0:T(8,128)S(1)} %get-tuple-element.61.own_ref), channel_id=1, source_target_pairs={{0,192},{64,128},{128,64},{192,0},{1,193},{65,129},{129,65},{193,1... | collective-permute-start | bytes 221192 | tf_op jit(solution)/shard_map/ppermute | solution.py:626
  12.6 4.8 %collective-permute-start.8 = (f32[144,128]{1,0:T(8,128)S(1)}, f32[144,128]{1,0:T(8,128)S(1)}, u32[]{:S(2)}, u32[]{:S(2)}) collective-permute-start(f32[144,128]{1,0:T(8,128)S(1)} %get-tuple-element.61.own_ref), channel_id=1, source_target_pairs={{0,128},{64,192},{128,0},{192,64},{1,129},{65,193},{129,1},{193,65... | collective-permute-start | bytes 221192 | tf_op jit(solution)/shard_map/ppermute | solution.py:626
  14.3 4.1 %collective-permute-start.7 = (f32[144,128]{1,0:T(8,128)S(1)}, f32[144,128]{1,0:T(8,128)S(1)}, u32[]{:S(2)}, u32[]{:S(2)}) collective-permute-start(f32[144,128]{1,0:T(8,128)S(1)} %get-tuple-element.61.own_ref), channel_id=1, source_target_pairs={{0,64},{64,0},{128,192},{192,128},{1,65},{65,1},{129,193},{193,129... | collective-permute-start | bytes 221192 | tf_op jit(solution)/shard_map/ppermute | solution.py:626
  15.7 16.6 %collective-permute-start.4 = (f32[224,256]{1,0:T(8,128)S(1)}, f32[224,256]{1,0:T(8,128)S(1)}, u32[]{:S(2)}, u32[]{:S(2)}) collective-permute-start(f32[224,256]{1,0:T(8,128)S(1)} %get-tuple-element.55.own_ref.refs_4_), channel_id=1, source_target_pairs={{0,64},{64,0},{128,192},{192,128},{1,65},{65,1},{129,193},{193,129... | collective-permute-start | bytes 688136 | tf_op jit(solution)/shard_map/ppermute | solution.py:626
  18.7 6.0 %collective-permute-start.12 = (f32[176,128]{1,0:T(8,128)S(1)}, f32[176,128]{1,0:T(8,128)S(1)}, u32[]{:S(2)}, u32[]{:S(2)}) collective-permute-start(f32[176,128]{1,0:T(8,128)S(1)} %get-tuple-element.62.refs_0_.q0_ref), channel_id=1, source_target_pairs={{0,6},{1,7},{2,4},{3,5},{4,2},{5,3},{6,0},{7,1},{8,14},{9,15},{10,... | collective-permute-start | bytes 270344 | tf_op jit(solution)/shard_map/ppermute | solution.py:626
  22.7 7.4 %collective-permute-start.11 = (f32[176,128]{1,0:T(8,128)S(1)}, f32[176,128]{1,0:T(8,128)S(1)}, u32[]{:S(2)}, u32[]{:S(2)}) collective-permute-start(f32[176,128]{1,0:T(8,128)S(1)} %get-tuple-element.62.refs_0_.q0_ref), channel_id=1, source_target_pairs={{0,4},{1,5},{2,6},{3,7},{4,0},{5,1},{6,2},{7,3},{8,12},{9,13},{10,... | collective-permute-start | bytes 270344 | tf_op jit(solution)/shard_map/ppermute | solution.py:626
  22.7 7.4 %collective-permute-start.10 = (f32[176,128]{1,0:T(8,128)S(1)}, f32[176,128]{1,0:T(8,128)S(1)}, u32[]{:S(2)}, u32[]{:S(2)}) collective-permute-start(f32[176,128]{1,0:T(8,128)S(1)} %get-tuple-element.62.refs_0_.q0_ref), channel_id=1, source_target_pairs={{0,2},{1,3},{2,0},{3,1},{4,6},{5,7},{6,4},{7,5},{8,10},{9,11},{10,... | collective-permute-start | bytes 270344 | tf_op jit(solution)/shard_map/ppermute | solution.py:626
  30.2 5.6 %collective-permute-start.13 = (f32[176,128]{1,0:T(8,128)S(1)}, f32[176,128]{1,0:T(8,128)S(1)}, u32[]{:S(2)}, u32[]{:S(2)}) collective-permute-start(f32[176,128]{1,0:T(8,128)S(1)} %quad.1.own_ref.own4_ref), channel_id=1, source_target_pairs={{0,12},{1,13},{2,14},{3,15},{4,8},{5,9},{6,10},{7,11},{8,4},{9,5},... | collective-permute-start | bytes 270344 | tf_op jit(solution)/shard_map/ppermute | solution.py:645
  32.5 7.6 %collective-permute-start.5 = (f32[104,256]{1,0:T(8,128)S(1)}, f32[104,256]{1,0:T(8,128)S(1)}, u32[]{:S(2)}, u32[]{:S(2)}) collective-permute-start(f32[104,256]{1,0:T(8,128)S(1)} %plane_pair.1.mine2_ref.after_ref), channel_id=1, source_target_pairs={{0,192},{64,128},{128,64},{192,0},{1,193},{65,129},{129,65},{193,1... | collective-permute-start | bytes 319496 | tf_op jit(solution)/shard_map/ppermute | solution.py:626
  35.8 7.7 %collective-permute-start.16 = (f32[176,128]{1,0:T(8,128)S(1)}, f32[176,128]{1,0:T(8,128)S(1)}, u32[]{:S(2)}, u32[]{:S(2)}) collective-permute-start(f32[176,128]{1,0:T(8,128)S(1)} %get-tuple-element.63.own_ref), channel_id=1, source_target_pairs={{0,32},{1,33},{2,34},{3,35},{4,36},{5,37},{6,38},{7,39},{8,40},{9,... | collective-permute-start | bytes 270344 | tf_op jit(solution)/shard_map/ppermute | solution.py:636
  38.6 4.9 %collective-permute-start.15 = (f32[176,128]{1,0:T(8,128)S(1)}, f32[176,128]{1,0:T(8,128)S(1)}, u32[]{:S(2)}, u32[]{:S(2)}) collective-permute-start(f32[176,128]{1,0:T(8,128)S(1)} %get-tuple-element.63.own_ref), channel_id=1, source_target_pairs={{0,48},{1,49},{2,50},{3,51},{4,52},{5,53},{6,54},{7,55},{8,56},{9,... | collective-permute-start | bytes 270344 | tf_op jit(solution)/shard_map/ppermute | solution.py:636
  39.4 4.2 %collective-permute-start.14 = (f32[96,128]{1,0:T(8,128)S(1)}, f32[96,128]{1,0:T(8,128)S(1)}, u32[]{:S(2)}, u32[]{:S(2)}) collective-permute-start(f32[96,128]{1,0:T(8,128)S(1)} %get-tuple-element.64), channel_id=1, source_target_pairs={{0,16},{1,17},{2,18},{3,19},{4,20},{5,21},{6,22},{7,23},{8,24},{9,... | collective-permute-start | bytes 147464 | tf_op jit(solution)/shard_map/ppermute | solution.py:636
  43.7 6.8 %collective-permute-start.17 = (f32[160,128]{1,0:T(8,128)S(1)}, f32[160,128]{1,0:T(8,128)S(1)}, u32[]{:S(2)}, u32[]{:S(2)}) collective-permute-start(f32[160,128]{1,0:T(8,128)S(1)} %get-tuple-element.68), channel_id=1, source_target_pairs={{0,1},{1,0},{2,3},{3,2},{4,5},{5,4},{6,7},{7,6},{8,9},{9,8},{10,11... | collective-permute-start | bytes 245768 | tf_op jit(solution)/shard_map/ppermute | solution.py:626
